TPU v7x, 512 devices: a whole 4x4x16 slice. The times are simulated.
512 devices in a mesh: grp: 64 (over y, z), rep: 8 (over x, core).
Axes of the slice: x: 4, y: 4, z: 16, core: 2. Of those that a mesh axis runs over, the one named last changes fastest.
Arguments:
- table: float32 [131072, 400], P(('grp', 'rep')), may hold values from -1.2 to 1.2
- row_state: float32 [131072], P(('grp', 'rep')), may hold values from 0.01 to 0.1
- relations: float32 [2, 400, 400], replicated, may hold values from -0.3125 to 0.3125
- touched: int32 [32768, 32], P(('grp', 'rep')), may hold values from 0 to 255
- source: int32 [262144], P(('grp', 'rep')), may hold values from 0 to 2047
- target: int32 [262144], P(('grp', 'rep')), may hold values from 0 to 2047
- neg_slots: int32 [1024], P(('grp', 'rep')), may hold values from 0 to 2047
Outputs:
- new_table: float32 [131072, 400], P(('grp', 'rep'))
- new_state: float32 [131072], P(('grp', 'rep'))
Inputs may be any that keep to these rules, and one draw needn't show every extreme that they name: `touched`: local row numbers of the owning device. `source`: slot numbers of the receiving device. `target`: slot numbers of the receiving device. `neg_slots`: slot numbers of the contributing device.
All inputs are finite; a program needn't handle non-finite values.
Results may differ from a plain program's by a relative error of at most 0.0001.
Values sent between devices are 32-bit elements; how exact they have to be, the bound alone decides.
No kernel may reach another device: no remote copies, remote signals or barrier semaphores. Data moves between devices by JAX's collectives and lax.ppermute only.
A program may use at most 64 MiB of HBM per device.

v0:
```python
import jax
import jax.numpy as jnp
from jax import lax
from jax.sharding import PartitionSpec as P

PRECISE = lax.Precision.HIGHEST
LEARN_RATE = 0.1
EPSILON = 1e-06


def per_device(table, row_state, relations, touched, source, target, neg_slots):
    width = table.shape[1]
    peers = lax.axis_size("grp")
    sent = touched.shape[1]
    kinds = relations.shape[0]
    per_rel = source.shape[0] // kinds
    slot_count = peers * sent
    outgoing = jnp.take(table, touched, axis=0)
    incoming = lax.all_to_all(outgoing, "grp", split_axis=0, concat_axis=0, tiled=True)
    slots = incoming.reshape(slot_count, width)
    head = jnp.take(slots, source, axis=0)
    query = jnp.einsum(
        "ked,kdf->kef", head.reshape(kinds, per_rel, width), relations, precision=PRECISE
    ).reshape(kinds * per_rel, width)
    tail = jnp.take(slots, target, axis=0)
    own_neg = jnp.take(slots, neg_slots, axis=0)
    negatives = lax.all_gather(own_neg, "grp", axis=0, tiled=True)
    neg_total = negatives.shape[0]
    positive = jnp.sum(query * tail, -1)
    negative = jnp.dot(query, negatives.T, precision=PRECISE)
    grad_pos = jax.nn.sigmoid(positive) - 1.0
    grad_neg = jax.nn.sigmoid(negative) / neg_total
    grad_query = grad_pos[:, None] * tail + jnp.dot(grad_neg, negatives, precision=PRECISE)
    grad_tail = grad_pos[:, None] * query
    grad_negs = jnp.dot(grad_neg.T, query, precision=PRECISE)
    own_count = neg_slots.shape[0]
    totals = lax.psum(grad_negs, "grp")
    mine = lax.dynamic_slice_in_dim(totals, lax.axis_index("grp") * own_count, own_count, 0)
    grad_head = jnp.einsum(
        "kef,kdf->ked", grad_query.reshape(kinds, per_rel, width), relations, precision=PRECISE
    ).reshape(kinds * per_rel, width)
    slot_grad = jnp.zeros((slot_count, width), jnp.float32).at[source].add(grad_head)
    slot_grad = slot_grad.at[target].add(grad_tail)
    slot_grad = slot_grad.at[neg_slots].add(mine)
    returned = lax.all_to_all(
        slot_grad.reshape(peers, sent, width), "grp", split_axis=0, concat_axis=0, tiled=True
    )
    row_grad = (
        jnp.zeros(table.shape, jnp.float32)
        .at[touched.reshape(-1)]
        .add(returned.reshape(slot_count, width))
    )
    new_state = row_state + jnp.mean(row_grad * row_grad, -1)
    new_table = table - LEARN_RATE * row_grad / (jnp.sqrt(new_state)[:, None] + EPSILON)
    return (new_table, new_state)


def solution(mesh):
    return jax.shard_map(
        per_device,
        mesh=mesh,
        in_specs=(
            P(("grp", "rep"), None),
            P(("grp", "rep")),
            P(),
            P(("grp", "rep"), None),
            P(("grp", "rep")),
            P(("grp", "rep")),
            P(("grp", "rep")),
        ),
        out_specs=(P(("grp", "rep"), None), P(("grp", "rep"))),
        check_vma=False,
    )
```

profile of v0, /device:TPU:6, one launch (start us, length us, event | category | flops | bytes accessed | tf_op | source)
XLA Modules:
  0.0 806.9 jit_solution(1788933596971726089)
XLA Ops:
  7.2 0.0 copy-start
  7.2 0.8 compare_and_fusion
  8.0 0.7 compare_select_fusion.1
  8.7 0.1 copy.30
  8.8 0.1 copy.31
  8.9 0.1 reshape.106
  9.0 1.2 copy.41
  10.2 8.9 %gather_fusion = f32[2048,400]{1,0:T(8,128)} fusion(f32[256,400]{1,0:T(8,128)S(1)} %copy.41, s32[2048]{0:T(1024)S(1)} %broadcast_clamp_fusion), kind=kCustom, calls=%fused_computation.2 | custom fusion | bytes 6561792 | tf_op jit(solution)/shard_map/jit(_take)/gather | solution.py:18
  19.1 3.8 broadcast_select_fusion
  22.9 19.1 %all-to-all-start = ((f32[64,32,400]{2,1,0:T(8,128)}), f32[64,32,400]{2,1,0:T(8,128)}, u32[]{:S(2)}, u32[]{:S(2)}) async-start(f32[64,32,400]{2,1,0:T(8,128)} %broadcast_select_fusion), calls=%async_computation | async-start | bytes 8388608 | tf_op jit(solution)/shard_map/all_to_all | solution.py:19
  42.1 0.0 all-reduce.2.cloned.1.call-start
  42.1 0.0 copy-done.4
  42.2 0.0 copy-done.5
  42.2 0.0 copy-done.7
  42.3 187.6 %all-to-all-done = f32[64,32,400]{2,1,0:T(8,128)} async-done(((f32[64,32,400]{2,1,0:T(8,128)}), f32[64,32,400]{2,1,0:T(8,128)}, u32[]{:S(2)}, u32[]{:S(2)}) %all-to-all-start) | async-done | bytes 3276832 | tf_op jit(solution)/shard_map/all_to_all | solution.py:19
  229.9 2.7 gather_fusion.1
  232.6 0.1 select_bitcast_fusion
  232.7 80.4 %all-gather = f32[64,2,400]{2,1,0:T(2,128)S(1)} all-gather(f32[1,2,400]{2,1,0:T(2,128)S(1)} %select_bitcast_fusion), channel_id=1, replica_groups=mesh['grp'=64,'rep'=8] {'grp'}, dimensions={0}, use_global_device_ids=true | all-gather | bytes 208000 | tf_op jit(solution)/shard_map/all_gather | solution.py:27
  313.1 0.2 reshape.161
  313.3 4.9 gather_fusion.3
  318.2 4.4 gather_fusion.2
  322.6 2.4 copy.36
  325.0 0.1 broadcast_select_fusion.1
  325.2 3.3 convolution_bitcast_fusion
  328.5 0.1 copy.48
  328.6 0.2 multiply_reduce_fusion
  328.8 1.9 fusion.5
  330.7 0.0 copy-start.2
  330.7 0.7 copy-done.2
  331.4 1.8 fusion.13
  333.2 3.0 convolution_add_fusion
  336.2 1.0 broadcast_multiply_fusion
  337.2 0.0 all-reduce.2.cloned.1.call-update
  337.2 1.5 copy.40
  338.7 5.6 fusion.6
  344.3 6.6 scatter_custom_fusion
  350.9 7.7 scatter_fusion
  358.6 235.1 %all-reduce.2.cloned.1.call-done = f32[128,400]{1,0:T(8,128)} async-done(((f32[128,400]{1,0:T(8,128)}), f32[128,400]{1,0:T(8,128)}) %all-reduce.2.cloned.1.call-update) | async-done | bytes 204816 | tf_op jit(solution)/shard_map/psum | solution.py:37
  593.7 4.9 scatter_custom_fusion.2
  598.6 9.0 %all-to-all-start.1 = ((f32[64,32,400]{2,1,0:T(8,128)}), f32[64,32,400]{2,1,0:T(8,128)}, u32[]{:S(2)}, u32[]{:S(2)}) async-start(f32[64,32,400]{2,1,0:T(8,128)} %bitcast.25), calls=%async_computation.1 | async-start | bytes 8388608 | tf_op jit(solution)/shard_map/all_to_all | solution.py:45
  607.6 0.1 copy.29
  607.7 0.1 reshape.80
  607.8 177.1 %all-to-all-done.1 = f32[64,32,400]{2,1,0:T(8,128)} async-done(((f32[64,32,400]{2,1,0:T(8,128)}), f32[64,32,400]{2,1,0:T(8,128)}, u32[]{:S(2)}, u32[]{:S(2)}) %all-to-all-start.1) | async-done | bytes 3276832 | tf_op jit(solution)/shard_map/all_to_all | solution.py:45
  784.9 13.4 %scatter_custom_fusion.3 = f32[256,400]{1,0:T(8,128)S(1)} fusion(s32[2048]{0:T(1024)S(1)} %bitcast.34, f32[2048,400]{1,0:T(8,128)} %bitcast.7, f32[]{:T(128)} %constant.25.clone.1), kind=kCustom, calls=%fused_computation.26 | custom fusion | flops 819200 | bytes 410112 | tf_op jit(solution)/shard_map/scatter-add | solution.py:51
  798.3 0.1 multiply_reduce_fusion.1
  798.4 0.6 sqrt_add_fusion
  799.0 0.1 divide_subtract_fusion
  799.1 0.9 copy.42
  (22 shorter events, 0.1 us)
Async XLA Ops:
  7.2 318.0 %copy-start = (f32[2,400,400]{2,1,0:T(8,128)S(1)}, f32[2,400,400]{2,1,0:T(8,128)}, u32[]{:S(2)}) copy-start(f32[2,400,400]{2,1,0:T(8,128)} %param.11) | copy-start | bytes 3840004
  22.9 19.2 %copy-start.4 = (s32[512]{0:T(512)S(1)}, s32[512]{0:T(512)}, u32[]{:S(2)}) copy-start(s32[512]{0:T(512)} %param.14) | copy-start | bytes 6148
  22.9 19.2 %copy-start.5 = (s32[512]{0:T(512)S(1)}, s32[512]{0:T(512)}, u32[]{:S(2)}) copy-start(s32[512]{0:T(512)} %param.13) | copy-start | bytes 6148
  22.9 19.3 %copy-start.7 = (s32[2]{0:T(128)S(1)}, s32[2]{0:T(128)}, u32[]{:S(2)}) copy-start(s32[2]{0:T(128)} %param.15) | copy-start | bytes 28
  22.9 206.9 %all-to-all-start = ((f32[64,32,400]{2,1,0:T(8,128)}), f32[64,32,400]{2,1,0:T(8,128)}, u32[]{:S(2)}, u32[]{:S(2)}) async-start(f32[64,32,400]{2,1,0:T(8,128)} %broadcast_select_fusion), calls=%async_computation | async-start | bytes 8388608 | tf_op jit(solution)/shard_map/all_to_all | solution.py:19
  42.1 551.6 %all-reduce.2.cloned.1.call-start = ((), (), s32[]{:S(2)}) async-start(), calls=%async_computation.2 | async-start | bytes 524288 | tf_op jit(solution)/shard_map/psum | solution.py:37
  325.0 3.6 copy-start.1
  330.7 0.7 copy-start.2
  598.6 9.1 %copy-start.3 = (s32[64,32]{0,1:T(8,128)S(1)}, s32[64,32]{0,1:T(8,128)}, u32[]{:S(2)}) copy-start(s32[64,32]{0,1:T(8,128)} %param.12) | copy-start | bytes 24580
  598.6 199.8 %copy-start.6 = (f32[256]{0:T(256)S(1)}, f32[256]{0:T(256)}, u32[]{:S(2)}) copy-start(f32[256]{0:T(256)} %param.10) | copy-start | bytes 3076
  598.6 186.3 %all-to-all-start.1 = ((f32[64,32,400]{2,1,0:T(8,128)}), f32[64,32,400]{2,1,0:T(8,128)}, u32[]{:S(2)}, u32[]{:S(2)}) async-start(f32[64,32,400]{2,1,0:T(8,128)} %bitcast.25), calls=%async_computation.1 | async-start | bytes 8388608 | tf_op jit(solution)/shard_map/all_to_all | solution.py:45
Sparse Core Ops, SparseCore 0:
  337.3 256.3 all-reduce.1
where the time goes:
time: 808 us; the launch traced here: 807 us
  waiting for transfers between devices  600 us (74%)
  blocking collectives  80.4 us (10%)
  other arithmetic  40.2 us (5%)
  local copies, waits for them, and re-layouts  28.4 us (4%)
  starting transfers between devices  28.2 us (3%)
  matrix products  15.6 us (2%)
  between operations  14.3 us (2%)
    psum x1, waiting for transfers between devices, per_device(): totals = lax.psum(grad_negs, 'grp')  235 us
    all_to_all x1, waiting for transfers between devices, per_device(): lax.all_to_all(outgoing, 'grp', split_axis=0, concat_axis=0, tiled=True)  188 us
    all_to_all x1, waiting for transfers between devices, per_device(): lax.all_to_all(slot_grad.reshape(peers, sent, width), 'grp', split_axis=0...  177 us
    all_gather x1, blocking collectives, per_device(): negatives = lax.all_gather(own_neg, 'grp', axis=0, tiled=True)  80.4 us
    all_to_all x1, starting transfers between devices, per_device(): lax.all_to_all(outgoing, 'grp', split_axis=0, concat_axis=0, tiled=True)  19.1 us
  transfers between devices with their start and end apart: 3, of which 3 were waited for; matrix products, arithmetic and copies ran while one was open for 3% of the time, Pallas kernels for 0%

commit v1 on v0

v1 whole, which is shorter than its diff:
```python
import jax
import jax.numpy as jnp
from jax import lax
from jax.sharding import PartitionSpec as P

PRECISE = lax.Precision.HIGHEST
LEARN_RATE = 0.1
EPSILON = 1e-06
LANES = 128


def exchange(blocks):
    return lax.all_to_all(blocks, "grp", split_axis=0, concat_axis=0, tiled=True)


def take_rows(rows, ids):
    return jnp.take(rows, ids, axis=0, mode="clip")


def to_lanes(rows, peers):
    width = rows.shape[1]
    wide = -(-width // LANES) * LANES
    return jnp.pad(rows, ((0, 0), (0, wide - width))).reshape(peers, -1, LANES)


def per_device(table, row_state, relations, touched, source, target, neg_slots):
    width = table.shape[1]
    peers, sent = touched.shape
    kinds = relations.shape[0]
    per_rel = source.shape[0] // kinds
    slot_count = peers * sent
    own_count = neg_slots.shape[0]
    neg_total = peers * own_count
    outgoing = take_rows(table, touched.reshape(-1))
    slots = exchange(outgoing.reshape(peers, -1, LANES)).reshape(slot_count, width)
    own_neg = to_lanes(take_rows(slots, neg_slots), 1)
    gathered = exchange(jnp.broadcast_to(own_neg, (peers,) + own_neg.shape[1:]))
    negatives = gathered.reshape(neg_total, -1)[:, :width]
    head = take_rows(slots, source)
    tail = take_rows(slots, target)
    query = jnp.einsum(
        "ked,kdf->kef", head.reshape(kinds, per_rel, width), relations, precision=PRECISE
    ).reshape(kinds * per_rel, width)
    positive = jnp.sum(query * tail, -1)
    negative = jnp.dot(query, negatives.T, precision=PRECISE)
    grad_pos = jax.nn.sigmoid(positive) - 1.0
    grad_neg = jax.nn.sigmoid(negative) / neg_total
    grad_negs = jnp.dot(grad_neg.T, query, precision=PRECISE)
    shares = exchange(to_lanes(grad_negs, peers))
    mine = jnp.sum(shares, 0).reshape(own_count, -1)[:, :width]
    grad_query = grad_pos[:, None] * tail + jnp.dot(grad_neg, negatives, precision=PRECISE)
    grad_tail = grad_pos[:, None] * query
    grad_head = jnp.einsum(
        "kef,kdf->ked", grad_query.reshape(kinds, per_rel, width), relations, precision=PRECISE
    ).reshape(kinds * per_rel, width)
    slot_grad = jnp.zeros((slot_count, width), jnp.float32).at[source].add(grad_head)
    slot_grad = slot_grad.at[target].add(grad_tail)
    slot_grad = slot_grad.at[neg_slots].add(mine)
    returned = exchange(slot_grad.reshape(peers, -1, LANES)).reshape(slot_count, width)
    row_grad = jnp.zeros(table.shape, jnp.float32).at[touched.reshape(-1)].add(returned)
    new_state = row_state + jnp.mean(row_grad * row_grad, -1)
    new_table = table - LEARN_RATE * row_grad / (jnp.sqrt(new_state)[:, None] + EPSILON)
    return (new_table, new_state)


def solution(mesh):
    return jax.shard_map(
        per_device,
        mesh=mesh,
        in_specs=(
            P(("grp", "rep"), None),
            P(("grp", "rep")),
            P(),
            P(("grp", "rep"), None),
            P(("grp", "rep")),
            P(("grp", "rep")),
            P(("grp", "rep")),
        ),
        out_specs=(P(("grp", "rep"), None), P(("grp", "rep"))),
        check_vma=False,
    )
```

time: 808 us -> 475 us (0.59)
  waiting for transfers between devices: 600 us -> 310 us
  blocking collectives: 80.4 us -> 0 us
  local copies, waits for them, and re-layouts: 28.4 us -> 59.1 us
  starting transfers between devices: 28.2 us -> 53.7 us
  between operations: 14.3 us -> 0.9 us
    psum x1 -> x0, waiting for transfers between devices: 235 us -> none  [per_device(): totals = lax.psum(grad_negs, 'grp')]
    all_gather x1 -> x0, blocking collectives: 80.4 us -> none  [per_device(): negatives = lax.all_gather(own_neg, 'grp', axis=0, tiled=True)]
    all_to_all x2 -> x4, waiting for transfers between devices: 365 us -> 310 us  [exchange(): lax.all_to_all(blocks, 'grp', split_axis=0, concat_axis=0, tiled=True)]
    reshape x0 -> x7, local copies, waits for them, and re-layouts: none -> 29 us  [the longest x1 6.66 us: per_device(): exchange(slot_grad.reshape(peers, -1, LANES)).reshape(slot_count, width)]
    all_to_all x2 -> x4, starting transfers between devices: 28.2 us -> 53.7 us  [exchange(): lax.all_to_all(blocks, 'grp', split_axis=0, concat_axis=0, tiled=True)]
    gather x5 -> x6, local copies, waits for them, and re-layouts: 23.4 us -> 23.2 us  [take_rows(): return jnp.take(rows, ids, axis=0, mode='clip')]
  transfers between devices with their start and end apart: 3 -> 4, of which waited for: 3 -> 3; matrix products, arithmetic and copies ran while one was open for 3% -> 8% of each run, Pallas kernels for 0% -> 0%
where the time goes in v1:
time: 475 us; the launch traced here: 473 us
  waiting for transfers between devices  310 us (65%)
  local copies, waits for them, and re-layouts  59.1 us (12%)
  starting transfers between devices  53.7 us (11%)
  other arithmetic  35.2 us (7%)
  matrix products  14.4 us (3%)
    all_to_all x4, waiting for transfers between devices, exchange(): lax.all_to_all(blocks, 'grp', split_axis=0, concat_axis=0, tiled=True)  310 us
    all_to_all x4, starting transfers between devices, exchange(): lax.all_to_all(blocks, 'grp', split_axis=0, concat_axis=0, tiled=True)  53.7 us
    gather x6, local copies, waits for them, and re-layouts, take_rows(): return jnp.take(rows, ids, axis=0, mode='clip')  23.2 us
    scatter-add x1, other arithmetic, per_device(): jnp.zeros(table.shape, jnp.float32).at[touched.reshape(-1)].add(returned)  13.4 us
  transfers between devices with their start and end apart: 4, of which 3 were waited for; matrix products, arithmetic and copies ran while one was open for 8% of the time, Pallas kernels for 0%

profile of v1, /device:TPU:6, one launch (start us, length us, event | category | flops | bytes accessed | tf_op | source)
XLA Modules:
  0.0 473.5 jit_solution(3058882633925827270)
XLA Ops:
  0.6 0.0 copy-start
  0.6 0.9 copy.14
  1.6 0.1 reshape.108
  1.6 1.2 copy.28
  2.9 8.9 %gather_fusion = f32[2048,400]{1,0:T(8,128)} fusion(f32[256,400]{1,0:T(8,128)S(1)} %copy.28, s32[2048]{0:T(1024)S(1)} %broadcast_clamp_fusion), kind=kCustom, calls=%fused_computation | custom fusion | bytes 6561792 | tf_op jit(solution)/shard_map/jit(_take)/gather | solution.py:17
  11.8 6.5 %reshape.93 = f32[64,100,128]{2,1,0:T(8,128)} reshape(f32[2048,400]{1,0:T(8,128)} %gather_fusion) | data formatting | bytes 6553600 | tf_op jit(solution)/shard_map/reshape | solution.py:35
  18.2 19.1 %all-to-all-start = ((f32[64,100,128]{2,1,0:T(8,128)}), f32[64,100,128]{2,1,0:T(8,128)}, u32[]{:S(2)}, u32[]{:S(2)}) async-start(f32[64,100,128]{2,1,0:T(8,128)} %reshape.93), calls=%async_computation | async-start | bytes 6815744 | tf_op jit(solution)/shard_map/all_to_all | solution.py:13
  37.4 0.0 copy-start.3
  37.4 154.3 %all-to-all-done = f32[64,100,128]{2,1,0:T(8,128)} async-done(((f32[64,100,128]{2,1,0:T(8,128)}), f32[64,100,128]{2,1,0:T(8,128)}, u32[]{:S(2)}, u32[]{:S(2)}) %all-to-all-start) | async-done | bytes 3276832 | tf_op jit(solution)/shard_map/all_to_all | solution.py:13
  191.7 6.7 %reshape.94 = f32[2048,400]{1,0:T(8,128)} reshape(f32[64,100,128]{2,1,0:T(8,128)} %all-to-all-done) | data formatting | bytes 6553600 | tf_op jit(solution)/shard_map/reshape | solution.py:35
  198.4 2.7 gather_fusion.3
  201.1 0.7 broadcast_in_dim.46
  201.9 7.7 %all-to-all-start.1 = ((f32[64,8,128]{2,1,0:T(8,128)}), f32[64,8,128]{2,1,0:T(8,128)}, u32[]{:S(2)}, u32[]{:S(2)}) async-start(f32[64,8,128]{2,1,0:T(8,128)} %broadcast_in_dim.46), calls=%async_computation.1 | async-start | bytes 524288 | tf_op jit(solution)/shard_map/all_to_all | solution.py:13
  209.7 4.2 gather_fusion.2
  213.9 4.9 %gather_fusion.1 = f32[512,400]{1,0:T(8,128)} fusion(f32[2048,400]{1,0:T(8,128)} %reshape.94, s32[1024]{0:T(1024)S(1)} %pad_clamp_fusion.2), kind=kCustom, calls=%fused_computation.1 | custom fusion | bytes 1640448 | tf_op jit(solution)/shard_map/jit(_take)/gather | solution.py:17
  218.8 1.2 copy.21
  220.0 1.2 copy.20
  221.2 4.8 %multiply_reduce_fusion = (f32[2,256]{1,0:T(2,128)S(1)}, f32[2,256,400]{1,2,0:T(8,128)S(1)}) fusion(f32[2,256,400]{1,2,0:T(8,128)} %copy.20, f32[2,256,400]{2,1,0:T(8,128)} %bitcast.24, f32[2,400,400]{2,1,0:T(8,128)S(1)} %copy-done), kind=kOutput, calls=%fused_computation.19 | convolution fusion | flops 983449088 | bytes 3739648 | tf_op jit(solution)/shard_map/ked,kdf->kef/dot_general | solution.py:41
  226.0 0.1 copy.38
  226.1 3.6 all-to-all-done.1
  229.7 1.0 reshape.97
  230.7 1.9 fusion.5
  232.6 0.0 copy-start.1
  232.6 0.7 copy-done.1
  233.3 1.1 fusion.15
  234.4 0.7 pad.9.clone
  235.1 1.7 reshape.100
  236.8 11.8 %all-to-all-start.2 = ((f32[64,8,128]{2,1,0:T(8,128)}), f32[64,8,128]{2,1,0:T(8,128)}, u32[]{:S(2)}, u32[]{:S(2)}) async-start(f32[64,8,128]{2,1,0:T(8,128)} %reshape.100), calls=%async_computation.2 | async-start | bytes 524288 | tf_op jit(solution)/shard_map/all_to_all | solution.py:13
  248.6 1.0 broadcast_multiply_fusion
  249.6 1.5 copy.26
  251.1 2.1 convolution_add_fusion
  253.2 4.6 fusion.6
  257.8 6.5 %scatter_custom_fusion = f32[2048,400]{1,0:T(8,128)} fusion(s32[512]{0:T(512)S(1)} %compare_select_fusion.2, f32[512,400]{1,0:T(8,128)} %bitcast.27, f32[]{:T(128)} %constant.10.clone.1), kind=kCustom, calls=%fused_computation.8 | custom fusion | flops 204800 | bytes 3277312 | tf_op jit(solution)/shard_map/scatter-add | solution.py:56
  264.3 7.7 %scatter_fusion = f32[2048,400]{1,0:T(8,128)} fusion(f32[2048,400]{1,0:T(8,128)} %scatter_custom_fusion, s32[512]{0:T(512)S(1)} %compare_select_fusion.1, f32[512,400]{1,0:T(8,128)S(1)} %copy.26), kind=kCustom, calls=%fused_computation.5 | custom fusion | flops 204800 | bytes 2459648 | tf_op jit(solution)/shard_map/scatter-add | solution.py:57
  272.0 0.0 all-to-all-done.2
  272.0 1.0 reduce_sum.28
  273.0 4.7 scatter_custom_fusion.2
  277.7 6.5 %reshape.102 = f32[64,100,128]{2,1,0:T(8,128)} reshape(f32[2048,400]{1,0:T(8,128)} %scatter_custom_fusion.2) | data formatting | bytes 6553600 | tf_op jit(solution)/shard_map/reshape | solution.py:59
  284.2 15.1 %all-to-all-start.3 = ((f32[64,100,128]{2,1,0:T(8,128)}), f32[64,100,128]{2,1,0:T(8,128)}, u32[]{:S(2)}, u32[]{:S(2)}) async-start(f32[64,100,128]{2,1,0:T(8,128)} %reshape.102), calls=%async_computation.3 | async-start | bytes 6815744 | tf_op jit(solution)/shard_map/all_to_all | solution.py:13
  299.3 0.1 reshape.92
  299.4 0.0 copy-start.4
  299.4 152.2 %all-to-all-done.3 = f32[64,100,128]{2,1,0:T(8,128)} async-done(((f32[64,100,128]{2,1,0:T(8,128)}), f32[64,100,128]{2,1,0:T(8,128)}, u32[]{:S(2)}, u32[]{:S(2)}) %all-to-all-start.3) | async-done | bytes 3276832 | tf_op jit(solution)/shard_map/all_to_all | solution.py:13
  451.7 6.7 %reshape.166 = f32[2048,400]{1,0:T(8,128)} reshape(f32[64,100,128]{2,1,0:T(8,128)} %all-to-all-done.3) | data formatting | bytes 6553600 | tf_op jit(solution)/shard_map/reshape | solution.py:59
  458.4 13.4 %scatter_custom_fusion.3 = f32[256,400]{1,0:T(8,128)S(1)} fusion(s32[2048]{0:T(1024)S(1)} %bitcast.30, f32[2048,400]{1,0:T(8,128)} %reshape.166, f32[]{:T(128)} %constant.10.clone.1), kind=kCustom, calls=%fused_computation.23 | custom fusion | flops 819200 | bytes 410112 | tf_op jit(solution)/shard_map/scatter-add | solution.py:60
  471.7 0.1 multiply_reduce_fusion.1
  471.8 0.6 sqrt_add_fusion
  472.4 0.1 divide_subtract_fusion
  472.5 0.9 copy.29
  (20 shorter events, 0.1 us)
Async XLA Ops:
  0.6 220.6 %copy-start = (f32[2,400,400]{2,1,0:T(8,128)S(1)}, f32[2,400,400]{2,1,0:T(8,128)}, u32[]{:S(2)}) copy-start(f32[2,400,400]{2,1,0:T(8,128)} %param.9) | copy-start | bytes 3840004
  18.2 19.1 %copy-start.2 = (s32[512]{0:T(512)S(1)}, s32[512]{0:T(512)}, u32[]{:S(2)}) copy-start(s32[512]{0:T(512)} %param.11) | copy-start | bytes 6148
  18.2 19.1 %copy-start.5 = (s32[2]{0:T(128)S(1)}, s32[2]{0:T(128)}, u32[]{:S(2)}) copy-start(s32[2]{0:T(128)} %param.13) | copy-start | bytes 28
  18.2 173.5 %all-to-all-start = ((f32[64,100,128]{2,1,0:T(8,128)}), f32[64,100,128]{2,1,0:T(8,128)}, u32[]{:S(2)}, u32[]{:S(2)}) async-start(f32[64,100,128]{2,1,0:T(8,128)} %reshape.93), calls=%async_computation | async-start | bytes 6815744 | tf_op jit(solution)/shard_map/all_to_all | solution.py:13
  37.4 172.2 %copy-start.3 = (s32[512]{0:T(512)S(1)}, s32[512]{0:T(512)}, u32[]{:S(2)}) copy-start(s32[512]{0:T(512)} %param.12) | copy-start | bytes 6148
  201.9 27.8 %all-to-all-start.1 = ((f32[64,8,128]{2,1,0:T(8,128)}), f32[64,8,128]{2,1,0:T(8,128)}, u32[]{:S(2)}, u32[]{:S(2)}) async-start(f32[64,8,128]{2,1,0:T(8,128)} %broadcast_in_dim.46), calls=%async_computation.1 | async-start | bytes 524288 | tf_op jit(solution)/shard_map/all_to_all | solution.py:13
  232.6 0.7 copy-start.1
  236.8 35.2 %all-to-all-start.2 = ((f32[64,8,128]{2,1,0:T(8,128)}), f32[64,8,128]{2,1,0:T(8,128)}, u32[]{:S(2)}, u32[]{:S(2)}) async-start(f32[64,8,128]{2,1,0:T(8,128)} %reshape.100), calls=%async_computation.2 | async-start | bytes 524288 | tf_op jit(solution)/shard_map/all_to_all | solution.py:13
  284.2 167.4 %all-to-all-start.3 = ((f32[64,100,128]{2,1,0:T(8,128)}), f32[64,100,128]{2,1,0:T(8,128)}, u32[]{:S(2)}, u32[]{:S(2)}) async-start(f32[64,100,128]{2,1,0:T(8,128)} %reshape.102), calls=%async_computation.3 | async-start | bytes 6815744 | tf_op jit(solution)/shard_map/all_to_all | solution.py:13
  299.4 172.4 %copy-start.4 = (f32[256]{0:T(256)S(1)}, f32[256]{0:T(256)}, u32[]{:S(2)}) copy-start(f32[256]{0:T(256)} %param.8) | copy-start | bytes 3076

commit v2 on v1

--- a/solution.py
+++ b/solution.py
@@ -1,12 +1,19 @@
+import functools
+
 import jax
 import jax.numpy as jnp
 from jax import lax
+from jax.experimental import pallas as pl
+from jax.experimental.pallas import tpu as pltpu
 from jax.sharding import PartitionSpec as P
 
 PRECISE = lax.Precision.HIGHEST
 LEARN_RATE = 0.1
 EPSILON = 1e-06
 LANES = 128
+VMEM = 56 * 1024 * 1024
+F32 = jnp.float32
+BF16 = jnp.bfloat16
 
 
 def exchange(blocks):
@@ -23,7 +30,7 @@
     return jnp.pad(rows, ((0, 0), (0, wide - width))).reshape(peers, -1, LANES)
 
 
-def per_device(table, row_state, relations, touched, source, target, neg_slots):
+def full_path(table, row_state, relations, touched, source, target, neg_slots):
     width = table.shape[1]
     peers, sent = touched.shape
     kinds = relations.shape[0]
@@ -53,14 +60,398 @@
     grad_head = jnp.einsum(
         "kef,kdf->ked", grad_query.reshape(kinds, per_rel, width), relations, precision=PRECISE
     ).reshape(kinds * per_rel, width)
-    slot_grad = jnp.zeros((slot_count, width), jnp.float32).at[source].add(grad_head)
+    slot_grad = jnp.zeros((slot_count, width), F32).at[source].add(grad_head)
     slot_grad = slot_grad.at[target].add(grad_tail)
     slot_grad = slot_grad.at[neg_slots].add(mine)
     returned = exchange(slot_grad.reshape(peers, -1, LANES)).reshape(slot_count, width)
-    row_grad = jnp.zeros(table.shape, jnp.float32).at[touched.reshape(-1)].add(returned)
+    row_grad = jnp.zeros(table.shape, F32).at[touched.reshape(-1)].add(returned)
     new_state = row_state + jnp.mean(row_grad * row_grad, -1)
     new_table = table - LEARN_RATE * row_grad / (jnp.sqrt(new_state)[:, None] + EPSILON)
-    return (new_table, new_state)
+    return new_table.T, new_state.reshape(1, -1)
+
+
+REGION = 24
+CAP = REGION - 1
+PARTS = 3
+BLOCK = PARTS * REGION
+TAIL = 16
+PER_LINE = LANES // TAIL
+WIDE = (PARTS + 1) * LANES
+
+
+def iota(shape, dim):
+    return lax.broadcasted_iota(jnp.int32, shape, dim)
+
+
+def pieces(x, count):
+    out = []
+    for _ in range(count):
+        piece = x.astype(BF16)
+        out.append(piece)
+        x = x - piece.astype(F32)
+    return out
+
+
+def dot(a, b, a_dim=1, b_dim=0):
+    return lax.dot_general(a, b, (((a_dim,), (b_dim,)), ((), ())), preferred_element_type=F32)
+
+
+def pick(onehot, x, count, b_dim=0):
+    total = None
+    for piece in reversed(pieces(x, count)):
+        term = dot(onehot, piece, 1, b_dim)
+        total = term if total is None else total + term
+    return total
+
+
+def dot3(a, b, a_dim=1, b_dim=0):
+    a_hi, a_lo = a if isinstance(a, tuple) else pieces(a, 2)
+    b_hi, b_lo = b if isinstance(b, tuple) else pieces(b, 2)
+    small = dot(a_lo, b_hi, a_dim, b_dim) + dot(a_hi, b_lo, a_dim, b_dim)
+    return small + dot(a_hi, b_hi, a_dim, b_dim)
+
+
+def spread(x):
+    step = TAIL
+    while step < LANES:
+        x = x + pltpu.roll(x, step, 1)
+        step *= 2
+    return x
+
+
+def call(kernel, outs, **kw):
+    return pl.pallas_call(
+        kernel,
+        out_shape=outs,
+        compiler_params=pltpu.CompilerParams(vmem_limit_bytes=VMEM),
+        **kw,
+    )
+
+
+def shaped(*shape, dtype=F32):
+    return jax.ShapeDtypeStruct(shape, dtype)
+
+
+def mark_kernel(sent, ids_ref, marks_ref, place_ref):
+    peers = marks_ref.shape[0]
+    ids = ids_ref[...]
+    count = ids.shape[1]
+    owner = lax.shift_right_arithmetic(ids, sent.bit_length() - 1)
+    within = lax.bitwise_and(ids, sent - 1)
+    at_owner = (iota((peers, count), 0) == owner).astype(BF16)
+    at_within = (iota((LANES, count), 0) == within).astype(BF16)
+    marks = dot(at_owner, at_within, 1, 1)
+    used = jnp.where(dot(at_within, at_owner, 1, 1) > 0.0, 1.0, 0.0).astype(BF16)
+    upto = (iota((LANES, LANES), 1) <= iota((LANES, LANES), 0)).astype(BF16)
+    rank = dot(upto, used)
+    flag = jnp.where(jnp.max(rank) > CAP, 1.0, 0.0)
+    lane = iota(marks.shape, 1)
+    marks_ref[...] = jnp.where(lane == sent, flag, jnp.where(marks > 0.0, 1.0, 0.0))
+    mine = dot(rank.astype(BF16), at_owner) * at_within.astype(F32)
+    order = jnp.sum(mine, 0, keepdims=True).astype(jnp.int32)
+    place_ref[...] = owner * REGION + order - 1
+
+
+def pack_kernel(sent, marks_ref, touched_ref, table_ref, out_ref, rows_ref, onehot):
+    peers = marks_ref.shape[0]
+    lane = iota((peers, LANES), 1)
+    marks = jnp.where(lane < sent, marks_ref[...], 0.0)
+    upto = (iota((LANES, LANES), 0) <= iota((LANES, LANES), 1)).astype(BF16)
+    rank = jnp.where(marks > 0.0, dot(marks.astype(BF16), upto), 0.0)
+    local = touched_ref[...].astype(F32) + 1.0
+    owned = table_ref.shape[1]
+    spot = iota((peers, owned), 1)
+    rows = jnp.full((peers, LANES), -1, jnp.int32)
+    for k in range(CAP):
+        chosen = jnp.where(rank == k + 1.0, local, 0.0)
+        row = jnp.sum(chosen, 1, keepdims=True).astype(jnp.int32) - 1
+        rows = jnp.where(lane == k, row, rows)
+        onehot[k * peers : (k + 1) * peers, :] = (spot == row).astype(F32).astype(BF16)
+    rows_ref[...] = rows
+    table = table_ref[...]
+    main = PARTS * LANES
+    wide = jnp.concatenate([table[:main]] + [table[main:]] * PER_LINE, 0)
+    wide = pieces(wide, 3)
+    group = lane // TAIL
+    for part in range(PARTS):
+        first = part * PER_LINE
+        last = min(first + PER_LINE, CAP)
+        chosen = onehot[first * peers : last * peers, :]
+        got = dot(chosen, wide[2], 1, 1) + dot(chosen, wide[1], 1, 1)
+        got = got + dot(chosen, wide[0], 1, 1)
+        line = jnp.zeros((peers, LANES), F32)
+        for k in range(first, last):
+            mine = got[(k - first) * peers : (k - first + 1) * peers]
+            for t in range(PARTS):
+                out_ref[pl.ds(t * REGION + k, peers, stride=BLOCK), :] = mine[
+                    :, t * LANES : (t + 1) * LANES
+                ]
+            line = line + jnp.where(group == k - first, mine[:, main:], 0.0)
+        out_ref[pl.ds(part * REGION + CAP, peers, stride=BLOCK), :] = line
+
+
+def unpack(ref, peers):
+    count = peers * REGION
+    parts, tails = [], []
+    for t in range(PARTS):
+        part = ref[:, t * REGION : (t + 1) * REGION, :]
+        parts.append(part.reshape(count, LANES))
+        tails.append(jnp.broadcast_to(part[:, CAP:, :], (peers, PER_LINE, LANES)))
+    tails = jnp.concatenate(tails, 1)
+    own = iota(tails.shape, 2) // TAIL == iota(tails.shape, 1) % PER_LINE
+    parts.append(jnp.where(own, tails, 0.0).reshape(count, LANES))
+    return parts
+
+
+def negs_kernel(place_ref, block_ref, out_ref):
+    n = pl.program_id(0)
+    k = lax.rem(place_ref[n], REGION)
+    part = lax.div(k, PER_LINE)
+    line = block_ref[0, pl.ds(part * REGION + CAP, 1), :]
+    shift = lax.rem(LANES - TAIL * lax.rem(k, PER_LINE), LANES)
+    line = pltpu.roll(line, shift, 1)
+    line = jnp.where(iota(line.shape, 1) < TAIL, line, 0.0)
+    rows = [block_ref[0, pl.ds(t * REGION + k, 1), :] for t in range(PARTS)] + [line]
+    peers = out_ref.shape[0]
+    depth = PARTS + 1
+    for i in range(out_ref.shape[1] // depth):
+
+        @pl.when(n == i)
+        def _():
+            for t in range(depth):
+                out_ref[:, i * depth + t : i * depth + t + 1, :] = jnp.broadcast_to(
+                    rows[t].reshape(1, 1, LANES), (peers, 1, LANES)
+                )
+
+
+def query_kernel(block_ref, place_ref, rel_hi_ref, rel_lo_ref, query_ref, tail_ref, pos_ref):
+    peers = block_ref.shape[0]
+    edges = query_ref.shape[0]
+    kinds = rel_hi_ref.shape[0]
+    per_rel = edges // kinds
+    count = peers * REGION
+    slots = [pieces(part, 2) for part in unpack(block_ref, peers)]
+    hi = jnp.concatenate([p[0] for p in slots], 1)
+    lo = jnp.concatenate([p[1] for p in slots], 1)
+    main = PARTS * LANES
+
+    def rows_at(start, size):
+        spot = place_ref[start : start + size, :]
+        chosen = (iota((size, count), 1) == spot).astype(F32).astype(BF16)
+        got = dot(chosen, lo) + dot(chosen, hi)
+        return jnp.concatenate([got[:, :main], spread(got[:, main:])], 1)
+
+    for kind in range(kinds):
+        start = kind * per_rel
+        head = rows_at(start, per_rel)
+        query = dot3(head, (rel_hi_ref[kind], rel_lo_ref[kind]))
+        tail = rows_at(edges + start, per_rel)
+        query_ref[start : start + per_rel, :] = query
+        tail_ref[start : start + per_rel, :] = tail
+        positive = jnp.sum(query * tail, 1, keepdims=True)
+        pos_ref[start : start + per_rel, :] = jax.nn.sigmoid(positive) - 1.0
+
+
+def negatives_of(ref):
+    depth = PARTS + 1
+    total = ref.shape[0] // depth
+    return jnp.concatenate([ref[pl.ds(t, total, stride=depth), :] for t in range(depth)], 1)
+
+
+def shares_kernel(query_ref, negs_ref, out_ref):
+    negs = negatives_of(negs_ref)
+    total = negs.shape[0]
+    query = tuple(pieces(query_ref[...], 2))
+    logits = dot3(tuple(pieces(negs, 2)), query, 1, 1)
+    grad = dot3(jax.nn.sigmoid(logits) / total, query)
+    depth = PARTS + 1
+    for t in range(depth):
+        out_ref[pl.ds(t, total, stride=depth), :] = grad[:, t * LANES : (t + 1) * LANES]
+
+
+def grads_kernel(
+    query_ref, tail_ref, pos_ref, negs_ref, place_ref, rel_hi_ref, rel_lo_ref, out_ref, grad_hi, grad_lo
+):
+    edges = query_ref.shape[0]
+    kinds = rel_hi_ref.shape[0]
+    per_rel = edges // kinds
+    peers = out_ref.shape[0]
+    main = PARTS * LANES
+    negs = negatives_of(negs_ref)
+    total = negs.shape[0]
+    negs = tuple(pieces(negs, 2))
+
+    def keep(start, grad):
+        grad = jnp.concatenate([grad[:, :main], spread(grad[:, main:])], 1)
+        hi, lo = pieces(grad, 2)
+        grad_hi[start : start + per_rel, :] = hi
+        grad_lo[start : start + per_rel, :] = lo
+
+    for kind in range(kinds):
+        start = kind * per_rel
+        span = slice(start, start + per_rel)
+        query = query_ref[span, :]
+        pos = pos_ref[span, :]
+        logits = dot3(query, negs, 1, 1)
+        grad_neg = jax.nn.sigmoid(logits) / total
+        grad_query = pos * tail_ref[span, :] + dot3(grad_neg, negs)
+        keep(start, dot3(grad_query, (rel_hi_ref[kind], rel_lo_ref[kind]), 1, 1))
+        keep(edges + start, pos * query)
+    spot = place_ref[...]
+    half = peers // 2
+    count = half * REGION
+    for first in (0, half):
+        chosen = iota((count, 2 * edges), 0) + first * REGION == spot
+        chosen = chosen.astype(F32).astype(BF16)
+        got = dot(chosen, grad_lo[...]) + dot(chosen, grad_hi[...])
+        tails = got[:, main:].reshape(half * PARTS, PER_LINE, LANES)
+        own = iota(tails.shape, 2) // TAIL == iota(tails.shape, 1)
+        line = jnp.sum(jnp.where(own, tails, 0.0), 1, keepdims=True)
+        line = jnp.broadcast_to(line, tails.shape).reshape(half, REGION, LANES)
+        last = iota((half, REGION, LANES), 1) == CAP
+        for t in range(PARTS):
+            part = got[:, t * LANES : (t + 1) * LANES].reshape(half, REGION, LANES)
+            mine = line[:, t * PER_LINE : (t + 1) * PER_LINE, :]
+            mine = jnp.concatenate([mine] * PARTS, 1)
+            out_ref[first : first + half, t * REGION : (t + 1) * REGION, :] = jnp.where(
+                last, mine, part
+            )
+
+
+def add_kernel(place_ref, shares_ref, blocks_ref, out_ref, held, sems):
+    depth = PARTS + 1
+    mine = jnp.sum(shares_ref[...], 0)
+    number = held.shape[0]
+    owner = [lax.div(place_ref[n], REGION) for n in range(number)]
+    for n in range(number):
+        pltpu.make_async_copy(blocks_ref.at[owner[n]], held.at[n], sems.at[n]).start()
+    for n in range(number):
+        pltpu.make_async_copy(blocks_ref.at[owner[n]], held.at[n], sems.at[n]).wait()
+    for n in range(number):
+        k = lax.rem(place_ref[n], REGION)
+        part = lax.div(k, PER_LINE)
+        shift = TAIL * lax.rem(k, PER_LINE)
+        lines = [mine[n * depth + t : n * depth + t + 1] for t in range(PARTS)]
+        last = pltpu.roll(mine[n * depth + PARTS : (n + 1) * depth], shift, 1)
+        slot = jnp.int32(n)
+        for other in reversed(range(n)):
+            slot = jnp.where(owner[other] == owner[n], other, slot)
+        for t in range(PARTS):
+            held[slot, pl.ds(t * REGION + k, 1), :] += lines[t]
+        held[slot, pl.ds(part * REGION + CAP, 1), :] += last
+        for other in range(n):
+
+            @pl.when(owner[other] == owner[n])
+            def _():
+                held[n] = held[other]
+
+    for n in range(number):
+        copy = pltpu.make_async_copy(held.at[n], out_ref.at[owner[n]], sems.at[n])
+        copy.start()
+        copy.wait()
+
+
+def update_kernel(blocks_ref, rows_ref, table_ref, state_ref, new_table_ref, new_state_ref):
+    peers = blocks_ref.shape[0]
+    width, owned = table_ref.shape
+    count = peers * REGION
+    main = PARTS * LANES
+    parts = [pieces(part, 2) for part in unpack(blocks_ref, peers)]
+    hi = jnp.concatenate([p[0] for p in parts], 1)
+    lo = jnp.concatenate([p[1] for p in parts], 1)
+    chosen = (iota((owned, count), 0) == rows_ref[...]).astype(F32).astype(BF16)
+    got = dot(chosen, lo) + dot(chosen, hi)
+    tails = spread(got[:, main:])
+    tails = jnp.where(iota(tails.shape, 1) < TAIL, tails, 0.0)
+    grad = jnp.concatenate([got[:, :main], tails], 1).T
+    state = state_ref[...] + jnp.sum(grad * grad, 0, keepdims=True) / width
+    new_state_ref[...] = state
+    grad = grad[:width]
+    new_table_ref[...] = table_ref[...] - LEARN_RATE * grad / (jnp.sqrt(state) + EPSILON)
+
+
+def compact_path(marks, place, table, row_state, relations, touched, neg_slots):
+    owned, width = table.shape
+    peers, sent = touched.shape
+    own_count = neg_slots.shape[0]
+    edges = (place.shape[1] - LANES) // 2
+    count = peers * REGION
+    wide = jnp.pad(relations, ((0, 0), (0, WIDE - width), (0, WIDE - width)))
+    rel_hi = lax.reduce_precision(wide, 8, 7)
+    rel_lo = (wide - rel_hi).astype(BF16)
+    rel_hi = rel_hi.astype(BF16)
+    spot = place[:, : 2 * edges]
+    spot_column = spot.reshape(2 * edges, 1)
+    neg_place = place[0, 2 * edges : 2 * edges + own_count]
+
+    blocks, rows = call(
+        functools.partial(pack_kernel, sent),
+        (shaped(peers * BLOCK, LANES), shaped(peers, LANES, dtype=jnp.int32)),
+        scratch_shapes=[pltpu.VMEM((CAP * peers, owned), BF16)],
+    )(marks, jnp.pad(touched, ((0, 0), (0, LANES - sent))), table.T)
+    blocks = exchange(blocks.reshape(peers, BLOCK, LANES))
+    depth = own_count * (PARTS + 1)
+    own_negs = call(
+        negs_kernel,
+        shaped(peers, depth, LANES),
+        grid_spec=pltpu.PrefetchScalarGridSpec(
+            num_scalar_prefetch=1,
+            grid=(own_count,),
+            in_specs=[pl.BlockSpec((1, BLOCK, LANES), lambda n, at: (at[n] // REGION, 0, 0))],
+            out_specs=pl.BlockSpec((peers, depth, LANES), lambda n, at: (0, 0, 0)),
+        ),
+    )(neg_place, blocks)
+    negs = exchange(own_negs).reshape(peers * depth, LANES)
+    query, tail, pos = call(
+        query_kernel,
+        (shaped(edges, WIDE), shaped(edges, WIDE), shaped(edges, 1)),
+    )(blocks, spot_column, rel_hi, rel_lo)
+    shares = call(shares_kernel, shaped(peers * depth, LANES))(query, negs)
+    shares = exchange(shares.reshape(peers, depth, LANES))
+    grads = call(
+        grads_kernel,
+        shaped(peers, BLOCK, LANES),
+        scratch_shapes=[pltpu.VMEM((2 * edges, WIDE), BF16)] * 2,
+    )(query, tail, pos, negs, spot, rel_hi, rel_lo)
+    grads = call(
+        add_kernel,
+        shaped(peers, BLOCK, LANES),
+        in_specs=[
+            pl.BlockSpec(memory_space=pltpu.SMEM),
+            pl.BlockSpec(memory_space=pltpu.VMEM),
+            pl.BlockSpec(memory_space=pl.ANY),
+        ],
+        out_specs=pl.BlockSpec(memory_space=pl.ANY),
+        scratch_shapes=[
+            pltpu.VMEM((own_count, BLOCK, LANES), F32),
+            pltpu.SemaphoreType.DMA((own_count,)),
+        ],
+        input_output_aliases={2: 0},
+    )(neg_place, shares, grads)
+    returned = exchange(grads)
+    return call(
+        update_kernel,
+        (shaped(width, owned), shaped(1, owned)),
+    )(returned, rows[:, :REGION].reshape(1, count), table.T, row_state.reshape(1, owned))
+
+
+def per_device(table, row_state, relations, touched, source, target, neg_slots):
+    peers, sent = touched.shape
+    own_count = neg_slots.shape[0]
+    filler = jnp.full((LANES - own_count,), -1, jnp.int32)
+    ids = jnp.concatenate([source, target, neg_slots, filler]).reshape(1, -1)
+    marks, place = call(
+        functools.partial(mark_kernel, sent),
+        (shaped(peers, LANES), shaped(1, ids.shape[1], dtype=jnp.int32)),
+    )(ids)
+    marks = exchange(marks.reshape(peers, 1, LANES)).reshape(peers, LANES)
+    crowded = jnp.max(marks[:, sent]) > 0.0
+    new_table, new_state = lax.cond(
+        crowded,
+        lambda: full_path(table, row_state, relations, touched, source, target, neg_slots),
+        lambda: compact_path(marks, place, table, row_state, relations, touched, neg_slots),
+    )
+    return new_table.T, new_state.reshape(-1)
 
 
 def solution(mesh):

time: 475 us -> 345 us (0.73)
  waiting for transfers between devices: 310 us -> 246 us
  local copies, waits for them, and re-layouts: 59.1 us -> 10.7 us
  Pallas kernels: 0 us -> 36.3 us
  other arithmetic: 35.2 us -> 3.72 us
  matrix products: 14.4 us -> 0 us
  starting transfers between devices: 53.7 us -> 45.5 us
    all_to_all x4 -> x5, waiting for transfers between devices: 310 us -> 246 us  [exchange(): lax.all_to_all(blocks, 'grp', split_axis=0, concat_axis=0, tiled=True)]
    pallas_call x0 -> x8, Pallas kernels: none -> 36.3 us  [the longest x1 9.86 us: compact_path(): call(grads_kernel, shaped(peers, BLOCK, LANES), scratch_shapes=[pltpu.VME...]
    scatter-add x4 -> x0, other arithmetic: 32.2 us -> none  [the longest x1 13.4 us: per_device(): jnp.zeros(table.shape, jnp.float32).at[touched.reshape(-1)].add(returned)]
    reshape x10 -> x3, local copies, waits for them, and re-layouts: 29.2 us -> 2.31 us  [the longest x1 1.03 us: compact_path(): spot_column = spot.reshape(2 * edges, 1)]
    gather x6 -> x0, local copies, waits for them, and re-layouts: 23.2 us -> none  [take_rows(): return jnp.take(rows, ids, axis=0, mode='clip')]
    dot_general x3 -> x0, matrix products: 8.76 us -> none  [the longest x1 4.77 us: per_device(): jnp.einsum('ked,kdf->kef', head.reshape(kinds, per_rel, width), relations...]
    all_to_all x4 -> x5, starting transfers between devices: 53.7 us -> 45.5 us  [exchange(): lax.all_to_all(blocks, 'grp', split_axis=0, concat_axis=0, tiled=True)]
  transfers between devices with their start and end apart: 4 -> 5, of which waited for: 3 -> 5; matrix products, arithmetic and copies ran while one was open for 8% -> 2% of each run, Pallas kernels for 0% -> 5%
where the time goes in v2:
time: 345 us; the launch traced here: 344 us
  waiting for transfers between devices  246 us (71%)
  starting transfers between devices  45.5 us (13%)
  Pallas kernels  36.3 us (11%)
  local copies, waits for them, and re-layouts  10.7 us (3%)
  other arithmetic  3.72 us (1%)
    all_to_all x5, waiting for transfers between devices, exchange(): lax.all_to_all(blocks, 'grp', split_axis=0, concat_axis=0, tiled=True)  246 us
    all_to_all x5, starting transfers between devices, exchange(): lax.all_to_all(blocks, 'grp', split_axis=0, concat_axis=0, tiled=True)  45.5 us
    pallas_call x1, Pallas kernels, compact_path(): call(grads_kernel, shaped(peers, BLOCK, LANES), scratch_shapes=[pltpu.VME...  9.86 us
    pallas_call x1, Pallas kernels, compact_path(): call(query_kernel, (shaped(edges, WIDE), shaped(edges, WIDE), shaped(edge...  8.54 us
  transfers between devices with their start and end apart: 5, of which 5 were waited for; matrix products, arithmetic and copies ran while one was open for 2% of the time, Pallas kernels for 5%

profile of v2, /device:TPU:6, one launch (start us, length us, event | category | flops | bytes accessed | tf_op | source)
XLA Modules:
  0.0 344.3 jit_solution(14950462955696639238)
XLA Ops:
  0.6 0.8 concatenate.3
  1.4 0.6 reshape.126.ids_ref
  2.0 1.9 shard_map.86
  3.9 18.7 %all-to-all-start.8 = ((f32[64,1,128]{2,1,0:T(1,128)}), f32[64,1,128]{2,1,0:T(1,128)S(1)}, u32[]{:S(2)}, u32[]{:S(2)}) async-start(f32[64,1,128]{2,1,0:T(1,128)} %bitcast.55), calls=%async_computation.8 | async-start | bytes 65536 | tf_op jit(solution)/shard_map/all_to_all | solution.py:20
  22.6 14.3 %all-to-all-done.8 = f32[64,1,128]{2,1,0:T(1,128)S(1)} async-done(((f32[64,1,128]{2,1,0:T(1,128)}), f32[64,1,128]{2,1,0:T(1,128)S(1)}, u32[]{:S(2)}, u32[]{:S(2)}) %all-to-all-start.8) | async-done | bytes 32800 | tf_op jit(solution)/shard_map/all_to_all | solution.py:20
  37.0 0.7 slice_reduce_fusion
  38.3 305.2 %conditional.1 = (f32[256]{0:T(256)S(1)}, f32[400,256]{1,0:T(8,128)S(1)}) conditional(s32[]{:T(128)} %convert_element_type.15, (s32[1,1152]{1,0:T(1,128)S(1)}, s32[64,32]{0,1:T(8,128)}, f32[256,400]{0,1:T(8,128)}, f32[64,128]{1,0:T(8,128)S(1)}, f32[2,400,400]{2,1,0:T(8,128)}, /*index=5*/f32[256]{0:T(256)}) %tuple.39, (s32[64,32]{0,1:T(8,128)}, ...), branch_computations={%region_1.2_spmd, %region_2.10_spmd} | conditional | flops 2912907008 | bytes 98554624 | solution.py:449
  38.3 0.8 copy.50
  39.1 0.6 pad.12.touched_ref
  39.7 4.3 %branch_0_fun.7 = (f32[4608,128]{1,0:T(8,128)}, s32[64,128]{1,0:T(8,128)}) custom-call(f32[64,128]{1,0:T(8,128)S(1)} %get-tuple-element.30.marks_ref, s32[64,128]{1,0:T(8,128)} %pad.12.touched_ref, f32[400,256]{1,0:T(8,128)} %bitcast.43), custom_call_target="tpu_custom_call" | custom-call | tf_op jit(solution)/shard_map/cond/branch_0_fun/pallas_call | solution.py:387
  44.1 4.7 %all-to-all-start = ((f32[64,72,128]{2,1,0:T(8,128)}), f32[64,72,128]{2,1,0:T(8,128)S(1)}, u32[]{:S(2)}, u32[]{:S(2)}) async-start(f32[64,72,128]{2,1,0:T(8,128)} %bitcast.47), calls=%async_computation | async-start | bytes 4718592 | tf_op jit(solution)/shard_map/cond/branch_0_fun/all_to_all | solution.py:20
  48.8 0.6 slice_bitcast_fusion.place_ref
  49.4 107.4 %all-to-all-done.block_ref = f32[64,72,128]{2,1,0:T(8,128)S(1)} async-done(((f32[64,72,128]{2,1,0:T(8,128)}), f32[64,72,128]{2,1,0:T(8,128)S(1)}, u32[]{:S(2)}, u32[]{:S(2)}) %all-to-all-start) | async-done | bytes 2359328 | tf_op jit(solution)/shard_map/cond/branch_0_fun/all_to_all | solution.py:20
  156.8 0.0 copy-start
  156.8 1.4 copy-done
  158.2 2.5 branch_0_fun.9
  160.7 7.7 %all-to-all-start.1 = ((f32[64,8,128]{2,1,0:T(8,128)}), f32[64,8,128]{2,1,0:T(8,128)S(1)}, u32[]{:S(2)}, u32[]{:S(2)}) async-start(f32[64,8,128]{2,1,0:T(8,128)} %branch_0_fun.9), calls=%async_computation.1 | async-start | bytes 524288 | tf_op jit(solution)/shard_map/cond/branch_0_fun/all_to_all | solution.py:20
  168.4 0.6 fusion.16
  169.0 1.0 copy.36.place_ref
  170.0 3.0 fusion
  173.0 8.5 %branch_0_fun.8 = (f32[512,512]{1,0:T(8,128)}, f32[512,512]{1,0:T(8,128)}, f32[512,1]{1,0:T(8,128)}) custom-call(f32[64,72,128]{2,1,0:T(8,128)} %copy-done, s32[1024,1]{1,0:T(8,128)} %copy.36.place_ref, bf16[2,512,512]{2,1,0:T(8,128)(2,1)} %get-tuple-element.108.rel_hi_ref, bf16[2,512,512]{2,1,0:T(8,128)(2,1)} %get-tuple-element.107.rel_lo_ref), custom_call_target="tpu_custom_call" | custom-call | tf_op jit(solution)/shard_map/cond/branch_0_fun/pallas_call | solution.py:405
  181.6 7.4 %all-to-all-done.1 = f32[64,8,128]{2,1,0:T(8,128)S(1)} async-done(((f32[64,8,128]{2,1,0:T(8,128)}), f32[64,8,128]{2,1,0:T(8,128)S(1)}, u32[]{:S(2)}, u32[]{:S(2)}) %all-to-all-start.1) | async-done | bytes 262176 | tf_op jit(solution)/shard_map/cond/branch_0_fun/all_to_all | solution.py:20
  189.0 0.0 copy-start.4
  189.0 0.7 copy-done.4
  189.7 3.0 branch_0_fun.10
  192.7 7.9 %all-to-all-start.2 = ((f32[64,8,128]{2,1,0:T(8,128)}), f32[64,8,128]{2,1,0:T(8,128)S(1)}, u32[]{:S(2)}, u32[]{:S(2)}) async-start(f32[64,8,128]{2,1,0:T(8,128)} %bitcast.51), calls=%async_computation.2 | async-start | bytes 524288 | tf_op jit(solution)/shard_map/cond/branch_0_fun/all_to_all | solution.py:20
  200.6 9.9 %branch_0_fun.11.blocks_ref = f32[64,72,128]{2,1,0:T(8,128)} custom-call(f32[512,512]{1,0:T(8,128)} %get-tuple-element.35.query_ref, f32[512,512]{1,0:T(8,128)} %get-tuple-element.36.tail_ref, f32[512,1]{1,0:T(8,128)} %get-tuple-element.37.pos_ref, f32[512,128]{1,0:T(8,128)} %bitcast.49, s32[1,1024]{1,0:T(1,128)} %get-tuple-element.109.place_ref, ...), custom_call_target="tpu_custom_call" | custom-call | tf_op jit(solution)/shard_map/cond/branch_0_fun/pallas_call | solution.py:411
  210.5 0.0 copy-start.7
  210.5 0.0 copy-start.3
  210.5 0.0 copy-start.10
  210.5 10.0 %all-to-all-done.2.shares_ref = f32[64,8,128]{2,1,0:T(8,128)S(1)} async-done(((f32[64,8,128]{2,1,0:T(8,128)}), f32[64,8,128]{2,1,0:T(8,128)S(1)}, u32[]{:S(2)}, u32[]{:S(2)}) %all-to-all-start.2) | async-done | bytes 262176 | tf_op jit(solution)/shard_map/cond/branch_0_fun/all_to_all | solution.py:20
  220.5 0.0 copy-start.5
  220.5 0.7 copy-done.5
  221.2 3.1 branch_0_fun.12
  224.2 6.4 %all-to-all-start.3 = ((f32[64,72,128]{2,1,0:T(8,128)}), f32[64,72,128]{2,1,0:T(8,128)S(1)}, u32[]{:S(2)}, u32[]{:S(2)}) async-start(f32[64,72,128]{2,1,0:T(8,128)} %branch_0_fun.12), calls=%async_computation.3 | async-start | bytes 4718592 | tf_op jit(solution)/shard_map/cond/branch_0_fun/all_to_all | solution.py:20
  230.7 0.0 copy-done.7
  230.7 0.7 reshape.108.rows_ref
  231.4 107.0 %all-to-all-done.3.blocks_ref = f32[64,72,128]{2,1,0:T(8,128)S(1)} async-done(((f32[64,72,128]{2,1,0:T(8,128)}), f32[64,72,128]{2,1,0:T(8,128)S(1)}, u32[]{:S(2)}, u32[]{:S(2)}) %all-to-all-start.3) | async-done | bytes 2359328 | tf_op jit(solution)/shard_map/cond/branch_0_fun/all_to_all | solution.py:20
  338.4 0.0 copy-start.2
  338.4 1.4 copy-done.2
  339.9 0.0 copy-done.3
  339.9 0.0 copy-done.10
  339.9 3.2 branch_0_fun.13
  343.6 0.0 copy-start.13
  343.6 0.0 copy-start.14
  343.6 0.7 copy-done.13
  344.3 0.0 copy-done.14
  (1 shorter events, 0.0 us)
Async XLA Ops:
  3.9 33.1 %all-to-all-start.8 = ((f32[64,1,128]{2,1,0:T(1,128)}), f32[64,1,128]{2,1,0:T(1,128)S(1)}, u32[]{:S(2)}, u32[]{:S(2)}) async-start(f32[64,1,128]{2,1,0:T(1,128)} %bitcast.55), calls=%async_computation.8 | async-start | bytes 65536 | tf_op jit(solution)/shard_map/all_to_all | solution.py:20
  44.1 112.7 %all-to-all-start = ((f32[64,72,128]{2,1,0:T(8,128)}), f32[64,72,128]{2,1,0:T(8,128)S(1)}, u32[]{:S(2)}, u32[]{:S(2)}) async-start(f32[64,72,128]{2,1,0:T(8,128)} %bitcast.47), calls=%async_computation | async-start | bytes 4718592 | tf_op jit(solution)/shard_map/cond/branch_0_fun/all_to_all | solution.py:20
  156.8 1.5 copy-start
  160.7 28.3 %all-to-all-start.1 = ((f32[64,8,128]{2,1,0:T(8,128)}), f32[64,8,128]{2,1,0:T(8,128)S(1)}, u32[]{:S(2)}, u32[]{:S(2)}) async-start(f32[64,8,128]{2,1,0:T(8,128)} %branch_0_fun.9), calls=%async_computation.1 | async-start | bytes 524288 | tf_op jit(solution)/shard_map/cond/branch_0_fun/all_to_all | solution.py:20
  189.0 0.7 copy-start.4
  192.7 27.8 %all-to-all-start.2 = ((f32[64,8,128]{2,1,0:T(8,128)}), f32[64,8,128]{2,1,0:T(8,128)S(1)}, u32[]{:S(2)}, u32[]{:S(2)}) async-start(f32[64,8,128]{2,1,0:T(8,128)} %bitcast.51), calls=%async_computation.2 | async-start | bytes 524288 | tf_op jit(solution)/shard_map/cond/branch_0_fun/all_to_all | solution.py:20
  210.5 20.2 %copy-start.7 = (s32[64,128]{1,0:T(8,128)S(1)}, s32[64,128]{1,0:T(8,128)}, u32[]{:S(2)}) copy-start(s32[64,128]{1,0:T(8,128)} %get-tuple-element.38) | copy-start | bytes 98308 | tf_op jit(solution)/shard_map/cond
  210.5 129.4 %copy-start.3 = (f32[256,400]{0,1:T(8,128)S(1)}, f32[256,400]{0,1:T(8,128)}, u32[]{:S(2)}) copy-start(f32[256,400]{0,1:T(8,128)} %get-tuple-element.32) | copy-start | bytes 1228804 | tf_op jit(solution)/shard_map/cond
  210.5 129.4 %copy-start.10 = (f32[256]{0:T(256)S(1)}, f32[256]{0:T(256)}, u32[]{:S(2)}) copy-start(f32[256]{0:T(256)} %get-tuple-element.39) | copy-start | bytes 3076 | tf_op jit(solution)/shard_map/cond
  220.5 0.7 copy-start.5
  224.2 114.2 %all-to-all-start.3 = ((f32[64,72,128]{2,1,0:T(8,128)}), f32[64,72,128]{2,1,0:T(8,128)S(1)}, u32[]{:S(2)}, u32[]{:S(2)}) async-start(f32[64,72,128]{2,1,0:T(8,128)} %branch_0_fun.12), calls=%async_computation.3 | async-start | bytes 4718592 | tf_op jit(solution)/shard_map/cond/branch_0_fun/all_to_all | solution.py:20
  338.4 1.4 copy-start.2
  343.6 0.8 copy-start.13
  343.6 0.7 copy-start.14

commit v3 on v1

--- a/solution.py
+++ b/solution.py
@@ -1,12 +1,19 @@
+import functools
+
 import jax
 import jax.numpy as jnp
 from jax import lax
+from jax.experimental import pallas as pl
+from jax.experimental.pallas import tpu as pltpu
 from jax.sharding import PartitionSpec as P
 
 PRECISE = lax.Precision.HIGHEST
 LEARN_RATE = 0.1
 EPSILON = 1e-06
 LANES = 128
+VMEM = 56 * 1024 * 1024
+F32 = jnp.float32
+BF16 = jnp.bfloat16
 
 
 def exchange(blocks):
@@ -23,7 +30,7 @@
     return jnp.pad(rows, ((0, 0), (0, wide - width))).reshape(peers, -1, LANES)
 
 
-def per_device(table, row_state, relations, touched, source, target, neg_slots):
+def full_path(table, row_state, relations, touched, source, target, neg_slots):
     width = table.shape[1]
     peers, sent = touched.shape
     kinds = relations.shape[0]
@@ -53,14 +60,465 @@
     grad_head = jnp.einsum(
         "kef,kdf->ked", grad_query.reshape(kinds, per_rel, width), relations, precision=PRECISE
     ).reshape(kinds * per_rel, width)
-    slot_grad = jnp.zeros((slot_count, width), jnp.float32).at[source].add(grad_head)
+    slot_grad = jnp.zeros((slot_count, width), F32).at[source].add(grad_head)
     slot_grad = slot_grad.at[target].add(grad_tail)
     slot_grad = slot_grad.at[neg_slots].add(mine)
     returned = exchange(slot_grad.reshape(peers, -1, LANES)).reshape(slot_count, width)
-    row_grad = jnp.zeros(table.shape, jnp.float32).at[touched.reshape(-1)].add(returned)
+    row_grad = jnp.zeros(table.shape, F32).at[touched.reshape(-1)].add(returned)
     new_state = row_state + jnp.mean(row_grad * row_grad, -1)
     new_table = table - LEARN_RATE * row_grad / (jnp.sqrt(new_state)[:, None] + EPSILON)
-    return (new_table, new_state)
+    return new_table.T, new_state.reshape(1, -1)
+
+
+HEAD = 16
+CAP = 20
+REGION = 24
+PARTS = 3
+BLOCK = 64
+EXTRA = PARTS * HEAD
+TAIL = 16
+PER_LINE = LANES // TAIL
+LINES = EXTRA + PARTS * (CAP - HEAD)
+WIDE = (PARTS + 1) * LANES
+MATE = 16
+SENT = 32
+AT_COUNTS = 2 * SENT
+AT_NEGS = 3 * SENT
+
+
+def line_of(part, k):
+    if k < HEAD:
+        return part * HEAD + k
+    return EXTRA + part * (CAP - HEAD) + k - HEAD
+
+
+def iota(shape, dim):
+    return lax.broadcasted_iota(jnp.int32, shape, dim)
+
+
+def bits(mask):
+    return jnp.where(mask, 1.0, 0.0).astype(BF16)
+
+
+def shift_down(x, by):
+    return lax.shift_right_logical(x, jnp.full(x.shape, by, x.dtype))
+
+
+def pair_of(owner):
+    return shift_down(owner, 5) * MATE + lax.bitwise_and(owner, MATE - 1)
+
+
+def mate_of(owner):
+    return lax.bitwise_xor(owner, MATE)
+
+
+def pieces(x, count):
+    out = []
+    for _ in range(count):
+        piece = x.astype(BF16)
+        out.append(piece)
+        x = x - piece.astype(F32)
+    return out
+
+
+def dot(a, b, a_dim=1, b_dim=0):
+    return lax.dot_general(a, b, (((a_dim,), (b_dim,)), ((), ())), preferred_element_type=F32)
+
+
+def dot3(a, b, a_dim=1, b_dim=0):
+    a_hi, a_lo = a if isinstance(a, tuple) else pieces(a, 2)
+    b_hi, b_lo = b if isinstance(b, tuple) else pieces(b, 2)
+    small = dot(a_lo, b_hi, a_dim, b_dim) + dot(a_hi, b_lo, a_dim, b_dim)
+    return small + dot(a_hi, b_hi, a_dim, b_dim)
+
+
+def spread(x):
+    step = TAIL
+    while step < LANES:
+        x = x + pltpu.roll(x, step, 1)
+        step *= 2
+    return x
+
+
+def call(kernel, outs, **kw):
+    return pl.pallas_call(
+        kernel,
+        out_shape=outs,
+        compiler_params=pltpu.CompilerParams(vmem_limit_bytes=VMEM),
+        **kw,
+    )
+
+
+def shaped(*shape, dtype=F32):
+    return jax.ShapeDtypeStruct(shape, dtype)
+
+
+VECTOR = pl.BlockSpec(memory_space=pltpu.VMEM)
+SCALAR = pl.BlockSpec(memory_space=pltpu.SMEM)
+
+
+def mark_kernel(negs_ref, source_ref, target_ref, out_ref):
+    peers = out_ref.shape[0]
+    ids = jnp.concatenate([source_ref[...], target_ref[...]], 1)
+    count = ids.shape[1]
+    owner = shift_down(ids, 5)
+    within = lax.bitwise_and(ids, SENT - 1)
+    row = iota((peers, count), 0)
+    spot = iota((LANES, count), 0)
+    marks = dot(bits(row == owner), bits(spot == within), 1, 1)
+    marks = marks + dot(bits(row == mate_of(owner)), bits(spot == within + SENT), 1, 1)
+    marks = jnp.where(marks > 0.0, 1.0, 0.0)
+    lane = iota(marks.shape, 1)
+    used = jnp.sum(jnp.where(lane < SENT, marks, 0.0), 1, keepdims=True)
+    at_pair = lane == AT_COUNTS + pair_of(iota(marks.shape, 0))
+    marks = marks + jnp.sum(jnp.where(at_pair, used, 0.0), 0, keepdims=True)
+    for n in range(negs_ref.shape[0]):
+        marks = jnp.where(lane == AT_NEGS + n, negs_ref[n].astype(F32), marks)
+    out_ref[...] = marks
+
+
+def neg_columns(marks, number):
+    lane = iota(marks.shape, 1)
+    columns = []
+    for n in range(number):
+        column = jnp.sum(jnp.where(lane == AT_NEGS + n, marks, 0.0), 1, keepdims=True)
+        columns.append(jnp.broadcast_to(column.astype(jnp.int32), marks.shape))
+    return columns
+
+
+def before(count):
+    return bits(iota((count, count), 1) < iota((count, count), 0))
+
+
+def pack_kernel(
+    number, me_ref, marks_ref, touched_ref, mate_touched_ref, table_ref, mate_table_ref,
+    out_ref, rows_ref, flag_ref, onehot,
+):
+    marks = marks_ref[...]
+    peers = marks.shape[0]
+    lane = iota(marks.shape, 1)
+    negs = neg_columns(marks, number)
+    me = me_ref[0]
+
+    at_pair = jnp.zeros(marks.shape, F32)
+    at_owner = jnp.zeros(marks.shape, F32)
+    for slot in negs:
+        owner = shift_down(slot, 5)
+        at_pair = at_pair + jnp.where(lane == AT_COUNTS + pair_of(owner), 1.0, 0.0)
+        at_owner = at_owner + jnp.where(lane == owner, 1.0, 0.0)
+    counts = marks + jnp.sum(at_pair, 0, keepdims=True)
+    counts = jnp.where((lane >= AT_COUNTS) & (lane < AT_NEGS), counts, 0.0)
+    over = (jnp.max(counts) > 2 * CAP) | (jnp.max(jnp.sum(at_owner, 0, keepdims=True)) > SENT)
+    flag_ref[0] = over.astype(jnp.int32)
+
+    def neg_rows(owner, touched):
+        total = jnp.zeros((1, LANES), F32)
+        rows = jnp.zeros((1, LANES), F32)
+        for slot in negs:
+            mine = shift_down(slot, 5) == owner
+            row = jnp.sum(
+                jnp.where(lane == lax.bitwise_and(slot, SENT - 1), touched, 0.0), 1, keepdims=True
+            )
+            rank = dot(before(peers), bits(mine)) + total
+            total = total + jnp.sum(jnp.where(mine, 1.0, 0.0), 0, keepdims=True)
+            here = mine & (lane == SENT + rank.astype(jnp.int32))
+            rows = rows + jnp.sum(jnp.where(here, row + 1.0, 0.0), 0, keepdims=True)
+        return rows
+
+    owned = table_ref.shape[1]
+    touched = touched_ref[...].astype(F32)
+    mate_touched = mate_touched_ref[...].astype(F32)
+    own_negs = jnp.broadcast_to(neg_rows(me, touched), marks.shape)
+    mate_negs = jnp.broadcast_to(neg_rows(mate_of(me), mate_touched), marks.shape)
+    mate_negs = pltpu.roll(mate_negs, 2 * SENT, 1)
+    own = lane < 2 * SENT
+    mask = jnp.where(
+        lane < SENT,
+        marks,
+        jnp.where(
+            own,
+            jnp.where(own_negs > 0.0, 1.0, 0.0),
+            jnp.where(
+                lane < 3 * SENT,
+                pltpu.roll(marks, SENT, 1),
+                jnp.where(mate_negs > 0.0, 1.0, 0.0),
+            ),
+        ),
+    )
+    local = jnp.where(
+        lane < SENT,
+        touched + 1.0,
+        jnp.where(
+            own,
+            own_negs,
+            jnp.where(
+                lane < 3 * SENT, pltpu.roll(mate_touched, 2 * SENT, 1) + 1.0, mate_negs
+            )
+            + owned,
+        ),
+    )
+    first, second = iota((LANES, LANES), 0), iota((LANES, LANES), 1)
+    same = (first < 2 * SENT) == (second < 2 * SENT)
+    rank = dot(mask.astype(BF16), bits(same & (first <= second)))
+    number_own = jnp.sum(jnp.where(own, mask, 0.0), 1, keepdims=True)
+    place = jnp.where(
+        own,
+        jnp.where(rank <= CAP, rank - 1.0, -1.0),
+        jnp.where(rank > CAP, number_own + rank - (CAP + 1.0), -1.0),
+    )
+    place = jnp.where(mask > 0.0, place, -1.0)
+    spot = iota((peers, 2 * owned), 1)
+    rows = jnp.full(marks.shape, -1, jnp.int32)
+    for k in range(CAP):
+        row = jnp.sum(jnp.where(place == k, local, 0.0), 1, keepdims=True).astype(jnp.int32) - 1
+        rows = jnp.where(lane == k, row, rows)
+        onehot[k * peers : (k + 1) * peers, :] = bits(spot == row)
+    rows_ref[...] = rows
+
+    main = PARTS * LANES
+    table = jnp.concatenate([table_ref[...], mate_table_ref[...]], 1)
+    wide = jnp.concatenate([table[:main]] + [table[main:]] * PER_LINE, 0)
+    wide = pieces(wide, 3)
+    group = lane // TAIL
+    for part in range(PARTS):
+        first = part * PER_LINE
+        last = min(first + PER_LINE, CAP)
+        chosen = onehot[first * peers : last * peers, :]
+        got = dot(chosen, wide[2], 1, 1) + dot(chosen, wide[1], 1, 1)
+        got = got + dot(chosen, wide[0], 1, 1)
+        line = jnp.zeros(marks.shape, F32)
+        for k in range(first, last):
+            mine = got[(k - first) * peers : (k - first + 1) * peers]
+            for t in range(PARTS):
+                out_ref[pl.ds(line_of(t, k), peers, stride=BLOCK), :] = mine[
+                    :, t * LANES : (t + 1) * LANES
+                ]
+            line = line + jnp.where(group == k - first, mine[:, main:], 0.0)
+        out_ref[pl.ds(LINES + part, peers, stride=BLOCK), :] = line
+    for spare in range(LINES + PARTS, BLOCK):
+        out_ref[pl.ds(spare, peers, stride=BLOCK), :] = jnp.zeros(marks.shape, F32)
+
+
+def place_kernel(number, marks_ref, source_ref, target_ref, edge_ref, neg_ref):
+    marks = marks_ref[...]
+    peers = marks.shape[0]
+    ids = jnp.concatenate([source_ref[...], target_ref[...]], 1)
+    count = ids.shape[1]
+    owner = shift_down(ids, 5)
+    at_owner = bits(iota((LANES, count), 0) == owner)
+    at_within = bits(iota((SENT, count), 0) == lax.bitwise_and(ids, SENT - 1))
+    used = bits(dot(at_within, at_owner, 1, 1) > 0.0)
+    upto = bits(iota((SENT, SENT), 1) <= iota((SENT, SENT), 0))
+    rank = dot(upto, used)
+    from_edges = rank[SENT - 1 :]
+    lane = iota(marks.shape, 1)
+    negs = [shift_down(slot, 5) for slot in neg_columns(marks, number)]
+    at_neg = [jnp.where(lane == slot, 1.0, 0.0) for slot in negs]
+    total = from_edges
+    for at in at_neg:
+        total = total + jnp.sum(at, 0, keepdims=True)
+    first, second = iota((LANES, LANES), 0), iota((LANES, LANES), 1)
+    swap = bits(first == mate_of(second))
+    total = jnp.broadcast_to(total, (PER_LINE, LANES)).astype(BF16)
+    mates = dot(total, swap)
+
+    def placed(owner, order, mate):
+        own = owner * REGION + order
+        return jnp.where(order < CAP, own, mate_of(owner) * REGION + mate + order - CAP)
+
+    order = jnp.sum(dot(rank.astype(BF16), at_owner) * at_within.astype(F32), 0, keepdims=True)
+    mate = dot(mates.astype(BF16), at_owner)[:1]
+    edge_ref[...] = placed(owner, order.astype(jnp.int32) - 1, mate.astype(jnp.int32))
+    earlier = from_edges
+    for n, at in enumerate(at_neg):
+        order = dot(before(peers), at.astype(BF16)) + earlier
+        order = jnp.sum(order * at, 1, keepdims=True)
+        mate = jnp.sum(mates[:1] * at, 1, keepdims=True)
+        at_place = placed(negs[n][:, :1], order.astype(jnp.int32), mate.astype(jnp.int32))
+        neg_ref[n * peers : (n + 1) * peers, :] = at_place
+        earlier = earlier + jnp.sum(at, 0, keepdims=True)
+
+
+def unpack(ref):
+    peers = ref.shape[0]
+    count = peers * REGION
+    ends = ref[:, EXTRA : EXTRA + PER_LINE, :], ref[:, EXTRA + PER_LINE :, :]
+    rest = ends[0], pltpu.roll(ends[0], PER_LINE // 2, 1), ends[1]
+    parts = []
+    for t in range(PARTS):
+        part = jnp.concatenate([ref[:, t * HEAD : (t + 1) * HEAD, :], rest[t]], 1)
+        parts.append(part.reshape(count, LANES))
+    at = LINES - EXTRA - PER_LINE
+    tails = [
+        jnp.broadcast_to(ends[1][:, at + t : at + t + 1, :], (peers, PER_LINE, LANES))
+        for t in range(PARTS)
+    ]
+    tails = jnp.concatenate(tails, 1)
+    own = iota(tails.shape, 2) // TAIL == iota(tails.shape, 1) % PER_LINE
+    parts.append(jnp.where(own, tails, 0.0).reshape(count, LANES))
+    both = [pieces(part, 2) for part in parts]
+    return jnp.concatenate([p[0] for p in both], 1), jnp.concatenate([p[1] for p in both], 1)
+
+
+def edges_kernel(
+    block_ref, place_ref, neg_place_ref, row_place_ref, rel_hi_ref, rel_lo_ref,
+    out_ref, slots_hi, slots_lo, grad_hi, grad_lo,
+):
+    peers = block_ref.shape[0]
+    edges = place_ref.shape[0] // 2
+    total = neg_place_ref.shape[0]
+    kinds = rel_hi_ref.shape[0]
+    per_rel = edges // kinds
+    count = peers * REGION
+    main = PARTS * LANES
+    slots_hi[...], slots_lo[...] = unpack(block_ref)
+
+    def rows_at(spot):
+        chosen = bits(iota((spot.shape[0], count), 1) == spot)
+        got = dot(chosen, slots_lo[...]) + dot(chosen, slots_hi[...])
+        return jnp.concatenate([got[:, :main], spread(got[:, main:])], 1)
+
+    def keep(start, grad):
+        grad = jnp.concatenate([grad[:, :main], spread(grad[:, main:])], 1)
+        hi, lo = pieces(grad, 2)
+        grad_hi[start : start + grad.shape[0], :] = hi
+        grad_lo[start : start + grad.shape[0], :] = lo
+
+    negs = tuple(pieces(rows_at(neg_place_ref[...]), 2))
+    shares = jnp.zeros((total, WIDE), F32)
+    for kind in range(kinds):
+        start = kind * per_rel
+        relation = rel_hi_ref[kind], rel_lo_ref[kind]
+        query = dot3(rows_at(place_ref[start : start + per_rel, :]), relation)
+        tail = rows_at(place_ref[edges + start : edges + start + per_rel, :])
+        positive = jnp.sum(query * tail, 1, keepdims=True)
+        grad_pos = jax.nn.sigmoid(positive) - 1.0
+        keep(edges + start, grad_pos * query)
+        query = tuple(pieces(query, 2))
+        grad_neg = jax.nn.sigmoid(dot3(query, negs, 1, 1)) / total
+        grad_query = grad_pos * tail + dot3(grad_neg, negs)
+        keep(start, dot3(grad_query, relation, 1, 1))
+        grad_neg = jax.nn.sigmoid(dot3(negs, query, 1, 1)) / total
+        shares = shares + dot3(grad_neg, query)
+    keep(2 * edges, shares)
+
+    spot = row_place_ref[...]
+    half = peers // 2
+    count = half * REGION
+    for first in (0, half):
+        chosen = bits(iota((count, spot.shape[1]), 0) + first * REGION == spot)
+        got = dot(chosen, grad_lo[...]) + dot(chosen, grad_hi[...])
+        span = slice(first, first + half)
+        rest = []
+        for t in range(PARTS):
+            part = got[:, t * LANES : (t + 1) * LANES].reshape(half, REGION, LANES)
+            out_ref[span, t * HEAD : (t + 1) * HEAD, :] = part[:, :HEAD]
+            rest.append(part[:, HEAD:])
+        out_ref[span, EXTRA : EXTRA + PER_LINE, :] = rest[0] + pltpu.roll(rest[1], PER_LINE // 2, 1)
+        last = rest[2]
+        line = got[:, main:].reshape(half, REGION, LANES)
+        own = iota(line.shape, 2) // TAIL == iota(line.shape, 1) % PER_LINE
+        line = jnp.where(own, line, 0.0)
+        at = LINES - EXTRA - PER_LINE
+        for t in range(PARTS):
+            mine = jnp.sum(line[:, t * PER_LINE : (t + 1) * PER_LINE], 1, keepdims=True)
+            here = iota(last.shape, 1) == at + t
+            last = jnp.where(here, jnp.broadcast_to(mine, last.shape), last)
+        out_ref[span, EXTRA + PER_LINE :, :] = last
+
+
+def sum_kernel(first, block_ref, rows_ref, out_ref):
+    width, owned = out_ref.shape
+    main = PARTS * LANES
+    hi, lo = unpack(block_ref)
+    count = hi.shape[0]
+    chosen = bits(iota((owned, count), 0) + first == rows_ref[...])
+    got = dot(chosen, lo) + dot(chosen, hi)
+    grad = jnp.concatenate([got[:, :main], spread(got[:, main:])], 1)
+    out_ref[...] = grad.T[:width]
+
+
+def update_kernel(own_ref, mate_ref, table_ref, state_ref, new_table_ref, new_state_ref):
+    width = table_ref.shape[0]
+    grad = own_ref[...] + mate_ref[...]
+    state = state_ref[...] + jnp.sum(grad * grad, 0, keepdims=True) / width
+    new_state_ref[...] = state
+    new_table_ref[...] = table_ref[...] - LEARN_RATE * grad / (jnp.sqrt(state) + EPSILON)
+
+
+def swap_mates(x):
+    peers = lax.axis_size("grp")
+    return lax.ppermute(x, "grp", [(p, p ^ MATE) for p in range(peers)])
+
+
+def compact_path(marks, blocks, rows, source, target, number, rel_hi, rel_lo, table, state):
+    peers = marks.shape[0]
+    edges = source.shape[1]
+    width, owned = table.shape
+    blocks = exchange(blocks.reshape(peers, BLOCK, LANES))
+    edge_place, neg_place = call(
+        functools.partial(place_kernel, number),
+        (shaped(1, 2 * edges, dtype=jnp.int32), shaped(peers * number, 1, dtype=jnp.int32)),
+    )(marks, source, target)
+    row_place = jnp.concatenate([edge_place, neg_place.reshape(1, -1)], 1)
+    grads = call(
+        edges_kernel,
+        shaped(peers, BLOCK, LANES),
+        scratch_shapes=[
+            pltpu.VMEM((peers * REGION, WIDE), BF16),
+            pltpu.VMEM((peers * REGION, WIDE), BF16),
+            pltpu.VMEM((row_place.shape[1], WIDE), BF16),
+            pltpu.VMEM((row_place.shape[1], WIDE), BF16),
+        ],
+    )(blocks, edge_place.reshape(-1, 1), neg_place, row_place, rel_hi, rel_lo)
+    returned = exchange(grads)
+    rows = rows[:, :REGION].reshape(1, -1)
+    for_mate = call(functools.partial(sum_kernel, owned), shaped(width, owned))(returned, rows)
+    from_mate = swap_mates(for_mate)
+    own = call(functools.partial(sum_kernel, 0), shaped(width, owned))(returned, rows)
+    return call(
+        update_kernel,
+        (shaped(width, owned), shaped(1, owned)),
+    )(own, from_mate, table, state)
+
+
+def per_device(table, row_state, relations, touched, source, target, neg_slots):
+    peers, sent = touched.shape
+    owned, width = table.shape
+    number = neg_slots.shape[0]
+    across = table.T
+    mate_table = swap_mates(across)
+    wide_touched = jnp.pad(touched, ((0, 0), (0, LANES - sent)))
+    mate_touched = swap_mates(wide_touched)
+    source_row, target_row = source.reshape(1, -1), target.reshape(1, -1)
+    marks = call(
+        mark_kernel, shaped(peers, LANES), in_specs=[SCALAR, VECTOR, VECTOR], out_specs=VECTOR
+    )(neg_slots, source_row, target_row)
+    marks = exchange(marks.reshape(peers, 1, LANES)).reshape(peers, LANES)
+    wide = jnp.pad(relations, ((0, 0), (0, WIDE - width), (0, WIDE - width)))
+    rel_hi = lax.reduce_precision(wide, 8, 7)
+    rel_lo = (wide - rel_hi).astype(BF16)
+    rel_hi = rel_hi.astype(BF16)
+    blocks, rows, crowded = call(
+        functools.partial(pack_kernel, number),
+        (
+            shaped(peers * BLOCK, LANES),
+            shaped(peers, LANES, dtype=jnp.int32),
+            shaped(1, dtype=jnp.int32),
+        ),
+        in_specs=[SCALAR] + [VECTOR] * 5,
+        out_specs=(VECTOR, VECTOR, SCALAR),
+        scratch_shapes=[pltpu.VMEM((CAP * peers, 2 * owned), BF16)],
+    )(lax.axis_index("grp").reshape(1), marks, wide_touched, mate_touched, across, mate_table)
+    new_table, new_state = lax.cond(
+        crowded[0] > 0,
+        lambda: full_path(table, row_state, relations, touched, source, target, neg_slots),
+        lambda: compact_path(
+            marks, blocks, rows, source_row, target_row, number, rel_hi, rel_lo, across,
+            row_state.reshape(1, -1),
+        ),
+    )
+    return new_table.T, new_state.reshape(-1)
 
 
 def solution(mesh):

time: 475 us -> 405 us (0.85)
  the two profiles are of different devices: /device:TPU:6 before, /device:TPU:3 now
where the time goes in v3:
time: 405 us; the launch traced here: 399 us
  waiting for transfers between devices  206 us (51%)
  starting transfers between devices  70.5 us (17%)
  local copies, waits for them, and re-layouts  60.1 us (15%)
  other arithmetic  37.6 us (9%)
  matrix products  14.4 us (4%)
  Pallas kernels  8.26 us (2%)
    all_to_all x5, waiting for transfers between devices, exchange(): lax.all_to_all(blocks, 'grp', split_axis=0, concat_axis=0, tiled=True)  206 us
    all_to_all x5, starting transfers between devices, exchange(): lax.all_to_all(blocks, 'grp', split_axis=0, concat_axis=0, tiled=True)  64.2 us
    gather x6, local copies, waits for them, and re-layouts, take_rows(): return jnp.take(rows, ids, axis=0, mode='clip')  23.2 us
    scatter-add x1, other arithmetic, full_path(): row_grad = jnp.zeros(table.shape, F32).at[touched.reshape(-1)].add(returned)  13.4 us
  transfers between devices with their start and end apart: 7, of which 4 were waited for; matrix products, arithmetic and copies ran while one was open for 11% of the time, Pallas kernels for 0%

profile of v3, /device:TPU:3, one launch (start us, length us, event | category | flops | bytes accessed | tf_op | source)
XLA Modules:
  0.0 399.3 jit_solution(231513196068923677)
XLA Ops:
  0.6 3.3 collective-permute-start.2
  4.0 1.7 shard_map.86
  5.7 18.2 %all-to-all-start.6 = ((f32[64,1,128]{2,1,0:T(1,128)}), f32[64,1,128]{2,1,0:T(1,128)S(1)}, u32[]{:S(2)}, u32[]{:S(2)}) async-start(f32[64,1,128]{2,1,0:T(1,128)} %bitcast.52), calls=%async_computation.6 | async-start | bytes 65536 | tf_op jit(solution)/shard_map/all_to_all | solution.py:20
  23.9 0.8 copy.49
  24.7 2.9 collective-permute-start.1
  27.6 2.7 fusion.15
  30.3 6.7 %all-to-all-done.6 = f32[64,1,128]{2,1,0:T(1,128)S(1)} async-done(((f32[64,1,128]{2,1,0:T(1,128)}), f32[64,1,128]{2,1,0:T(1,128)S(1)}, u32[]{:S(2)}, u32[]{:S(2)}) %all-to-all-start.6) | async-done | bytes 32800 | tf_op jit(solution)/shard_map/all_to_all | solution.py:20
  37.1 0.7 copy-done.5
  37.8 6.5 %shard_map.87 = (f32[4096,128]{1,0:T(8,128)}, s32[64,128]{1,0:T(8,128)}, s32[1]{0:T(128)}) custom-call(s32[1]{0:T(128)} %bitcast.9.me_ref, f32[64,128]{1,0:T(8,128)S(1)} %bitcast.50, s32[64,128]{1,0:T(8,128)} %copy-done.10, s32[64,128]{1,0:T(8,128)} %copy-done.11, f32[400,256]{1,0:T(8,128)S(1)} %bitcast.44, f32[400,256]{1,0:T(8,128)} %copy-done.5), custom_call_target="tpu_custom_call" | custom-call | tf_op jit(solution)/shard_map/pallas_call | solution.py:502
  45.0 353.2 %conditional.1 = (f32[256]{0:T(256)S(1)}, f32[400,256]{1,0:T(8,128)S(1)}) conditional(s32[]{:T(128)} %bitcast.16, (f32[4096,128]{1,0:T(8,128)}, f32[64,128]{1,0:T(8,128)S(1)}, s32[1,512]{1,0:T(1,128)}, s32[1,512]{1,0:T(1,128)}, bf16[2,512,512]{2,1,0:T(8,128)(2,1)}, /*index=5*/bf16[2,512,512]{2,1,0:T(8,128)(2,1)S(1)}, s32[64,128]{1,0:T(8,128)}, ...), branch_computations={%region_0.1_spmd, %region_1.9_spmd} | conditional | flops 2912907008 | bytes 98620208 | solution.py:513
  45.2 0.8 copy.50
  46.1 0.5 copy-done.8
  46.6 0.2 copy.51
  46.8 8.9 %gather_fusion = f32[2048,400]{1,0:T(8,128)} fusion(f32[256,400]{1,0:T(8,128)S(1)} %copy.51, s32[2048]{0:T(1024)S(1)} %broadcast_clamp_fusion), kind=kCustom, calls=%fused_computation | custom fusion | bytes 6561792 | tf_op jit(solution)/shard_map/cond/branch_1_fun/jit(_take)/gather | solution.py:24
  55.8 6.5 %reshape.117 = f32[64,100,128]{2,1,0:T(8,128)} reshape(f32[2048,400]{1,0:T(8,128)} %gather_fusion) | data formatting | bytes 6553600 | tf_op jit(solution)/shard_map/cond/branch_1_fun/reshape | solution.py:42
  62.2 8.2 %all-to-all-start.2 = ((f32[64,100,128]{2,1,0:T(8,128)}), f32[64,100,128]{2,1,0:T(8,128)}, u32[]{:S(2)}, u32[]{:S(2)}) async-start(f32[64,100,128]{2,1,0:T(8,128)} %reshape.117), calls=%async_computation.2 | async-start | bytes 6815744 | tf_op jit(solution)/shard_map/cond/branch_1_fun/all_to_all | solution.py:20
  70.5 112.7 %all-to-all-done.2 = f32[64,100,128]{2,1,0:T(8,128)} async-done(((f32[64,100,128]{2,1,0:T(8,128)}), f32[64,100,128]{2,1,0:T(8,128)}, u32[]{:S(2)}, u32[]{:S(2)}) %all-to-all-start.2) | async-done | bytes 3276832 | tf_op jit(solution)/shard_map/cond/branch_1_fun/all_to_all | solution.py:20
  183.2 6.7 %reshape.118 = f32[2048,400]{1,0:T(8,128)} reshape(f32[64,100,128]{2,1,0:T(8,128)} %all-to-all-done.2) | data formatting | bytes 6553600 | tf_op jit(solution)/shard_map/cond/branch_1_fun/reshape | solution.py:42
  189.9 2.7 gather_fusion.3
  192.7 0.7 broadcast_in_dim.30
  193.4 14.0 %all-to-all-start.3 = ((f32[64,8,128]{2,1,0:T(8,128)}), f32[64,8,128]{2,1,0:T(8,128)}, u32[]{:S(2)}, u32[]{:S(2)}) async-start(f32[64,8,128]{2,1,0:T(8,128)} %broadcast_in_dim.30), calls=%async_computation.3 | async-start | bytes 524288 | tf_op jit(solution)/shard_map/cond/branch_1_fun/all_to_all | solution.py:20
  207.5 4.2 %gather_fusion.2 = f32[512,400]{1,0:T(8,128)S(1)} fusion(f32[2048,400]{1,0:T(8,128)} %reshape.118, s32[1024]{0:T(1024)S(1)} %get-tuple-element.100), kind=kCustom, calls=%fused_computation.2 | custom fusion | bytes 1640448 | tf_op jit(solution)/shard_map/cond/branch_1_fun/jit(_take)/gather | solution.py:24
  211.7 4.9 %gather_fusion.1 = f32[512,400]{1,0:T(8,128)} fusion(f32[2048,400]{1,0:T(8,128)} %reshape.118, s32[1024]{0:T(1024)S(1)} %pad_clamp_fusion.2), kind=kCustom, calls=%fused_computation.1 | custom fusion | bytes 1640448 | tf_op jit(solution)/shard_map/cond/branch_1_fun/jit(_take)/gather | solution.py:24
  216.6 1.2 copy.41
  217.8 1.2 copy.40
  219.0 4.8 %multiply_reduce_fusion = (f32[2,256]{1,0:T(2,128)S(1)}, f32[2,256,400]{1,2,0:T(8,128)S(1)}) fusion(f32[2,256,400]{1,2,0:T(8,128)} %copy.40, f32[2,256,400]{2,1,0:T(8,128)} %bitcast.42, f32[2,400,400]{2,1,0:T(8,128)S(1)} %copy-done.1), kind=kOutput, calls=%fused_computation.19 | convolution fusion | flops 983449088 | bytes 3739648 | tf_op jit(solution)/shard_map/cond/branch_1_fun/ked,kdf->kef/dot_general | solution.py:48
  223.9 5.6 %all-to-all-done.3 = f32[64,8,128]{2,1,0:T(8,128)} async-done(((f32[64,8,128]{2,1,0:T(8,128)}), f32[64,8,128]{2,1,0:T(8,128)}, u32[]{:S(2)}, u32[]{:S(2)}) %all-to-all-start.3) | async-done | bytes 262176 | tf_op jit(solution)/shard_map/cond/branch_1_fun/all_to_all | solution.py:20
  229.4 1.0 reshape.121
  230.4 1.9 fusion.5
  232.3 0.7 copy-done.4
  233.0 1.1 fusion.16
  234.1 0.7 pad.13.clone
  234.8 1.7 reshape.124
  236.5 8.9 %all-to-all-start.4 = ((f32[64,8,128]{2,1,0:T(8,128)}), f32[64,8,128]{2,1,0:T(8,128)}, u32[]{:S(2)}, u32[]{:S(2)}) async-start(f32[64,8,128]{2,1,0:T(8,128)} %reshape.124), calls=%async_computation.4 | async-start | bytes 524288 | tf_op jit(solution)/shard_map/cond/branch_1_fun/all_to_all | solution.py:20
  245.4 1.0 broadcast_multiply_fusion
  246.4 1.5 copy.46
  247.9 2.1 convolution_add_fusion
  250.0 4.6 %fusion.6 = f32[2,256,400]{2,1,0:T(8,128)} fusion(f32[2,400,400]{2,1,0:T(8,128)S(1)} %copy-done.1, f32[50,2,8,256]{3,2,1,0:T(8,128)S(1)} %bitcast.46), kind=kOutput, calls=%fused_computation.16 | convolution fusion | flops 983040000 | bytes 2918400 | tf_op jit(solution)/shard_map/cond/branch_1_fun/reshape | solution.py:62
  254.6 6.5 %scatter_custom_fusion = f32[2048,400]{1,0:T(8,128)} fusion(s32[512]{0:T(512)S(1)} %compare_select_fusion.2, f32[512,400]{1,0:T(8,128)} %bitcast.49, f32[]{:T(128)} %constant.15.clone), kind=kCustom, calls=%fused_computation.8 | custom fusion | flops 204800 | bytes 3277312 | tf_op jit(solution)/shard_map/cond/branch_1_fun/scatter-add | solution.py:63
  261.1 7.7 %scatter_fusion = f32[2048,400]{1,0:T(8,128)} fusion(f32[2048,400]{1,0:T(8,128)} %scatter_custom_fusion, s32[512]{0:T(512)S(1)} %compare_select_fusion.1, f32[512,400]{1,0:T(8,128)S(1)} %copy.46), kind=kCustom, calls=%fused_computation.5 | custom fusion | flops 204800 | bytes 2459648 | tf_op jit(solution)/shard_map/cond/branch_1_fun/scatter-add | solution.py:64
  268.8 1.0 reduce_sum.25
  269.8 5.0 %scatter_custom_fusion.2 = f32[2048,400]{1,0:T(8,128)} fusion(f32[2048,400]{1,0:T(8,128)} %scatter_fusion, s32[2]{0:T(128)S(1)} %compare_select_fusion.3, f32[2,512]{1,0:T(2,128)S(1)} %reshape.125), kind=kCustom, calls=%fused_computation.30 | custom fusion | flops 800 | bytes 3280896 | tf_op jit(solution)/shard_map/cond/branch_1_fun/scatter-add | solution.py:65
  274.8 6.5 %reshape.126 = f32[64,100,128]{2,1,0:T(8,128)} reshape(f32[2048,400]{1,0:T(8,128)} %scatter_custom_fusion.2) | data formatting | bytes 6553600 | tf_op jit(solution)/shard_map/cond/branch_1_fun/reshape | solution.py:66
  281.3 15.0 %all-to-all-start.5 = ((f32[64,100,128]{2,1,0:T(8,128)}), f32[64,100,128]{2,1,0:T(8,128)}, u32[]{:S(2)}, u32[]{:S(2)}) async-start(f32[64,100,128]{2,1,0:T(8,128)} %reshape.126), calls=%async_computation.5 | async-start | bytes 6815744 | tf_op jit(solution)/shard_map/cond/branch_1_fun/all_to_all | solution.py:20
  296.4 81.0 %all-to-all-done.5 = f32[64,100,128]{2,1,0:T(8,128)} async-done(((f32[64,100,128]{2,1,0:T(8,128)}), f32[64,100,128]{2,1,0:T(8,128)}, u32[]{:S(2)}, u32[]{:S(2)}) %all-to-all-start.5) | async-done | bytes 3276832 | tf_op jit(solution)/shard_map/cond/branch_1_fun/all_to_all | solution.py:20
  377.5 6.7 %reshape.201 = f32[2048,400]{1,0:T(8,128)} reshape(f32[64,100,128]{2,1,0:T(8,128)} %all-to-all-done.5) | data formatting | bytes 6553600 | tf_op jit(solution)/shard_map/cond/branch_1_fun/reshape | solution.py:66
  384.1 13.4 %scatter_custom_fusion.3 = f32[256,400]{1,0:T(8,128)S(1)} fusion(s32[2048]{0:T(1024)S(1)} %bitcast.61, f32[2048,400]{1,0:T(8,128)} %reshape.201, f32[]{:T(128)} %constant.15.clone), kind=kCustom, calls=%fused_computation.23 | custom fusion | flops 819200 | bytes 410112 | tf_op jit(solution)/shard_map/cond/branch_1_fun/scatter-add | solution.py:67
  398.2 0.7 copy-done.18
  (47 shorter events, 0.8 us)
Async XLA Ops:
  0.6 37.2 %copy-start.3 = (f32[256,400]{0,1:T(8,128)S(1)}, f32[256,400]{0,1:T(8,128)}, u32[]{:S(2)}) copy-start(f32[256,400]{0,1:T(8,128)} %param.9) | copy-start | bytes 1228804
  0.6 36.4 %collective-permute-start.2 = (f32[400,256]{1,0:T(8,128)}, f32[400,256]{1,0:T(8,128)S(1)}, u32[]{:S(2)}, u32[]{:S(2)}) collective-permute-start(f32[400,256]{1,0:T(8,128)} %bitcast.43), channel_id=1, source_target_pairs={{0,128},{8,136},{16,144},{24,152},{32,160},{40,168},{48,176},{56,1... | collective-permute-start | bytes 1228808 | tf_op jit(solution)/shard_map/ppermute | solution.py:451
  5.7 31.4 %all-to-all-start.6 = ((f32[64,1,128]{2,1,0:T(1,128)}), f32[64,1,128]{2,1,0:T(1,128)S(1)}, u32[]{:S(2)}, u32[]{:S(2)}) async-start(f32[64,1,128]{2,1,0:T(1,128)} %bitcast.52), calls=%async_computation.6 | async-start | bytes 65536 | tf_op jit(solution)/shard_map/all_to_all | solution.py:20
  24.7 12.4 %copy-start.10 = (s32[64,128]{1,0:T(8,128)}, s32[64,128]{1,0:T(8,128)S(1)}, u32[]{:S(2)}) copy-start(s32[64,128]{1,0:T(8,128)S(1)} %pad.16.touched_ref) | copy-start | bytes 98308
  24.7 5.7 %collective-permute-start.1 = (s32[64,128]{1,0:T(8,128)S(1)}, s32[64,128]{1,0:T(8,128)S(1)}, u32[]{:S(2)}, u32[]{:S(2)}) collective-permute-start(s32[64,128]{1,0:T(8,128)S(1)} %pad.16.touched_ref), channel_id=1, source_target_pairs={{0,128},{8,136},{16,144},{24,152},{32,160},{40,168},{48,176},{56,1... | collective-permute-start | bytes 98312 | tf_op jit(solution)/shard_map/ppermute | solution.py:451
  30.3 6.8 %copy-start.11 = (s32[64,128]{1,0:T(8,128)}, s32[64,128]{1,0:T(8,128)S(1)}, u32[]{:S(2)}) copy-start(s32[64,128]{1,0:T(8,128)S(1)} %collective-permute-done.1.mate_touched_ref) | copy-start | bytes 98308
  37.1 0.8 copy-start.5
  46.0 0.6 copy-start.8
  62.2 8.2 %copy-start.14 = (s32[512]{0:T(512)S(1)}, s32[512]{0:T(512)}, u32[]{:S(2)}) copy-start(s32[512]{0:T(512)} %get-tuple-element.52) | copy-start | bytes 6148 | tf_op jit(solution)/shard_map/cond
  62.2 8.2 %copy-start.17 = (s32[2]{0:T(128)S(1)}, s32[2]{0:T(128)}, u32[]{:S(2)}) copy-start(s32[2]{0:T(128)} %get-tuple-element.53) | copy-start | bytes 28 | tf_op jit(solution)/shard_map/cond
  62.2 120.9 %all-to-all-start.2 = ((f32[64,100,128]{2,1,0:T(8,128)}), f32[64,100,128]{2,1,0:T(8,128)}, u32[]{:S(2)}, u32[]{:S(2)}) async-start(f32[64,100,128]{2,1,0:T(8,128)} %reshape.117), calls=%async_computation.2 | async-start | bytes 6815744 | tf_op jit(solution)/shard_map/cond/branch_1_fun/all_to_all | solution.py:20
  70.5 136.9 %copy-start.12 = (s32[512]{0:T(512)S(1)}, s32[512]{0:T(512)}, u32[]{:S(2)}) copy-start(s32[512]{0:T(512)} %get-tuple-element.50) | copy-start | bytes 6148 | tf_op jit(solution)/shard_map/cond
  193.4 36.0 %all-to-all-start.3 = ((f32[64,8,128]{2,1,0:T(8,128)}), f32[64,8,128]{2,1,0:T(8,128)}, u32[]{:S(2)}, u32[]{:S(2)}) async-start(f32[64,8,128]{2,1,0:T(8,128)} %broadcast_in_dim.30), calls=%async_computation.3 | async-start | bytes 524288 | tf_op jit(solution)/shard_map/cond/branch_1_fun/all_to_all | solution.py:20
  216.6 2.4 copy-start.1
  232.3 0.7 copy-start.4
  236.5 32.3 %all-to-all-start.4 = ((f32[64,8,128]{2,1,0:T(8,128)}), f32[64,8,128]{2,1,0:T(8,128)}, u32[]{:S(2)}, u32[]{:S(2)}) async-start(f32[64,8,128]{2,1,0:T(8,128)} %reshape.124), calls=%async_computation.4 | async-start | bytes 524288 | tf_op jit(solution)/shard_map/cond/branch_1_fun/all_to_all | solution.py:20
  281.3 15.1 %copy-start.9 = (s32[64,32]{1,0:T(8,128)S(1)}, s32[64,32]{1,0:T(8,128)}, u32[]{:S(2)}) copy-start(s32[64,32]{1,0:T(8,128)} %copy-done.8) | copy-start | bytes 24580 | tf_op jit(solution)/shard_map/cond
  281.3 96.2 %all-to-all-start.5 = ((f32[64,100,128]{2,1,0:T(8,128)}), f32[64,100,128]{2,1,0:T(8,128)}, u32[]{:S(2)}, u32[]{:S(2)}) async-start(f32[64,100,128]{2,1,0:T(8,128)} %reshape.126), calls=%async_computation.5 | async-start | bytes 6815744 | tf_op jit(solution)/shard_map/cond/branch_1_fun/all_to_all | solution.py:20
  296.4 101.2 %copy-start.16 = (f32[256]{0:T(256)S(1)}, f32[256]{0:T(256)}, u32[]{:S(2)}) copy-start(f32[256]{0:T(256)} %get-tuple-element.54) | copy-start | bytes 3076 | tf_op jit(solution)/shard_map/cond
  398.2 0.8 copy-start.18
  398.2 0.7 copy-start.19

commit v4 on v3

--- a/solution.py
+++ b/solution.py
@@ -70,26 +70,17 @@
     return new_table.T, new_state.reshape(1, -1)
 
 
-HEAD = 16
-CAP = 20
-REGION = 24
+CAP = 22
 PARTS = 3
-BLOCK = 64
-EXTRA = PARTS * HEAD
 TAIL = 16
 PER_LINE = LANES // TAIL
-LINES = EXTRA + PARTS * (CAP - HEAD)
+LINES = PARTS * CAP
+BLOCK = LINES + -(-CAP // PER_LINE)
 WIDE = (PARTS + 1) * LANES
 MATE = 16
 SENT = 32
 AT_COUNTS = 2 * SENT
 AT_NEGS = 3 * SENT
-
-
-def line_of(part, k):
-    if k < HEAD:
-        return part * HEAD + k
-    return EXTRA + part * (CAP - HEAD) + k - HEAD
 
 
 def iota(shape, dim):
@@ -278,25 +269,22 @@
     main = PARTS * LANES
     table = jnp.concatenate([table_ref[...], mate_table_ref[...]], 1)
     wide = jnp.concatenate([table[:main]] + [table[main:]] * PER_LINE, 0)
-    wide = pieces(wide, 3)
+    wide = pieces(wide, 2)
     group = lane // TAIL
-    for part in range(PARTS):
+    for part in range(BLOCK - LINES):
         first = part * PER_LINE
         last = min(first + PER_LINE, CAP)
         chosen = onehot[first * peers : last * peers, :]
-        got = dot(chosen, wide[2], 1, 1) + dot(chosen, wide[1], 1, 1)
-        got = got + dot(chosen, wide[0], 1, 1)
+        got = dot(chosen, wide[1], 1, 1) + dot(chosen, wide[0], 1, 1)
         line = jnp.zeros(marks.shape, F32)
         for k in range(first, last):
             mine = got[(k - first) * peers : (k - first + 1) * peers]
             for t in range(PARTS):
-                out_ref[pl.ds(line_of(t, k), peers, stride=BLOCK), :] = mine[
+                out_ref[pl.ds(t * CAP + k, peers, stride=BLOCK), :] = mine[
                     :, t * LANES : (t + 1) * LANES
                 ]
             line = line + jnp.where(group == k - first, mine[:, main:], 0.0)
         out_ref[pl.ds(LINES + part, peers, stride=BLOCK), :] = line
-    for spare in range(LINES + PARTS, BLOCK):
-        out_ref[pl.ds(spare, peers, stride=BLOCK), :] = jnp.zeros(marks.shape, F32)
 
 
 def place_kernel(number, marks_ref, source_ref, target_ref, edge_ref, neg_ref):
@@ -323,8 +311,8 @@
     mates = dot(total, swap)
 
     def placed(owner, order, mate):
-        own = owner * REGION + order
-        return jnp.where(order < CAP, own, mate_of(owner) * REGION + mate + order - CAP)
+        at_mate = (mate + order - CAP) * peers + mate_of(owner)
+        return jnp.where(order < CAP, order * peers + owner, at_mate)
 
     order = jnp.sum(dot(rank.astype(BF16), at_owner) * at_within.astype(F32), 0, keepdims=True)
     mate = dot(mates.astype(BF16), at_owner)[:1]
@@ -339,39 +327,31 @@
         earlier = earlier + jnp.sum(at, 0, keepdims=True)
 
 
-def unpack(ref):
-    peers = ref.shape[0]
-    count = peers * REGION
-    ends = ref[:, EXTRA : EXTRA + PER_LINE, :], ref[:, EXTRA + PER_LINE :, :]
-    rest = ends[0], pltpu.roll(ends[0], PER_LINE // 2, 1), ends[1]
-    parts = []
-    for t in range(PARTS):
-        part = jnp.concatenate([ref[:, t * HEAD : (t + 1) * HEAD, :], rest[t]], 1)
-        parts.append(part.reshape(count, LANES))
-    at = LINES - EXTRA - PER_LINE
-    tails = [
-        jnp.broadcast_to(ends[1][:, at + t : at + t + 1, :], (peers, PER_LINE, LANES))
-        for t in range(PARTS)
-    ]
-    tails = jnp.concatenate(tails, 1)
-    own = iota(tails.shape, 2) // TAIL == iota(tails.shape, 1) % PER_LINE
-    parts.append(jnp.where(own, tails, 0.0).reshape(count, LANES))
-    both = [pieces(part, 2) for part in parts]
-    return jnp.concatenate([p[0] for p in both], 1), jnp.concatenate([p[1] for p in both], 1)
+def unpack(ref, hi_ref, lo_ref):
+    peers = ref.shape[0] // BLOCK
+    group = iota((peers, LANES), 1) // TAIL
+    for k in range(CAP):
+        tails = ref[pl.ds(LINES + k // PER_LINE, peers, stride=BLOCK), :]
+        parts = [ref[pl.ds(t * CAP + k, peers, stride=BLOCK), :] for t in range(PARTS)]
+        parts.append(jnp.where(group == k % PER_LINE, tails, 0.0))
+        for t, part in enumerate(parts):
+            hi, lo = pieces(part, 2)
+            hi_ref[k * peers : (k + 1) * peers, t * LANES : (t + 1) * LANES] = hi
+            lo_ref[k * peers : (k + 1) * peers, t * LANES : (t + 1) * LANES] = lo
 
 
 def edges_kernel(
     block_ref, place_ref, neg_place_ref, row_place_ref, rel_hi_ref, rel_lo_ref,
     out_ref, slots_hi, slots_lo, grad_hi, grad_lo,
 ):
-    peers = block_ref.shape[0]
+    peers = block_ref.shape[0] // BLOCK
     edges = place_ref.shape[0] // 2
     total = neg_place_ref.shape[0]
     kinds = rel_hi_ref.shape[0]
     per_rel = edges // kinds
-    count = peers * REGION
+    count = peers * CAP
     main = PARTS * LANES
-    slots_hi[...], slots_lo[...] = unpack(block_ref)
+    unpack(block_ref, slots_hi, slots_lo)
 
     def rows_at(spot):
         chosen = bits(iota((spot.shape[0], count), 1) == spot)
@@ -403,37 +383,30 @@
     keep(2 * edges, shares)
 
     spot = row_place_ref[...]
-    half = peers // 2
-    count = half * REGION
-    for first in (0, half):
-        chosen = bits(iota((count, spot.shape[1]), 0) + first * REGION == spot)
+    group = iota((peers, LANES), 1) // TAIL
+    for part in range(BLOCK - LINES):
+        first = part * PER_LINE
+        last = min(first + PER_LINE, CAP)
+        chosen = iota(((last - first) * peers, spot.shape[1]), 0) + first * peers
+        chosen = bits(chosen == spot)
         got = dot(chosen, grad_lo[...]) + dot(chosen, grad_hi[...])
-        span = slice(first, first + half)
-        rest = []
-        for t in range(PARTS):
-            part = got[:, t * LANES : (t + 1) * LANES].reshape(half, REGION, LANES)
-            out_ref[span, t * HEAD : (t + 1) * HEAD, :] = part[:, :HEAD]
-            rest.append(part[:, HEAD:])
-        out_ref[span, EXTRA : EXTRA + PER_LINE, :] = rest[0] + pltpu.roll(rest[1], PER_LINE // 2, 1)
-        last = rest[2]
-        line = got[:, main:].reshape(half, REGION, LANES)
-        own = iota(line.shape, 2) // TAIL == iota(line.shape, 1) % PER_LINE
-        line = jnp.where(own, line, 0.0)
-        at = LINES - EXTRA - PER_LINE
-        for t in range(PARTS):
-            mine = jnp.sum(line[:, t * PER_LINE : (t + 1) * PER_LINE], 1, keepdims=True)
-            here = iota(last.shape, 1) == at + t
-            last = jnp.where(here, jnp.broadcast_to(mine, last.shape), last)
-        out_ref[span, EXTRA + PER_LINE :, :] = last
-
-
-def sum_kernel(first, block_ref, rows_ref, out_ref):
+        line = jnp.zeros((peers, LANES), F32)
+        for k in range(first, last):
+            mine = got[(k - first) * peers : (k - first + 1) * peers]
+            for t in range(PARTS):
+                out_ref[pl.ds(t * CAP + k, peers, stride=BLOCK), :] = mine[
+                    :, t * LANES : (t + 1) * LANES
+                ]
+            line = line + jnp.where(group == k - first, mine[:, main:], 0.0)
+        out_ref[pl.ds(LINES + part, peers, stride=BLOCK), :] = line
+
+
+def sum_kernel(first, block_ref, rows_ref, out_ref, hi_ref, lo_ref):
     width, owned = out_ref.shape
     main = PARTS * LANES
-    hi, lo = unpack(block_ref)
-    count = hi.shape[0]
-    chosen = bits(iota((owned, count), 0) + first == rows_ref[...])
-    got = dot(chosen, lo) + dot(chosen, hi)
+    unpack(block_ref, hi_ref, lo_ref)
+    chosen = bits(iota((owned, hi_ref.shape[0]), 0) + first == rows_ref[...])
+    got = dot(chosen, lo_ref[...]) + dot(chosen, hi_ref[...])
     grad = jnp.concatenate([got[:, :main], spread(got[:, main:])], 1)
     out_ref[...] = grad.T[:width]
 
@@ -451,11 +424,18 @@
     return lax.ppermute(x, "grp", [(p, p ^ MATE) for p in range(peers)])
 
 
+def exchange_blocks(blocks):
+    peers = lax.axis_size("grp")
+    return exchange(blocks.reshape(peers, BLOCK, 1, LANES)).reshape(blocks.shape)
+
+
 def compact_path(marks, blocks, rows, source, target, number, rel_hi, rel_lo, table, state):
     peers = marks.shape[0]
     edges = source.shape[1]
     width, owned = table.shape
-    blocks = exchange(blocks.reshape(peers, BLOCK, LANES))
+    count = peers * CAP
+    split = [pltpu.VMEM((count, WIDE), BF16)] * 2
+    blocks = exchange_blocks(blocks)
     edge_place, neg_place = call(
         functools.partial(place_kernel, number),
         (shaped(1, 2 * edges, dtype=jnp.int32), shaped(peers * number, 1, dtype=jnp.int32)),
@@ -463,23 +443,21 @@
     row_place = jnp.concatenate([edge_place, neg_place.reshape(1, -1)], 1)
     grads = call(
         edges_kernel,
-        shaped(peers, BLOCK, LANES),
-        scratch_shapes=[
-            pltpu.VMEM((peers * REGION, WIDE), BF16),
-            pltpu.VMEM((peers * REGION, WIDE), BF16),
-            pltpu.VMEM((row_place.shape[1], WIDE), BF16),
-            pltpu.VMEM((row_place.shape[1], WIDE), BF16),
-        ],
+        shaped(*blocks.shape),
+        scratch_shapes=split + [pltpu.VMEM((row_place.shape[1], WIDE), BF16)] * 2,
     )(blocks, edge_place.reshape(-1, 1), neg_place, row_place, rel_hi, rel_lo)
-    returned = exchange(grads)
-    rows = rows[:, :REGION].reshape(1, -1)
-    for_mate = call(functools.partial(sum_kernel, owned), shaped(width, owned))(returned, rows)
-    from_mate = swap_mates(for_mate)
-    own = call(functools.partial(sum_kernel, 0), shaped(width, owned))(returned, rows)
+    returned = exchange_blocks(grads)
+    rows = rows[:, :CAP].T.reshape(1, -1)
+
+    def summed(first):
+        kernel = functools.partial(sum_kernel, first)
+        return call(kernel, shaped(width, owned), scratch_shapes=split)(returned, rows)
+
+    from_mate = swap_mates(summed(owned))
     return call(
         update_kernel,
         (shaped(width, owned), shaped(1, owned)),
-    )(own, from_mate, table, state)
+    )(summed(0), from_mate, table, state)
 
 
 def per_device(table, row_state, relations, touched, source, target, neg_slots):

time: 405 us -> 308 us (0.76)
  the two profiles are of different devices: /device:TPU:3 before, /device:TPU:6 now
where the time goes in v4:
time: 308 us; the launch traced here: 306 us
  waiting for transfers between devices  211 us (69%)
  starting transfers between devices  44.8 us (15%)
  Pallas kernels  34.3 us (11%)
  local copies, waits for them, and re-layouts  8.28 us (3%)
  other arithmetic  5.27 us (2%)
    all_to_all x3, waiting for transfers between devices, exchange(): lax.all_to_all(blocks, 'grp', split_axis=0, concat_axis=0, tiled=True)  209 us
    all_to_all x3, starting transfers between devices, exchange(): lax.all_to_all(blocks, 'grp', split_axis=0, concat_axis=0, tiled=True)  34.4 us
    pallas_call x1, Pallas kernels, compact_path(): call(edges_kernel, shaped(*blocks.shape), scratch_shapes=split + [pltpu.V...  16.6 us
    ppermute x3, starting transfers between devices, swap_mates(): return lax.ppermute(x, 'grp', [(p, p ^ MATE) for p in range(peers)])  10.4 us
    pallas_call x2, Pallas kernels, summed(): call(kernel, shaped(width, owned), scratch_shapes=split)(returned, rows)  7.91 us
  transfers between devices with their start and end apart: 6, of which 4 were waited for; matrix products, arithmetic and copies ran while one was open for 3% of the time, Pallas kernels for 2%

profile of v4, /device:TPU:6, one launch (start us, length us, event | category | flops | bytes accessed | tf_op | source)
XLA Modules:
  0.0 305.5 jit_solution(17000991169476600668)
XLA Ops:
  0.6 0.0 copy-start.3
  0.6 0.0 copy-start.15
  0.7 0.0 copy-start.11
  0.7 0.0 copy-start.10
  0.7 0.0 copy-start.8
  0.7 0.0 copy-start.12
  0.7 3.6 %collective-permute-start.2 = (f32[400,256]{1,0:T(8,128)}, f32[400,256]{1,0:T(8,128)S(1)}, u32[]{:S(2)}, u32[]{:S(2)}) collective-permute-start(f32[400,256]{1,0:T(8,128)} %bitcast.51), channel_id=1, source_target_pairs={{0,128},{8,136},{16,144},{24,152},{32,160},{40,168},{48,176},{56,1... | collective-permute-start | bytes 1228808 | tf_op jit(solution)/shard_map/ppermute | solution.py:424
  4.3 1.7 shard_map.86
  6.0 18.4 %all-to-all-start.6 = ((f32[64,1,128]{2,1,0:T(1,128)}), f32[64,1,128]{2,1,0:T(1,128)S(1)}, u32[]{:S(2)}, u32[]{:S(2)}) async-start(f32[64,1,128]{2,1,0:T(1,128)} %bitcast.60), calls=%async_computation.6 | async-start | bytes 65536 | tf_op jit(solution)/shard_map/all_to_all | solution.py:20
  24.5 0.8 copy.53
  25.3 0.0 copy-start.7
  25.3 3.5 %collective-permute-start.1 = (s32[64,128]{1,0:T(8,128)S(1)}, s32[64,128]{1,0:T(8,128)S(1)}, u32[]{:S(2)}, u32[]{:S(2)}) collective-permute-start(s32[64,128]{1,0:T(8,128)S(1)} %pad.16.touched_ref), channel_id=1, source_target_pairs={{0,128},{8,136},{16,144},{24,152},{32,160},{40,168},{48,176},{56,1... | collective-permute-start | bytes 98312 | tf_op jit(solution)/shard_map/ppermute | solution.py:424
  28.8 3.1 fusion.15
  31.8 0.0 collective-permute-done.1.mate_touched_ref
  31.9 0.0 copy-start.9
  31.9 7.0 %all-to-all-done.6 = f32[64,1,128]{2,1,0:T(1,128)S(1)} async-done(((f32[64,1,128]{2,1,0:T(1,128)}), f32[64,1,128]{2,1,0:T(1,128)S(1)}, u32[]{:S(2)}, u32[]{:S(2)}) %all-to-all-start.6) | async-done | bytes 32800 | tf_op jit(solution)/shard_map/all_to_all | solution.py:20
  38.8 0.0 collective-permute-done.2.mate_table_ref
  38.8 0.0 copy-done.7
  38.8 0.0 copy-done.9
  38.8 0.7 copy-done.5
  39.6 0.0 copy-done.3
  39.6 4.7 %shard_map.87 = (f32[4416,128]{1,0:T(8,128)}, s32[64,128]{1,0:T(8,128)S(1)}, s32[1]{0:T(128)}) custom-call(s32[1]{0:T(128)} %bitcast.13.me_ref, f32[64,128]{1,0:T(8,128)S(1)} %bitcast.58, s32[64,128]{1,0:T(8,128)} %copy-done.7, s32[64,128]{1,0:T(8,128)} %copy-done.9, f32[400,256]{1,0:T(8,128)S(1)} %bitcast.52, f32[400,256]{1,0:T(8,128)} %copy-done.5), custom_call_target="tpu_custom_call" | custom-call | tf_op jit(solution)/shard_map/pallas_call | solution.py:480
  44.9 0.0 copy-done.15
  44.9 0.0 copy-done.11
  44.9 0.0 copy-done.10
  44.9 0.0 copy-done.8
  44.9 0.0 copy-done.12
  44.9 260.0 %conditional.1 = (f32[256]{0:T(256)S(1)}, f32[400,256]{1,0:T(8,128)}) conditional(s32[]{:T(128)} %bitcast.20, (f32[4416,128]{1,0:T(8,128)}, f32[64,128]{1,0:T(8,128)S(1)}, s32[1,512]{1,0:T(1,128)S(1)}, s32[1,512]{1,0:T(1,128)S(1)}, bf16[2,512,512]{2,1,0:T(8,128)(2,1)}, /*index=5*/bf16[2,512,512]{2,1,0:T(8,128)(2,1)}, s32[64,128]{1,0:T(8,128)S(1)}, ...), branch_computations={%region_0.1_spmd, %region_1.9_spmd} | conditional | flops 2912907008 | bytes 98542240 | solution.py:491
  44.9 8.1 %all-to-all-start = ((f32[64,69,1,128]{3,2,1,0:T(1,128)}), f32[64,69,1,128]{3,2,1,0:T(1,128)S(1)}, u32[]{:S(2)}, u32[]{:S(2)}) async-start(f32[64,69,1,128]{3,2,1,0:T(1,128)} %bitcast.56), calls=%async_computation | async-start | bytes 4521984 | tf_op jit(solution)/shard_map/cond/branch_0_fun/all_to_all | solution.py:20
  53.0 1.4 branch_0_fun.5
  54.4 1.7 copy.38.place_ref
  56.1 0.9 reduce.1
  57.0 1.3 pad_add_fusion.row_place_ref
  58.3 98.3 %all-to-all-done = f32[64,69,1,128]{3,2,1,0:T(1,128)S(1)} async-done(((f32[64,69,1,128]{3,2,1,0:T(1,128)}), f32[64,69,1,128]{3,2,1,0:T(1,128)S(1)}, u32[]{:S(2)}, u32[]{:S(2)}) %all-to-all-start) | async-done | bytes 2261024 | tf_op jit(solution)/shard_map/cond/branch_0_fun/all_to_all | solution.py:20
  156.6 1.5 copy-done.2
  158.1 16.6 %branch_0_fun.6 = f32[4416,128]{1,0:T(8,128)} custom-call(f32[4416,128]{1,0:T(8,128)} %bitcast.45, s32[1024,1]{1,0:T(8,128)} %copy.38.place_ref, s32[128,1]{1,0:T(8,128)} %get-tuple-element.40.neg_place_ref, s32[1,1152]{1,0:T(1,128)} %pad_add_fusion.row_place_ref, bf16[2,512,512]{2,1,0:T(8,128)(2,1)} %get-tuple-element.41.rel_hi_ref, ...), custom_call_target="tpu_custom_call" | custom-call | tf_op jit(solution)/shard_map/cond/branch_0_fun/pallas_call | solution.py:444
  174.7 7.9 %all-to-all-start.1 = ((f32[64,69,1,128]{3,2,1,0:T(1,128)}), f32[64,69,1,128]{3,2,1,0:T(1,128)S(1)}, u32[]{:S(2)}, u32[]{:S(2)}) async-start(f32[64,69,1,128]{3,2,1,0:T(1,128)} %bitcast.46), calls=%async_computation.1 | async-start | bytes 4521984 | tf_op jit(solution)/shard_map/cond/branch_0_fun/all_to_all | solution.py:20
  182.5 0.1 copy.54
  182.7 0.7 reshape.122.rows_ref
  183.3 103.4 %all-to-all-done.1 = f32[64,69,1,128]{3,2,1,0:T(1,128)S(1)} async-done(((f32[64,69,1,128]{3,2,1,0:T(1,128)}), f32[64,69,1,128]{3,2,1,0:T(1,128)S(1)}, u32[]{:S(2)}, u32[]{:S(2)}) %all-to-all-start.1) | async-done | bytes 2261024 | tf_op jit(solution)/shard_map/cond/branch_0_fun/all_to_all | solution.py:20
  286.7 1.4 copy-done
  288.2 3.9 %branch_0_fun.8 = f32[400,256]{1,0:T(8,128)} custom-call(f32[4416,128]{1,0:T(8,128)} %bitcast.42, s32[1,1408]{1,0:T(1,128)} %reshape.122.rows_ref), custom_call_target="tpu_custom_call" | custom-call | tf_op jit(solution)/shard_map/cond/branch_0_fun/pallas_call | solution.py:454
  292.1 3.3 %collective-permute-start = (f32[400,256]{1,0:T(8,128)}, f32[400,256]{1,0:T(8,128)S(1)}, u32[]{:S(2)}, u32[]{:S(2)}) collective-permute-start(f32[400,256]{1,0:T(8,128)} %branch_0_fun.8), channel_id=1, source_target_pairs={{0,128},{8,136},{16,144},{24,152},{32,160},{40,168},{48,176},{56,1... | collective-permute-start | bytes 1228808 | tf_op jit(solution)/shard_map/cond/branch_0_fun/ppermute | solution.py:424
  295.5 4.0 %branch_0_fun.7.own_ref = f32[400,256]{1,0:T(8,128)} custom-call(f32[4416,128]{1,0:T(8,128)} %bitcast.43, s32[1,1408]{1,0:T(1,128)} %reshape.122.rows_ref), custom_call_target="tpu_custom_call" | custom-call | tf_op jit(solution)/shard_map/cond/branch_0_fun/pallas_call | solution.py:454
  299.4 2.8 collective-permute-done.mate_ref
  302.2 0.8 copy-done.6
  302.9 2.0 branch_0_fun.9
  305.0 0.6 copy-done.16
  (7 shorter events, 0.0 us)
Async XLA Ops:
  0.6 39.0 %copy-start.3 = (f32[256,400]{0,1:T(8,128)S(1)}, f32[256,400]{0,1:T(8,128)}, u32[]{:S(2)}) copy-start(f32[256,400]{0,1:T(8,128)} %param.9) | copy-start | bytes 1228804
  0.6 44.2 %copy-start.15 = (s32[2]{0:T(128)S(1)}, s32[2]{0:T(128)}, u32[]{:S(2)}) copy-start(s32[2]{0:T(128)} %negs_ref.1) | copy-start | bytes 28
  0.7 44.2 %copy-start.11 = (s32[512]{0:T(512)S(1)}, s32[512]{0:T(512)}, u32[]{:S(2)}) copy-start(s32[512]{0:T(512)} %param.14) | copy-start | bytes 6148
  0.7 44.2 %copy-start.10 = (s32[512]{0:T(512)S(1)}, s32[512]{0:T(512)}, u32[]{:S(2)}) copy-start(s32[512]{0:T(512)} %param.13) | copy-start | bytes 6148
  0.7 44.2 %copy-start.8 = (s32[64,32]{0,1:T(8,128)S(1)}, s32[64,32]{0,1:T(8,128)}, u32[]{:S(2)}) copy-start(s32[64,32]{0,1:T(8,128)} %param.12) | copy-start | bytes 24580
  0.7 44.2 %copy-start.12 = (f32[256]{0:T(256)S(1)}, f32[256]{0:T(256)}, u32[]{:S(2)}) copy-start(f32[256]{0:T(256)} %param.10) | copy-start | bytes 3076
  0.7 38.1 %collective-permute-start.2 = (f32[400,256]{1,0:T(8,128)}, f32[400,256]{1,0:T(8,128)S(1)}, u32[]{:S(2)}, u32[]{:S(2)}) collective-permute-start(f32[400,256]{1,0:T(8,128)} %bitcast.51), channel_id=1, source_target_pairs={{0,128},{8,136},{16,144},{24,152},{32,160},{40,168},{48,176},{56,1... | collective-permute-start | bytes 1228808 | tf_op jit(solution)/shard_map/ppermute | solution.py:424
  6.0 32.8 %all-to-all-start.6 = ((f32[64,1,128]{2,1,0:T(1,128)}), f32[64,1,128]{2,1,0:T(1,128)S(1)}, u32[]{:S(2)}, u32[]{:S(2)}) async-start(f32[64,1,128]{2,1,0:T(1,128)} %bitcast.60), calls=%async_computation.6 | async-start | bytes 65536 | tf_op jit(solution)/shard_map/all_to_all | solution.py:20
  25.3 13.5 %copy-start.7 = (s32[64,128]{1,0:T(8,128)}, s32[64,128]{1,0:T(8,128)S(1)}, u32[]{:S(2)}) copy-start(s32[64,128]{1,0:T(8,128)S(1)} %pad.16.touched_ref) | copy-start | bytes 98308
  25.3 6.6 %collective-permute-start.1 = (s32[64,128]{1,0:T(8,128)S(1)}, s32[64,128]{1,0:T(8,128)S(1)}, u32[]{:S(2)}, u32[]{:S(2)}) collective-permute-start(s32[64,128]{1,0:T(8,128)S(1)} %pad.16.touched_ref), channel_id=1, source_target_pairs={{0,128},{8,136},{16,144},{24,152},{32,160},{40,168},{48,176},{56,1... | collective-permute-start | bytes 98312 | tf_op jit(solution)/shard_map/ppermute | solution.py:424
  31.9 7.0 %copy-start.9 = (s32[64,128]{1,0:T(8,128)}, s32[64,128]{1,0:T(8,128)S(1)}, u32[]{:S(2)}) copy-start(s32[64,128]{1,0:T(8,128)S(1)} %collective-permute-done.1.mate_touched_ref) | copy-start | bytes 98308
  38.8 0.8 copy-start.5
  44.9 111.7 %all-to-all-start = ((f32[64,69,1,128]{3,2,1,0:T(1,128)}), f32[64,69,1,128]{3,2,1,0:T(1,128)S(1)}, u32[]{:S(2)}, u32[]{:S(2)}) async-start(f32[64,69,1,128]{3,2,1,0:T(1,128)} %bitcast.56), calls=%async_computation | async-start | bytes 4521984 | tf_op jit(solution)/shard_map/cond/branch_0_fun/all_to_all | solution.py:20
  156.6 1.5 copy-start.2
  174.7 112.1 %all-to-all-start.1 = ((f32[64,69,1,128]{3,2,1,0:T(1,128)}), f32[64,69,1,128]{3,2,1,0:T(1,128)S(1)}, u32[]{:S(2)}, u32[]{:S(2)}) async-start(f32[64,69,1,128]{3,2,1,0:T(1,128)} %bitcast.46), calls=%async_computation.1 | async-start | bytes 4521984 | tf_op jit(solution)/shard_map/cond/branch_0_fun/all_to_all | solution.py:20
  286.7 1.4 copy-start
  292.1 10.0 %collective-permute-start = (f32[400,256]{1,0:T(8,128)}, f32[400,256]{1,0:T(8,128)S(1)}, u32[]{:S(2)}, u32[]{:S(2)}) collective-permute-start(f32[400,256]{1,0:T(8,128)} %branch_0_fun.8), channel_id=1, source_target_pairs={{0,128},{8,136},{16,144},{24,152},{32,160},{40,168},{48,176},{56,1... | collective-permute-start | bytes 1228808 | tf_op jit(solution)/shard_map/cond/branch_0_fun/ppermute | solution.py:424
  302.2 0.8 copy-start.6
  305.0 0.6 copy-start.16

commit v5 on v1

--- a/solution.py
+++ b/solution.py
@@ -1,12 +1,19 @@
+import functools
+
 import jax
 import jax.numpy as jnp
 from jax import lax
+from jax.experimental import pallas as pl
+from jax.experimental.pallas import tpu as pltpu
 from jax.sharding import PartitionSpec as P
 
 PRECISE = lax.Precision.HIGHEST
 LEARN_RATE = 0.1
 EPSILON = 1e-06
 LANES = 128
+VMEM = 56 * 1024 * 1024
+F32 = jnp.float32
+BF16 = jnp.bfloat16
 
 
 def exchange(blocks):
@@ -23,7 +30,7 @@
     return jnp.pad(rows, ((0, 0), (0, wide - width))).reshape(peers, -1, LANES)
 
 
-def per_device(table, row_state, relations, touched, source, target, neg_slots):
+def full_path(table, row_state, relations, touched, source, target, neg_slots):
     width = table.shape[1]
     peers, sent = touched.shape
     kinds = relations.shape[0]
@@ -53,14 +60,479 @@
     grad_head = jnp.einsum(
         "kef,kdf->ked", grad_query.reshape(kinds, per_rel, width), relations, precision=PRECISE
     ).reshape(kinds * per_rel, width)
-    slot_grad = jnp.zeros((slot_count, width), jnp.float32).at[source].add(grad_head)
+    slot_grad = jnp.zeros((slot_count, width), F32).at[source].add(grad_head)
     slot_grad = slot_grad.at[target].add(grad_tail)
     slot_grad = slot_grad.at[neg_slots].add(mine)
     returned = exchange(slot_grad.reshape(peers, -1, LANES)).reshape(slot_count, width)
-    row_grad = jnp.zeros(table.shape, jnp.float32).at[touched.reshape(-1)].add(returned)
+    row_grad = jnp.zeros(table.shape, F32).at[touched.reshape(-1)].add(returned)
     new_state = row_state + jnp.mean(row_grad * row_grad, -1)
     new_table = table - LEARN_RATE * row_grad / (jnp.sqrt(new_state)[:, None] + EPSILON)
-    return (new_table, new_state)
+    return new_table.T, new_state.reshape(1, -1)
+
+
+CAP = 19
+PARTS = 3
+TAIL = 16
+PER_LINE = LANES // TAIL
+LINES = PARTS * CAP
+BLOCK = LINES + -(-CAP // PER_LINE)
+WIDE = (PARTS + 1) * LANES
+COLUMN = 4
+DEPTH = 16
+SENT = 32
+ROOM = 32
+AT_NEGS = 64
+CODE = 2048
+
+
+def iota(shape, dim):
+    return lax.broadcasted_iota(jnp.int32, shape, dim)
+
+
+def bits(mask):
+    return jnp.where(mask, 1.0, 0.0).astype(BF16)
+
+
+def shift_down(x, by):
+    return lax.shift_right_logical(x, jnp.full(x.shape, by, x.dtype))
+
+
+def same_depth(a, b):
+    return lax.bitwise_and(a, DEPTH - 1) == lax.bitwise_and(b, DEPTH - 1)
+
+
+def grid(condition, size=LANES):
+    return bits(condition(iota((size, size), 0), iota((size, size), 1)))
+
+
+def pieces(x, count):
+    out = []
+    for _ in range(count):
+        piece = x.astype(BF16)
+        out.append(piece)
+        x = x - piece.astype(F32)
+    return out
+
+
+def dot(a, b, a_dim=1, b_dim=0):
+    return lax.dot_general(a, b, (((a_dim,), (b_dim,)), ((), ())), preferred_element_type=F32)
+
+
+def dot3(a, b, a_dim=1, b_dim=0):
+    a_hi, a_lo = a if isinstance(a, tuple) else pieces(a, 2)
+    b_hi, b_lo = b if isinstance(b, tuple) else pieces(b, 2)
+    small = dot(a_lo, b_hi, a_dim, b_dim) + dot(a_hi, b_lo, a_dim, b_dim)
+    return small + dot(a_hi, b_hi, a_dim, b_dim)
+
+
+def spread(x):
+    step = TAIL
+    while step < LANES:
+        x = x + pltpu.roll(x, step, 1)
+        step *= 2
+    return x
+
+
+def call(kernel, outs, **kw):
+    return pl.pallas_call(
+        kernel,
+        out_shape=outs,
+        compiler_params=pltpu.CompilerParams(vmem_limit_bytes=VMEM),
+        **kw,
+    )
+
+
+def shaped(*shape, dtype=F32):
+    return jax.ShapeDtypeStruct(shape, dtype)
+
+
+VECTOR = pl.BlockSpec(memory_space=pltpu.VMEM)
+SCALAR = pl.BlockSpec(memory_space=pltpu.SMEM)
+
+
+def mark_kernel(negs_ref, source_ref, target_ref, touched_ref, table_ref, out_ref, bundle_ref):
+    width = table_ref.shape[0]
+    sent, wide = touched_ref.shape
+    bundle_ref[:width, :] = table_ref[...]
+    bundle_ref[width:, :LANES] = jnp.concatenate(
+        [touched_ref[...].astype(F32), jnp.zeros((sent, LANES - wide), F32)], 1
+    )
+    bundle_ref[width:, LANES:] = jnp.zeros((sent, bundle_ref.shape[1] - LANES), F32)
+    peers = out_ref.shape[0] // 2
+    ids = jnp.concatenate([source_ref[...], target_ref[...]], 1)
+    count = ids.shape[1]
+    owner = shift_down(ids, 5)
+    within = lax.bitwise_and(ids, SENT - 1)
+    at_depth = bits(same_depth(iota((peers, count), 0), owner))
+    at_slot = bits(iota((LANES, count), 0) == shift_down(owner, 4) * SENT + within)
+    marks = dot(at_depth, at_slot, 1, 1)
+    out_ref[pl.ds(0, peers, stride=2), :] = jnp.where(marks > 0.0, 1.0, 0.0)
+    at_owner = bits(iota((LANES, count), 0) == owner)
+    at_within = bits(iota((SENT, count), 0) == within)
+    used = jnp.where(dot(at_within, at_owner, 1, 1) > 0.0, 1.0, 0.0)
+    info = jnp.broadcast_to(jnp.sum(used, 0, keepdims=True), marks.shape)
+    lane = iota(marks.shape, 1)
+    for n in range(negs_ref.shape[0]):
+        info = jnp.where(lane == AT_NEGS + n, negs_ref[n].astype(F32), info)
+    out_ref[pl.ds(1, peers, stride=2), :] = info
+
+
+def neg_columns(info, number):
+    lane = iota(info.shape, 1)
+    columns = []
+    for n in range(number):
+        column = jnp.sum(jnp.where(lane == AT_NEGS + n, info, 0.0), 1, keepdims=True)
+        columns.append(jnp.broadcast_to(column.astype(jnp.int32), info.shape))
+    return columns
+
+
+def before(count):
+    return grid(lambda a, b: b < a, count)
+
+
+def pack(rows, ref):
+    peers = ref.shape[0] // BLOCK
+    group = iota((peers, LANES), 1) // TAIL
+    for part in range(BLOCK - LINES):
+        line = jnp.zeros((peers, LANES), F32)
+        for k in range(part * PER_LINE, min((part + 1) * PER_LINE, CAP)):
+            mine = rows[k * peers : (k + 1) * peers]
+            for t in range(PARTS):
+                ref[pl.ds(t * CAP + k, peers, stride=BLOCK), :] = mine[:, t * LANES : (t + 1) * LANES]
+            line = line + jnp.where(group == k % PER_LINE, mine[:, PARTS * LANES :], 0.0)
+        ref[pl.ds(LINES + part, peers, stride=BLOCK), :] = line
+
+
+def pack_kernel(
+    number, me_ref, marks_ref, own_ref, first_ref, second_ref, third_ref, out_ref, codes_ref, flag_ref, onehot
+):
+    peers = marks_ref.shape[0] // 2
+    marks = marks_ref[pl.ds(0, peers, stride=2), :]
+    info = marks_ref[pl.ds(1, peers, stride=2), :]
+    lane = iota(marks.shape, 1)
+    negs = neg_columns(info, number)
+    me = me_ref[0]
+    depth, up = lax.bitwise_and(me, DEPTH - 1), lax.shift_right_logical(me, jnp.int32(4))
+    refs = own_ref, first_ref, second_ref, third_ref
+    width, owned = own_ref.shape[0] - SENT, own_ref.shape[1]
+
+    touched = jnp.zeros(marks.shape, F32)
+    for d, ref in enumerate(refs):
+        rows = jnp.concatenate([ref[width:, :LANES], jnp.zeros((LANES - SENT, LANES), F32)], 0)
+        rows = jnp.where(lane < SENT, rows.T[:peers] + (d * owned + 1.0), 0.0)
+        touched = touched + pltpu.roll(rows, SENT * lax.bitwise_xor(up, jnp.int32(d)), 1)
+
+    earlier = jnp.zeros((1, LANES), F32)
+    neg_rows = jnp.zeros((1, LANES), F32)
+    for slot in negs:
+        owner = shift_down(slot, 5)
+        at = jnp.where(lane == owner, 1.0, 0.0)
+        rank = jnp.sum((dot(before(peers), at.astype(BF16)) + earlier) * at, 1, keepdims=True)
+        earlier = earlier + jnp.sum(at, 0, keepdims=True)
+        base = shift_down(owner, 4) * SENT
+        at_row = lane == base + lax.bitwise_and(slot, SENT - 1)
+        row = jnp.sum(jnp.where(at_row, touched, 0.0), 1, keepdims=True)
+        here = same_depth(owner, depth) & (lane == base + rank.astype(jnp.int32))
+        neg_rows = neg_rows + jnp.sum(jnp.where(here, row, 0.0), 0, keepdims=True)
+
+    slots = jnp.where(lane < peers, info, 0.0)
+    column = grid(same_depth)
+    over_slots = jnp.sum(jnp.maximum(slots - CAP, 0.0), 0, keepdims=True)
+    sums = jnp.where(iota((PER_LINE, LANES), 0) == 0, earlier, over_slots).astype(BF16)
+    sums = jnp.max(dot(sums, column))
+    total = jnp.max(dot((slots + earlier).astype(BF16), column))
+    over = (total > COLUMN * CAP) | (sums > ROOM) | (jnp.max(over_slots) > ROOM)
+    flag_ref[0] = over.astype(jnp.int32)
+
+    neg_rows = jnp.broadcast_to(neg_rows, marks.shape)
+    neg_marks = jnp.where(neg_rows > 0.0, 1.0, 0.0)
+    block = grid(lambda a, b: a // SENT == b // SENT)
+    earlier_block = grid(lambda a, b: (a % SENT == 0) & (a // SENT < b // SENT))
+    rank = dot(marks.astype(BF16), grid(lambda a, b: (a // SENT == b // SENT) & (a <= b)))
+    used = dot(marks.astype(BF16), block)
+    neg_rank = used + (lane % SENT).astype(F32) + 1.0
+    need = used + dot(neg_marks.astype(BF16), block)
+    spare = jnp.maximum(CAP - need, 0.0)
+    excess_from = dot(jnp.maximum(need - CAP, 0.0).astype(BF16), earlier_block)
+    spare_from = dot(spare.astype(BF16), earlier_block)
+    own = lane // SENT == up
+
+    def mine(x):
+        return jnp.sum(jnp.where(lane == SENT * up, x, 0.0), 1, keepdims=True)
+
+    need, spare, spare_from = mine(need), mine(spare), mine(spare_from)
+
+    def placed(rank, mask):
+        x = excess_from + rank - (CAP + 1.0) - spare_from
+        helped = jnp.where((rank > CAP) & (x >= 0.0) & (x < spare), need + x, -1.0)
+        at = jnp.where(own, jnp.where(rank <= CAP, rank - 1.0, -1.0), helped)
+        return jnp.where(mask > 0.0, at, -1.0)
+
+    place, neg_place = placed(rank, marks), placed(neg_rank, neg_marks)
+    upto = grid(lambda a, b: a <= b)
+    helped = jnp.where((place >= 0.0) & ~own, 1.0, 0.0)
+    held = jnp.broadcast_to(jnp.sum(helped, 1, keepdims=True), marks.shape)
+    entry = dot(before(peers), held.astype(BF16)) + dot(helped.astype(BF16), upto)
+    codes = touched + CODE * jnp.where(helped > 0.0, entry + ROOM, 0.0)
+    neg_entry = dot(neg_marks.astype(BF16), upto)
+    neg_codes = neg_rows + CODE * jnp.where((neg_place >= 0.0) & ~own, neg_entry, 0.0)
+
+    spot = iota((peers, len(refs) * owned), 1)
+    out = jnp.zeros(marks.shape, jnp.int32)
+    for k in range(CAP):
+        code = jnp.where(place == k, codes, 0.0) + jnp.where(neg_place == k, neg_codes, 0.0)
+        code = jnp.sum(code, 1, keepdims=True).astype(jnp.int32)
+        out = jnp.where(lane == k, code, out)
+        onehot[k * peers : (k + 1) * peers, :] = bits(spot == lax.bitwise_and(code, CODE - 1) - 1)
+    codes_ref[...] = out
+
+    main = PARTS * LANES
+    table = jnp.concatenate([ref[:width] for ref in refs], 1)
+    wide = jnp.concatenate([table[:main]] + [table[main:]] * PER_LINE, 0)
+    wide = pieces(wide, 2)
+    pack(dot(onehot[...], wide[1], 1, 1) + dot(onehot[...], wide[0], 1, 1), out_ref)
+
+
+def place_kernel(number, marks_ref, source_ref, target_ref, edge_ref, neg_ref):
+    peers = marks_ref.shape[0] // 2
+    info = marks_ref[pl.ds(1, peers, stride=2), :]
+    ids = jnp.concatenate([source_ref[...], target_ref[...]], 1)
+    count = ids.shape[1]
+    owner = shift_down(ids, 5)
+    at_owner = bits(iota((LANES, count), 0) == owner)
+    at_within = bits(iota((SENT, count), 0) == lax.bitwise_and(ids, SENT - 1))
+    used = bits(dot(at_within, at_owner, 1, 1) > 0.0)
+    rank = dot(grid(lambda a, b: b <= a, SENT), used)
+    from_edges = rank[SENT - 1 :]
+    lane = iota(info.shape, 1)
+    negs = [shift_down(slot, 5) for slot in neg_columns(info, number)]
+    at_neg = [jnp.where(lane == slot, 1.0, 0.0) for slot in negs]
+    need = from_edges
+    for at in at_neg:
+        need = need + jnp.sum(at, 0, keepdims=True)
+
+    line = iota((PER_LINE, LANES), 0)
+    spare = jnp.maximum(CAP - need, 0.0)
+    excess = jnp.maximum(need - CAP, 0.0)
+    first = jnp.where(line == 0, need, jnp.where(line == 1, spare, jnp.where(line == 2, excess, 0.0)))
+    first = first.astype(BF16)
+    earlier = dot(first, grid(lambda a, b: same_depth(a, b) & (a // DEPTH < b // DEPTH)))
+    excess_from = earlier[2:3]
+    first = jnp.where(line == 2, jnp.broadcast_to(earlier[1:2], first.shape), first.astype(F32))
+    first = first.astype(BF16)
+    mates = [
+        dot(first, grid(lambda a, b: same_depth(a, b) & (a // DEPTH == y))) for y in range(COLUMN)
+    ]
+
+    def placed(owner, order, value):
+        owner = owner.astype(F32)
+        depth = owner - DEPTH * jnp.floor(owner / DEPTH)
+        place = order * peers + owner
+        x = value(excess_from) + order - CAP
+        for y, mate in enumerate(mates):
+            need, spare, start = (value(mate[i : i + 1]) for i in range(3))
+            here = (order >= CAP) & (x >= start) & (x < start + spare)
+            place = jnp.where(here, (need + x - start) * peers + y * DEPTH + depth, place)
+        return place.astype(jnp.int32)
+
+    def at_edges(row):
+        row = jnp.broadcast_to(row, (PER_LINE, LANES)).astype(BF16)
+        return dot(row, at_owner)[:1]
+
+    order = jnp.sum(dot(rank.astype(BF16), at_owner) * at_within.astype(F32), 0, keepdims=True)
+    edge_ref[...] = placed(owner, order - 1.0, at_edges)
+    for n, at in enumerate(at_neg):
+        order = dot(before(peers), at.astype(BF16)) + from_edges
+        order = jnp.sum(order * at, 1, keepdims=True)
+
+        def at_these(row):
+            return jnp.sum(row * at, 1, keepdims=True)
+
+        neg_ref[n * peers : (n + 1) * peers, :] = placed(negs[n][:, :1], order, at_these)
+        from_edges = from_edges + jnp.sum(at, 0, keepdims=True)
+
+
+def unpack(ref, hi_ref, lo_ref):
+    peers = ref.shape[0] // BLOCK
+    group = iota((peers, LANES), 1) // TAIL
+    for k in range(CAP):
+        tails = ref[pl.ds(LINES + k // PER_LINE, peers, stride=BLOCK), :]
+        parts = [ref[pl.ds(t * CAP + k, peers, stride=BLOCK), :] for t in range(PARTS)]
+        parts.append(jnp.where(group == k % PER_LINE, tails, 0.0))
+        for t, part in enumerate(parts):
+            hi, lo = pieces(part, 2)
+            hi_ref[k * peers : (k + 1) * peers, t * LANES : (t + 1) * LANES] = hi
+            lo_ref[k * peers : (k + 1) * peers, t * LANES : (t + 1) * LANES] = lo
+
+
+def edges_kernel(
+    block_ref, place_ref, neg_place_ref, row_place_ref, rel_hi_ref, rel_lo_ref,
+    out_ref, slots_hi, slots_lo, grad_hi, grad_lo,
+):
+    peers = block_ref.shape[0] // BLOCK
+    edges = place_ref.shape[0] // 2
+    total = neg_place_ref.shape[0]
+    kinds = rel_hi_ref.shape[0]
+    per_rel = edges // kinds
+    count = peers * CAP
+    main = PARTS * LANES
+    unpack(block_ref, slots_hi, slots_lo)
+
+    spot = jnp.concatenate([place_ref[...], neg_place_ref[...]], 0)
+    chosen = bits(iota((spot.shape[0], count), 1) == spot)
+    got = dot(chosen, slots_lo[...]) + dot(chosen, slots_hi[...])
+    got = jnp.concatenate([got[:, :main], spread(got[:, main:])], 1)
+
+    def keep(start, grad):
+        grad = jnp.concatenate([grad[:, :main], spread(grad[:, main:])], 1)
+        hi, lo = pieces(grad, 2)
+        grad_hi[start : start + grad.shape[0], :] = hi
+        grad_lo[start : start + grad.shape[0], :] = lo
+
+    negs = tuple(pieces(got[2 * edges :], 2))
+    shares = jnp.zeros((total, WIDE), F32)
+    for kind in range(kinds):
+        start = kind * per_rel
+        relation = rel_hi_ref[kind], rel_lo_ref[kind]
+        query = dot3(got[start : start + per_rel], relation)
+        tail = got[edges + start : edges + start + per_rel]
+        positive = jnp.sum(query * tail, 1, keepdims=True)
+        grad_pos = jax.nn.sigmoid(positive) - 1.0
+        keep(edges + start, grad_pos * query)
+        query = tuple(pieces(query, 2))
+        grad_neg = jax.nn.sigmoid(dot3(query, negs, 1, 1)) / total
+        grad_query = grad_pos * tail + dot3(grad_neg, negs)
+        keep(start, dot3(grad_query, relation, 1, 1))
+        grad_neg = jax.nn.sigmoid(dot3(negs, query, 1, 1)) / total
+        shares = shares + dot3(grad_neg, query)
+    keep(2 * edges, shares)
+
+    spot = row_place_ref[...]
+    chosen = bits(iota((count, spot.shape[1]), 0) == spot)
+    pack(dot(chosen, grad_lo[...]) + dot(chosen, grad_hi[...]), out_ref)
+
+
+def gathered(chosen, hi_ref, lo_ref):
+    got = dot(chosen, lo_ref[...]) + dot(chosen, hi_ref[...])
+    main = PARTS * LANES
+    return got[:, :main], spread(got[:, main:])
+
+
+def help_kernel(block_ref, code_ref, out_ref, hi_ref, lo_ref):
+    unpack(block_ref, hi_ref, lo_ref)
+    code = code_ref[...]
+    entry = shift_down(code, 11) - 1
+    here = iota((out_ref.shape[0], code.shape[1]), 0) == entry
+    row = jnp.where(here, (lax.bitwise_and(code, CODE - 1) - 1).astype(F32), -1.0)
+    row = jnp.max(row, 1, keepdims=True)
+    main, tails = gathered(bits(here), hi_ref, lo_ref)
+    tails = jnp.where(iota(tails.shape, 1) < TAIL, tails, row)
+    out_ref[...] = jnp.concatenate([main, tails], 1)
+
+
+def sum_kernel(block_ref, code_ref, out_ref, hi_ref, lo_ref):
+    unpack(block_ref, hi_ref, lo_ref)
+    row = lax.bitwise_and(code_ref[...], CODE - 1) - 1
+    chosen = bits(iota((out_ref.shape[0], row.shape[1]), 0) == row)
+    out_ref[...] = jnp.concatenate(gathered(chosen, hi_ref, lo_ref), 1)
+
+
+def update_kernel(
+    own_ref, first_ref, second_ref, third_ref, table_ref, state_ref, new_table_ref, new_state_ref
+):
+    width, owned = table_ref.shape
+    grad = own_ref[...]
+    for d, ref in enumerate((first_ref, second_ref, third_ref)):
+        rows = ref[...]
+        at = rows[:, WIDE - 1 :].astype(jnp.int32) - (d + 1) * owned
+        chosen = bits(iota((rows.shape[0], owned), 1) == at)
+        hi, lo = pieces(rows, 2)
+        grad = grad + (dot(chosen, lo, 0, 0) + dot(chosen, hi, 0, 0))
+    grad = grad.T[:width]
+    state = state_ref[...] + jnp.sum(grad * grad, 0, keepdims=True) / width
+    new_state_ref[...] = state
+    new_table_ref[...] = table_ref[...] - LEARN_RATE * grad / (jnp.sqrt(state) + EPSILON)
+
+
+def to_mates(x):
+    peers = lax.axis_size("grp")
+    return [
+        lax.ppermute(x, "grp", [(p, p ^ (d * DEPTH)) for p in range(peers)])
+        for d in range(1, COLUMN)
+    ]
+
+
+def exchange_blocks(blocks):
+    peers = lax.axis_size("grp")
+    return exchange(blocks.reshape(peers, BLOCK, 1, LANES)).reshape(blocks.shape)
+
+
+def compact_path(marks, blocks, codes, source, target, number, rel_hi, rel_lo, table, state):
+    peers = marks.shape[0] // 2
+    edges = source.shape[1]
+    width, owned = table.shape
+    count = peers * CAP
+    split = [pltpu.VMEM((count, WIDE), BF16)] * 2
+    blocks = exchange_blocks(blocks)
+    edge_place, neg_place = call(
+        functools.partial(place_kernel, number),
+        (shaped(1, 2 * edges, dtype=jnp.int32), shaped(peers * number, 1, dtype=jnp.int32)),
+    )(marks, source, target)
+    row_place = jnp.concatenate([edge_place, neg_place.reshape(1, -1)], 1)
+    grads = call(
+        edges_kernel,
+        shaped(*blocks.shape),
+        scratch_shapes=split + [pltpu.VMEM((row_place.shape[1], WIDE), BF16)] * 2,
+    )(blocks, edge_place.reshape(-1, 1), neg_place, row_place, rel_hi, rel_lo)
+    returned = exchange_blocks(grads)
+    codes = codes[:, :CAP].T.reshape(1, -1)
+    helped = call(help_kernel, shaped(2 * ROOM, WIDE), scratch_shapes=split)(returned, codes)
+    helped = to_mates(helped)
+    own = call(sum_kernel, shaped(owned, WIDE), scratch_shapes=split)(returned, codes)
+    return call(
+        update_kernel,
+        (shaped(width, owned), shaped(1, owned)),
+    )(own, *helped, table, state)
+
+
+def per_device(table, row_state, relations, touched, source, target, neg_slots):
+    peers, sent = touched.shape
+    owned, width = table.shape
+    number = neg_slots.shape[0]
+    across = table.T
+    source_row, target_row = source.reshape(1, -1), target.reshape(1, -1)
+    marks, bundle = call(
+        mark_kernel,
+        (shaped(2 * peers, LANES), shaped(width + sent, owned)),
+        in_specs=[SCALAR] + [VECTOR] * 4,
+        out_specs=(VECTOR, VECTOR),
+    )(neg_slots, source_row, target_row, touched.T, across)
+    marks = exchange(marks.reshape(peers, 2, 1, LANES)).reshape(2 * peers, LANES)
+    bundles = [bundle] + to_mates(bundle)
+    wide = jnp.pad(relations, ((0, 0), (0, WIDE - width), (0, WIDE - width)))
+    rel_hi = lax.reduce_precision(wide, 8, 7)
+    rel_lo = (wide - rel_hi).astype(BF16)
+    rel_hi = rel_hi.astype(BF16)
+    blocks, codes, crowded = call(
+        functools.partial(pack_kernel, number),
+        (
+            shaped(peers * BLOCK, LANES),
+            shaped(peers, LANES, dtype=jnp.int32),
+            shaped(1, dtype=jnp.int32),
+        ),
+        in_specs=[SCALAR] + [VECTOR] * (1 + COLUMN),
+        out_specs=(VECTOR, VECTOR, SCALAR),
+        scratch_shapes=[pltpu.VMEM((CAP * peers, COLUMN * owned), BF16)],
+    )(lax.axis_index("grp").reshape(1), marks, *bundles)
+    new_table, new_state = lax.cond(
+        crowded[0] > 0,
+        lambda: full_path(table, row_state, relations, touched, source, target, neg_slots),
+        lambda: compact_path(
+            marks, blocks, codes, source_row, target_row, number, rel_hi, rel_lo, across,
+            row_state.reshape(1, -1),
+        ),
+    )
+    return new_table.T, new_state.reshape(-1)
 
 
 def solution(mesh):

time: 475 us -> 289 us (0.61)
  waiting for transfers between devices: 310 us -> 188 us
  local copies, waits for them, and re-layouts: 59.1 us -> 7.38 us
  Pallas kernels: 0 us -> 35.7 us
  other arithmetic: 35.2 us -> 4.95 us
  matrix products: 14.4 us -> 0 us
    all_to_all x4 -> x3, waiting for transfers between devices: 310 us -> 187 us  [exchange(): lax.all_to_all(blocks, 'grp', split_axis=0, concat_axis=0, tiled=True)]
    pallas_call x0 -> x7, Pallas kernels: none -> 35.7 us  [the longest x1 15.5 us: compact_path(): call(edges_kernel, shaped(*blocks.shape), scratch_shapes=split + [pltpu.V...]
    scatter-add x4 -> x0, other arithmetic: 32.2 us -> none  [the longest x1 13.4 us: per_device(): jnp.zeros(table.shape, jnp.float32).at[touched.reshape(-1)].add(returned)]
    reshape x10 -> x2, local copies, waits for them, and re-layouts: 29.2 us -> 2.4 us  [the longest x1 1.73 us: compact_path(): edge_place.reshape(-1, 1)]
    gather x6 -> x0, local copies, waits for them, and re-layouts: 23.2 us -> none  [take_rows(): return jnp.take(rows, ids, axis=0, mode='clip')]
    all_to_all x4 -> x3, starting transfers between devices: 53.7 us -> 31 us  [exchange(): lax.all_to_all(blocks, 'grp', split_axis=0, concat_axis=0, tiled=True)]
    ppermute x0 -> x6, starting transfers between devices: none -> 19.6 us  [to_mates(): lax.ppermute(x, 'grp', [(p, p ^ d * DEPTH) for p in range(peers)])]
    dot_general x3 -> x0, matrix products: 8.76 us -> none  [the longest x1 4.77 us: per_device(): jnp.einsum('ked,kdf->kef', head.reshape(kinds, per_rel, width), relations...]
  transfers between devices with their start and end apart: 4 -> 9, of which waited for: 3 -> 4; matrix products, arithmetic and copies ran while one was open for 8% -> 3% of each run, Pallas kernels for 0% -> 2%
where the time goes in v5:
time: 289 us; the launch traced here: 288 us
  waiting for transfers between devices  188 us (65%)
  starting transfers between devices  50.6 us (18%)
  Pallas kernels  35.7 us (12%)
  local copies, waits for them, and re-layouts  7.38 us (3%)
  other arithmetic  4.95 us (2%)
    all_to_all x3, waiting for transfers between devices, exchange(): lax.all_to_all(blocks, 'grp', split_axis=0, concat_axis=0, tiled=True)  187 us
    all_to_all x3, starting transfers between devices, exchange(): lax.all_to_all(blocks, 'grp', split_axis=0, concat_axis=0, tiled=True)  31 us
    ppermute x6, starting transfers between devices, to_mates(): lax.ppermute(x, 'grp', [(p, p ^ d * DEPTH) for p in range(peers)])  19.6 us
    pallas_call x1, Pallas kernels, compact_path(): call(edges_kernel, shaped(*blocks.shape), scratch_shapes=split + [pltpu.V...  15.5 us
    pallas_call x1, Pallas kernels, per_device(): call(functools.partial(pack_kernel, number), (shaped(peers * BLOCK, LANES...  6.43 us
  transfers between devices with their start and end apart: 9, of which 4 were waited for; matrix products, arithmetic and copies ran while one was open for 3% of the time, Pallas kernels for 2%

profile of v5, /device:TPU:6, one launch (start us, length us, event | category | flops | bytes accessed | tf_op | source)
XLA Modules:
  0.0 288.4 jit_solution(7191344082844430589)
XLA Ops:
  0.6 0.0 copy-start.13
  0.6 0.0 copy-start.12
  0.7 0.0 copy-start.3
  0.7 0.0 copy-start.11
  0.7 0.0 copy-start.14
  0.7 2.1 shard_map.86
  2.8 4.9 %collective-permute-start.5 = (f32[432,256]{1,0:T(8,128)}, f32[432,256]{1,0:T(8,128)S(1)}, u32[]{:S(2)}, u32[]{:S(2)}) collective-permute-start(f32[432,256]{1,0:T(8,128)} %get-tuple-element.65.own_ref), channel_id=1, source_target_pairs={{0,384},{8,392},{16,400},{24,408},{32,416},{40,424},{48,432},{56,4... | collective-permute-start | bytes 1327112 | tf_op jit(solution)/shard_map/ppermute | solution.py:460
  7.7 2.5 collective-permute-start.4
  10.2 2.4 collective-permute-start.3
  12.6 18.7 %all-to-all-start.6 = ((f32[64,2,1,128]{3,1,2,0:T(2,128)}), f32[64,2,1,128]{3,1,2,0:T(2,128)S(1)}, u32[]{:S(2)}, u32[]{:S(2)}) async-start(f32[64,2,1,128]{3,1,2,0:T(2,128)} %bitcast.60), calls=%async_computation.6 | async-start | bytes 131072 | tf_op jit(solution)/shard_map/all_to_all | solution.py:20
  31.3 2.7 fusion.15
  34.1 12.0 %all-to-all-done.6 = f32[64,2,1,128]{3,1,2,0:T(2,128)S(1)} async-done(((f32[64,2,1,128]{3,1,2,0:T(2,128)}), f32[64,2,1,128]{3,1,2,0:T(2,128)S(1)}, u32[]{:S(2)}, u32[]{:S(2)}) %all-to-all-start.6) | async-done | bytes 65568 | tf_op jit(solution)/shard_map/all_to_all | solution.py:20
  46.1 0.0 collective-permute-done.5.third_ref
  46.1 0.0 collective-permute-done.4.second_ref
  46.1 0.0 copy-start.6
  46.1 0.0 collective-permute-done.3.first_ref
  46.1 0.0 copy-start.7
  46.1 0.8 copy-done.5
  46.9 0.1 copy-done.6
  47.0 0.1 copy-done.7
  47.1 6.4 %shard_map.87 = (f32[3840,128]{1,0:T(8,128)}, s32[64,128]{1,0:T(8,128)S(1)}, s32[1]{0:T(128)}) custom-call(s32[1]{0:T(128)} %bitcast.13.me_ref, f32[128,128]{1,0:T(8,128)S(1)} %bitcast.58, f32[432,256]{1,0:T(8,128)} %get-tuple-element.65.own_ref, f32[432,256]{1,0:T(8,128)} %copy-done.7, f32[432,256]{1,0:T(8,128)} %copy-done.6, f32[432,256]{1,0:T(8,128)} %copy-done.5), custom_call_target="tpu_custom_call" | custom-call | tf_op jit(solution)/shard_map/pallas_call | solution.py:516
  54.2 0.0 copy-done.13
  54.3 233.6 %conditional.1 = (f32[256]{0:T(256)S(1)}, f32[400,256]{1,0:T(8,128)}) conditional(s32[]{:T(128)} %bitcast.21, (f32[3840,128]{1,0:T(8,128)}, f32[128,128]{1,0:T(8,128)S(1)}, s32[1,512]{1,0:T(1,128)S(1)}, s32[1,512]{1,0:T(1,128)S(1)}, bf16[2,512,512]{2,1,0:T(8,128)(2,1)}, /*index=5*/bf16[2,512,512]{2,1,0:T(8,128)(2,1)S(1)}, s32[64,128]{1,0:T(8,128)S(1)}, ...), branch_computations={%region_0.1_spmd, %region_1.9_spmd} | conditional | flops 2912907008 | bytes 98542304 | solution.py:527
  54.3 4.9 %all-to-all-start = ((f32[64,60,1,128]{3,2,1,0:T(1,128)}), f32[64,60,1,128]{3,2,1,0:T(1,128)S(1)}, u32[]{:S(2)}, u32[]{:S(2)}) async-start(f32[64,60,1,128]{3,2,1,0:T(1,128)} %bitcast.56), calls=%async_computation | async-start | bytes 3932160 | tf_op jit(solution)/shard_map/cond/branch_0_fun/all_to_all | solution.py:20
  59.2 2.0 branch_0_fun.5
  61.1 1.7 copy.36.place_ref
  62.9 0.9 reduce.1
  63.8 1.3 pad_add_fusion.row_place_ref
  65.1 84.5 %all-to-all-done = f32[64,60,1,128]{3,2,1,0:T(1,128)S(1)} async-done(((f32[64,60,1,128]{3,2,1,0:T(1,128)}), f32[64,60,1,128]{3,2,1,0:T(1,128)S(1)}, u32[]{:S(2)}, u32[]{:S(2)}) %all-to-all-start) | async-done | bytes 1966112 | tf_op jit(solution)/shard_map/cond/branch_0_fun/all_to_all | solution.py:20
  149.5 1.3 copy-done.2
  150.8 15.5 %branch_0_fun.6 = f32[3840,128]{1,0:T(8,128)} custom-call(f32[3840,128]{1,0:T(8,128)} %bitcast.46, s32[1024,1]{1,0:T(8,128)} %copy.36.place_ref, s32[128,1]{1,0:T(8,128)} %get-tuple-element.40.neg_place_ref, s32[1,1152]{1,0:T(1,128)} %pad_add_fusion.row_place_ref, bf16[2,512,512]{2,1,0:T(8,128)(2,1)} %get-tuple-element.41.rel_hi_ref, ...), custom_call_target="tpu_custom_call" | custom-call | tf_op jit(solution)/shard_map/cond/branch_0_fun/pallas_call | solution.py:482
  166.3 7.4 %all-to-all-start.1 = ((f32[64,60,1,128]{3,2,1,0:T(1,128)}), f32[64,60,1,128]{3,2,1,0:T(1,128)S(1)}, u32[]{:S(2)}, u32[]{:S(2)}) async-start(f32[64,60,1,128]{3,2,1,0:T(1,128)} %bitcast.47), calls=%async_computation.1 | async-start | bytes 3932160 | tf_op jit(solution)/shard_map/cond/branch_0_fun/all_to_all | solution.py:20
  173.7 0.1 copy.51
  173.8 0.7 reshape.122.code_ref
  174.5 90.7 %all-to-all-done.1 = f32[64,60,1,128]{3,2,1,0:T(1,128)S(1)} async-done(((f32[64,60,1,128]{3,2,1,0:T(1,128)}), f32[64,60,1,128]{3,2,1,0:T(1,128)S(1)}, u32[]{:S(2)}, u32[]{:S(2)}) %all-to-all-start.1) | async-done | bytes 1966112 | tf_op jit(solution)/shard_map/cond/branch_0_fun/all_to_all | solution.py:20
  265.2 1.3 copy-done
  266.6 3.4 %branch_0_fun.8 = f32[64,512]{1,0:T(8,128)} custom-call(f32[3840,128]{1,0:T(8,128)} %bitcast.43, s32[1,1216]{1,0:T(1,128)} %reshape.122.code_ref), custom_call_target="tpu_custom_call" | custom-call | tf_op jit(solution)/shard_map/cond/branch_0_fun/pallas_call | solution.py:489
  269.9 4.8 %collective-permute-start.2 = (f32[64,512]{1,0:T(8,128)}, f32[64,512]{1,0:T(8,128)S(1)}, u32[]{:S(2)}, u32[]{:S(2)}) collective-permute-start(f32[64,512]{1,0:T(8,128)} %branch_0_fun.8), channel_id=1, source_target_pairs={{0,384},{8,392},{16,400},{24,408},{32,416},{40,424},{48,432},{56,4... | collective-permute-start | bytes 393224 | tf_op jit(solution)/shard_map/cond/branch_0_fun/ppermute | solution.py:460
  274.7 2.6 collective-permute-start.1
  277.3 2.5 collective-permute-start
  279.8 3.6 %branch_0_fun.7.own_ref = f32[256,512]{1,0:T(8,128)} custom-call(f32[3840,128]{1,0:T(8,128)} %bitcast.44, s32[1,1216]{1,0:T(1,128)} %reshape.122.code_ref), custom_call_target="tpu_custom_call" | custom-call | tf_op jit(solution)/shard_map/cond/branch_0_fun/pallas_call | solution.py:491
  283.3 0.0 collective-permute-done.2.third_ref
  283.3 0.0 collective-permute-done.1.second_ref
  283.3 1.0 collective-permute-done.first_ref
  284.4 0.0 copy-done.8
  284.4 0.6 copy-done.10
  285.0 2.8 branch_0_fun.9
  287.8 0.6 copy-done.18
  (13 shorter events, 0.0 us)
Async XLA Ops:
  0.6 53.6 %copy-start.13 = (s32[512]{0:T(512)S(1)}, s32[512]{0:T(512)}, u32[]{:S(2)}) copy-start(s32[512]{0:T(512)} %param.14) | copy-start | bytes 6148
  0.6 53.6 %copy-start.12 = (s32[512]{0:T(512)S(1)}, s32[512]{0:T(512)}, u32[]{:S(2)}) copy-start(s32[512]{0:T(512)} %param.13) | copy-start | bytes 6148
  0.7 53.6 %copy-start.3 = (f32[256,400]{0,1:T(8,128)S(1)}, f32[256,400]{0,1:T(8,128)}, u32[]{:S(2)}) copy-start(f32[256,400]{0,1:T(8,128)} %param.9) | copy-start | bytes 1228804
  0.7 53.6 %copy-start.11 = (s32[64,32]{0,1:T(8,128)S(1)}, s32[64,32]{0,1:T(8,128)}, u32[]{:S(2)}) copy-start(s32[64,32]{0,1:T(8,128)} %param.12) | copy-start | bytes 24580
  0.7 53.6 %copy-start.14 = (f32[256]{0:T(256)S(1)}, f32[256]{0:T(256)}, u32[]{:S(2)}) copy-start(f32[256]{0:T(256)} %param.10) | copy-start | bytes 3076
  2.8 43.3 %collective-permute-start.5 = (f32[432,256]{1,0:T(8,128)}, f32[432,256]{1,0:T(8,128)S(1)}, u32[]{:S(2)}, u32[]{:S(2)}) collective-permute-start(f32[432,256]{1,0:T(8,128)} %get-tuple-element.65.own_ref), channel_id=1, source_target_pairs={{0,384},{8,392},{16,400},{24,408},{32,416},{40,424},{48,432},{56,4... | collective-permute-start | bytes 1327112 | tf_op jit(solution)/shard_map/ppermute | solution.py:460
  7.7 38.4 %collective-permute-start.4 = (f32[432,256]{1,0:T(8,128)}, f32[432,256]{1,0:T(8,128)S(1)}, u32[]{:S(2)}, u32[]{:S(2)}) collective-permute-start(f32[432,256]{1,0:T(8,128)} %get-tuple-element.65.own_ref), channel_id=1, source_target_pairs={{0,256},{8,264},{16,272},{24,280},{32,288},{40,296},{48,304},{56,3... | collective-permute-start | bytes 1327112 | tf_op jit(solution)/shard_map/ppermute | solution.py:460
  10.2 35.9 %collective-permute-start.3 = (f32[432,256]{1,0:T(8,128)}, f32[432,256]{1,0:T(8,128)S(1)}, u32[]{:S(2)}, u32[]{:S(2)}) collective-permute-start(f32[432,256]{1,0:T(8,128)} %get-tuple-element.65.own_ref), channel_id=1, source_target_pairs={{0,128},{8,136},{16,144},{24,152},{32,160},{40,168},{48,176},{56,1... | collective-permute-start | bytes 1327112 | tf_op jit(solution)/shard_map/ppermute | solution.py:460
  12.6 33.5 %all-to-all-start.6 = ((f32[64,2,1,128]{3,1,2,0:T(2,128)}), f32[64,2,1,128]{3,1,2,0:T(2,128)S(1)}, u32[]{:S(2)}, u32[]{:S(2)}) async-start(f32[64,2,1,128]{3,1,2,0:T(2,128)} %bitcast.60), calls=%async_computation.6 | async-start | bytes 131072 | tf_op jit(solution)/shard_map/all_to_all | solution.py:20
  46.1 0.8 copy-start.5
  46.1 0.9 copy-start.6
  46.1 1.0 copy-start.7
  54.3 95.3 %all-to-all-start = ((f32[64,60,1,128]{3,2,1,0:T(1,128)}), f32[64,60,1,128]{3,2,1,0:T(1,128)S(1)}, u32[]{:S(2)}, u32[]{:S(2)}) async-start(f32[64,60,1,128]{3,2,1,0:T(1,128)} %bitcast.56), calls=%async_computation | async-start | bytes 3932160 | tf_op jit(solution)/shard_map/cond/branch_0_fun/all_to_all | solution.py:20
  149.5 1.3 copy-start.2
  166.3 98.9 %all-to-all-start.1 = ((f32[64,60,1,128]{3,2,1,0:T(1,128)}), f32[64,60,1,128]{3,2,1,0:T(1,128)S(1)}, u32[]{:S(2)}, u32[]{:S(2)}) async-start(f32[64,60,1,128]{3,2,1,0:T(1,128)} %bitcast.47), calls=%async_computation.1 | async-start | bytes 3932160 | tf_op jit(solution)/shard_map/cond/branch_0_fun/all_to_all | solution.py:20
  265.2 1.3 copy-start
  269.9 13.4 %collective-permute-start.2 = (f32[64,512]{1,0:T(8,128)}, f32[64,512]{1,0:T(8,128)S(1)}, u32[]{:S(2)}, u32[]{:S(2)}) collective-permute-start(f32[64,512]{1,0:T(8,128)} %branch_0_fun.8), channel_id=1, source_target_pairs={{0,384},{8,392},{16,400},{24,408},{32,416},{40,424},{48,432},{56,4... | collective-permute-start | bytes 393224 | tf_op jit(solution)/shard_map/cond/branch_0_fun/ppermute | solution.py:460
  274.7 8.6 %collective-permute-start.1 = (f32[64,512]{1,0:T(8,128)}, f32[64,512]{1,0:T(8,128)S(1)}, u32[]{:S(2)}, u32[]{:S(2)}) collective-permute-start(f32[64,512]{1,0:T(8,128)} %branch_0_fun.8), channel_id=1, source_target_pairs={{0,256},{8,264},{16,272},{24,280},{32,288},{40,296},{48,304},{56,3... | collective-permute-start | bytes 393224 | tf_op jit(solution)/shard_map/cond/branch_0_fun/ppermute | solution.py:460
  277.3 7.1 %collective-permute-start = (f32[64,512]{1,0:T(8,128)}, f32[64,512]{1,0:T(8,128)S(1)}, u32[]{:S(2)}, u32[]{:S(2)}) collective-permute-start(f32[64,512]{1,0:T(8,128)} %branch_0_fun.8), channel_id=1, source_target_pairs={{0,128},{8,136},{16,144},{24,152},{32,160},{40,168},{48,176},{56,1... | collective-permute-start | bytes 393224 | tf_op jit(solution)/shard_map/cond/branch_0_fun/ppermute | solution.py:460
  283.3 1.0 copy-start.8
  283.3 1.0 copy-start.9
  284.4 0.7 copy-start.10
  287.8 0.6 copy-start.18

commit v6 on v5

--- a/solution.py
+++ b/solution.py
@@ -76,7 +76,8 @@
 PER_LINE = LANES // TAIL
 LINES = PARTS * CAP
 BLOCK = LINES + -(-CAP // PER_LINE)
-WIDE = (PARTS + 1) * LANES
+MAIN = PARTS * LANES
+WIDE = MAIN + LANES
 COLUMN = 4
 DEPTH = 16
 SENT = 32
@@ -123,6 +124,15 @@
     b_hi, b_lo = b if isinstance(b, tuple) else pieces(b, 2)
     small = dot(a_lo, b_hi, a_dim, b_dim) + dot(a_hi, b_lo, a_dim, b_dim)
     return small + dot(a_hi, b_hi, a_dim, b_dim)
+
+
+def halves(hi, lo):
+    lane = iota(hi.shape, 1)
+    return jnp.where(lane < LANES // 2, hi.astype(F32), lo.astype(F32)).astype(BF16)
+
+
+def fold(x):
+    return x + pltpu.roll(x, LANES // 2, 1)
 
 
 def spread(x):
@@ -277,20 +287,46 @@
     neg_entry = dot(neg_marks.astype(BF16), upto)
     neg_codes = neg_rows + CODE * jnp.where((neg_place >= 0.0) & ~own, neg_entry, 0.0)
 
-    spot = iota((peers, len(refs) * owned), 1)
+    mates = len(refs) - 1
+    column = iota((ROOM, LANES), 0)
+    of_slots = jnp.zeros((ROOM, LANES), F32)
+    for e in range(ROOM):
+        row = jnp.sum(jnp.where((helped > 0.0) & (entry == e + 1.0), touched, 0.0), 0, keepdims=True)
+        of_slots = jnp.where(column == e, row, of_slots)
+    of_negs = jnp.where((neg_entry[:1] == column + 1.0) & (neg_marks[:1] > 0.0), neg_rows[:1], 0.0)
+    row = jnp.sum(jnp.concatenate([of_negs, of_slots], 0), 1, keepdims=True).astype(jnp.int32)
+    from_mates = bits(iota((2 * ROOM, mates * owned), 1) == row - (owned + 1))
+
+    spot = iota((peers, owned + LANES), 1)
     out = jnp.zeros(marks.shape, jnp.int32)
     for k in range(CAP):
         code = jnp.where(place == k, codes, 0.0) + jnp.where(neg_place == k, neg_codes, 0.0)
         code = jnp.sum(code, 1, keepdims=True).astype(jnp.int32)
         out = jnp.where(lane == k, code, out)
-        onehot[k * peers : (k + 1) * peers, :] = bits(spot == lax.bitwise_and(code, CODE - 1) - 1)
+        helping = shift_down(code, 11)
+        own_row = lax.bitwise_and(code, CODE - 1) - 1
+        at = jnp.where(helping > 0, owned - 1 + helping, own_row)
+        onehot[k * peers : (k + 1) * peers, :] = bits(spot == at)
     codes_ref[...] = out
 
-    main = PARTS * LANES
-    table = jnp.concatenate([ref[:width] for ref in refs], 1)
-    wide = jnp.concatenate([table[:main]] + [table[main:]] * PER_LINE, 0)
-    wide = pieces(wide, 2)
-    pack(dot(onehot[...], wide[1], 1, 1) + dot(onehot[...], wide[0], 1, 1), out_ref)
+    hi, lo = pieces(jnp.concatenate([ref[:width] for ref in refs], 1), 2)
+    tails = [hi[MAIN:]] * (PER_LINE // 2) + [lo[MAIN:]] * (PER_LINE // 2)
+    hi, lo = jnp.concatenate([hi[:MAIN]] + tails, 0), lo[:MAIN]
+
+    def joined(of_hi, of_lo):
+        return jnp.concatenate([of_hi[:, :MAIN] + of_lo, fold(of_hi[:, MAIN:])], 1)
+
+    held = joined(dot(from_mates, hi[:, owned:], 1, 1), dot(from_mates, lo[:, owned:], 1, 1))
+    held = jnp.concatenate([held, jnp.zeros((LANES - 2 * ROOM, WIDE), F32)], 0)
+    held_hi, held_lo = pieces(held, 2)
+    held_hi = jnp.concatenate([held_hi[:, :MAIN], halves(held_hi[:, MAIN:], held_lo[:, MAIN:])], 1)
+    held_lo = held_lo[:, :MAIN]
+    own, other = onehot[:, :owned], onehot[:, owned:]
+    got = joined(
+        dot(own, hi[:, :owned], 1, 1) + dot(other, held_hi),
+        dot(own, lo[:, :owned], 1, 1) + dot(other, held_lo),
+    )
+    pack(got, out_ref)
 
 
 def place_kernel(number, marks_ref, source_ref, target_ref, edge_ref, neg_ref):
@@ -356,13 +392,20 @@
     peers = ref.shape[0] // BLOCK
     group = iota((peers, LANES), 1) // TAIL
     for k in range(CAP):
+        span = slice(k * peers, (k + 1) * peers)
+        for t in range(PARTS):
+            hi, lo = pieces(ref[pl.ds(t * CAP + k, peers, stride=BLOCK), :], 2)
+            hi_ref[span, t * LANES : (t + 1) * LANES] = hi
+            lo_ref[span, t * LANES : (t + 1) * LANES] = lo
         tails = ref[pl.ds(LINES + k // PER_LINE, peers, stride=BLOCK), :]
-        parts = [ref[pl.ds(t * CAP + k, peers, stride=BLOCK), :] for t in range(PARTS)]
-        parts.append(jnp.where(group == k % PER_LINE, tails, 0.0))
-        for t, part in enumerate(parts):
-            hi, lo = pieces(part, 2)
-            hi_ref[k * peers : (k + 1) * peers, t * LANES : (t + 1) * LANES] = hi
-            lo_ref[k * peers : (k + 1) * peers, t * LANES : (t + 1) * LANES] = lo
+        hi, lo = pieces(jnp.where(group == k % PER_LINE, tails, 0.0), 2)
+        both = hi.astype(F32) + pltpu.roll(lo.astype(F32), LANES // 2, 1)
+        hi_ref[span, MAIN:] = both.astype(BF16)
+
+
+def gathered(chosen, hi_ref, lo_ref):
+    of_hi = dot(chosen, hi_ref[...])
+    return of_hi[:, :MAIN] + dot(chosen, lo_ref[...]), spread(of_hi[:, MAIN:])
 
 
 def edges_kernel(
@@ -375,19 +418,16 @@
     kinds = rel_hi_ref.shape[0]
     per_rel = edges // kinds
     count = peers * CAP
-    main = PARTS * LANES
     unpack(block_ref, slots_hi, slots_lo)
 
     spot = jnp.concatenate([place_ref[...], neg_place_ref[...]], 0)
     chosen = bits(iota((spot.shape[0], count), 1) == spot)
-    got = dot(chosen, slots_lo[...]) + dot(chosen, slots_hi[...])
-    got = jnp.concatenate([got[:, :main], spread(got[:, main:])], 1)
+    got = jnp.concatenate(gathered(chosen, slots_hi, slots_lo), 1)
 
     def keep(start, grad):
-        grad = jnp.concatenate([grad[:, :main], spread(grad[:, main:])], 1)
-        hi, lo = pieces(grad, 2)
-        grad_hi[start : start + grad.shape[0], :] = hi
-        grad_lo[start : start + grad.shape[0], :] = lo
+        span = slice(start, start + grad.shape[0])
+        grad_hi[span, :MAIN], grad_lo[span, :] = pieces(grad[:, :MAIN], 2)
+        grad_hi[span, MAIN:] = halves(*pieces(spread(grad[:, MAIN:]), 2))
 
     negs = tuple(pieces(got[2 * edges :], 2))
     shares = jnp.zeros((total, WIDE), F32)
@@ -409,25 +449,22 @@
 
     spot = row_place_ref[...]
     chosen = bits(iota((count, spot.shape[1]), 0) == spot)
-    pack(dot(chosen, grad_lo[...]) + dot(chosen, grad_hi[...]), out_ref)
-
-
-def gathered(chosen, hi_ref, lo_ref):
-    got = dot(chosen, lo_ref[...]) + dot(chosen, hi_ref[...])
-    main = PARTS * LANES
-    return got[:, :main], spread(got[:, main:])
+    of_hi = dot(chosen, grad_hi[...])
+    of_main = of_hi[:, :MAIN] + dot(chosen, grad_lo[...])
+    pack(jnp.concatenate([of_main, fold(of_hi[:, MAIN:])], 1), out_ref)
 
 
 def help_kernel(block_ref, code_ref, out_ref, hi_ref, lo_ref):
     unpack(block_ref, hi_ref, lo_ref)
     code = code_ref[...]
     entry = shift_down(code, 11) - 1
-    here = iota((out_ref.shape[0], code.shape[1]), 0) == entry
+    here = iota((out_ref.shape[1], code.shape[1]), 0) == entry
     row = jnp.where(here, (lax.bitwise_and(code, CODE - 1) - 1).astype(F32), -1.0)
     row = jnp.max(row, 1, keepdims=True)
     main, tails = gathered(bits(here), hi_ref, lo_ref)
     tails = jnp.where(iota(tails.shape, 1) < TAIL, tails, row)
-    out_ref[...] = jnp.concatenate([main, tails], 1)
+    for y in range(out_ref.shape[0]):
+        out_ref[y] = jnp.concatenate([main, tails], 1)
 
 
 def sum_kernel(block_ref, code_ref, out_ref, hi_ref, lo_ref):
@@ -437,17 +474,16 @@
     out_ref[...] = jnp.concatenate(gathered(chosen, hi_ref, lo_ref), 1)
 
 
-def update_kernel(
-    own_ref, first_ref, second_ref, third_ref, table_ref, state_ref, new_table_ref, new_state_ref
-):
+def update_kernel(me_ref, own_ref, lists_ref, table_ref, state_ref, new_table_ref, new_state_ref):
     width, owned = table_ref.shape
-    grad = own_ref[...]
-    for d, ref in enumerate((first_ref, second_ref, third_ref)):
-        rows = ref[...]
-        at = rows[:, WIDE - 1 :].astype(jnp.int32) - (d + 1) * owned
-        chosen = bits(iota((rows.shape[0], owned), 1) == at)
-        hi, lo = pieces(rows, 2)
-        grad = grad + (dot(chosen, lo, 0, 0) + dot(chosen, hi, 0, 0))
+    rows = lists_ref[...].reshape(-1, WIDE)
+    up = lax.shift_right_logical(me_ref[0], jnp.int32(4))
+    mate = iota((rows.shape[0], 1), 0) // (2 * ROOM)
+    first = lax.bitwise_xor(mate, jnp.broadcast_to(up, mate.shape)) * owned
+    at = rows[:, WIDE - 1 :].astype(jnp.int32) - first
+    chosen = bits(iota((rows.shape[0], owned), 1) == at)
+    hi, lo = pieces(rows, 2)
+    grad = own_ref[...] + (dot(chosen, lo, 0, 0) + dot(chosen, hi, 0, 0))
     grad = grad.T[:width]
     state = state_ref[...] + jnp.sum(grad * grad, 0, keepdims=True) / width
     new_state_ref[...] = state
@@ -467,12 +503,12 @@
     return exchange(blocks.reshape(peers, BLOCK, 1, LANES)).reshape(blocks.shape)
 
 
-def compact_path(marks, blocks, codes, source, target, number, rel_hi, rel_lo, table, state):
+def compact_path(me, marks, blocks, codes, source, target, number, rel_hi, rel_lo, table, state):
     peers = marks.shape[0] // 2
     edges = source.shape[1]
     width, owned = table.shape
     count = peers * CAP
-    split = [pltpu.VMEM((count, WIDE), BF16)] * 2
+    split = [pltpu.VMEM((count, WIDE), BF16), pltpu.VMEM((count, MAIN), BF16)]
     blocks = exchange_blocks(blocks)
     edge_place, neg_place = call(
         functools.partial(place_kernel, number),
@@ -482,17 +518,22 @@
     grads = call(
         edges_kernel,
         shaped(*blocks.shape),
-        scratch_shapes=split + [pltpu.VMEM((row_place.shape[1], WIDE), BF16)] * 2,
+        scratch_shapes=split
+        + [pltpu.VMEM((row_place.shape[1], size), BF16) for size in (WIDE, MAIN)],
     )(blocks, edge_place.reshape(-1, 1), neg_place, row_place, rel_hi, rel_lo)
     returned = exchange_blocks(grads)
     codes = codes[:, :CAP].T.reshape(1, -1)
-    helped = call(help_kernel, shaped(2 * ROOM, WIDE), scratch_shapes=split)(returned, codes)
-    helped = to_mates(helped)
+    lists = call(help_kernel, shaped(COLUMN, 2 * ROOM, WIDE), scratch_shapes=split)(returned, codes)
+    lists = lax.all_to_all(
+        lists, "grp", 0, 0, tiled=True,
+        axis_index_groups=[list(range(z, peers, DEPTH)) for z in range(DEPTH)],
+    )
     own = call(sum_kernel, shaped(owned, WIDE), scratch_shapes=split)(returned, codes)
     return call(
         update_kernel,
         (shaped(width, owned), shaped(1, owned)),
-    )(own, *helped, table, state)
+        in_specs=[SCALAR] + [VECTOR] * 4,
+    )(me, own, lists, table, state)
 
 
 def per_device(table, row_state, relations, touched, source, target, neg_slots):
@@ -513,6 +554,7 @@
     rel_hi = lax.reduce_precision(wide, 8, 7)
     rel_lo = (wide - rel_hi).astype(BF16)
     rel_hi = rel_hi.astype(BF16)
+    me = lax.axis_index("grp").reshape(1)
     blocks, codes, crowded = call(
         functools.partial(pack_kernel, number),
         (
@@ -522,13 +564,13 @@
         ),
         in_specs=[SCALAR] + [VECTOR] * (1 + COLUMN),
         out_specs=(VECTOR, VECTOR, SCALAR),
-        scratch_shapes=[pltpu.VMEM((CAP * peers, COLUMN * owned), BF16)],
-    )(lax.axis_index("grp").reshape(1), marks, *bundles)
+        scratch_shapes=[pltpu.VMEM((CAP * peers, owned + LANES), BF16)],
+    )(me, marks, *bundles)
     new_table, new_state = lax.cond(
         crowded[0] > 0,
         lambda: full_path(table, row_state, relations, touched, source, target, neg_slots),
         lambda: compact_path(
-            marks, blocks, codes, source_row, target_row, number, rel_hi, rel_lo, across,
+            me, marks, blocks, codes, source_row, target_row, number, rel_hi, rel_lo, across,
             row_state.reshape(1, -1),
         ),
     )

time: 289 us -> 286 us (0.990)
  starting transfers between devices: 50.6 us -> 45.7 us
  waiting for transfers between devices: 188 us -> 191 us
    ppermute x6 -> x3, starting transfers between devices: 19.6 us -> 9.81 us  [to_mates(): lax.ppermute(x, 'grp', [(p, p ^ d * DEPTH) for p in range(peers)])]
    all_to_all x0 -> x1, waiting for transfers between devices: none -> 4.67 us  [compact_path(): lax.all_to_all(lists, 'grp', 0, 0, tiled=True, axis_index_groups=[list(ra...]
    all_to_all x0 -> x1, starting transfers between devices: none -> 4.64 us  [compact_path(): lax.all_to_all(lists, 'grp', 0, 0, tiled=True, axis_index_groups=[list(ra...]
  transfers between devices with their start and end apart: 9 -> 7, of which waited for: 4 -> 4; matrix products, arithmetic and copies ran while one was open for 3% -> 3% of each run, Pallas kernels for 2% -> 2%
where the time goes in v6:
time: 286 us; the launch traced here: 285 us
  waiting for transfers between devices  191 us (67%)
  starting transfers between devices  45.7 us (16%)
  Pallas kernels  34.3 us (12%)
  local copies, waits for them, and re-layouts  7.5 us (3%)
  other arithmetic  4.95 us (2%)
    all_to_all x3, waiting for transfers between devices, exchange(): lax.all_to_all(blocks, 'grp', split_axis=0, concat_axis=0, tiled=True)  187 us
    all_to_all x3, starting transfers between devices, exchange(): lax.all_to_all(blocks, 'grp', split_axis=0, concat_axis=0, tiled=True)  31.2 us
    pallas_call x1, Pallas kernels, compact_path(): call(edges_kernel, shaped(*blocks.shape), scratch_shapes=split + [pltpu.V...  15 us
    ppermute x3, starting transfers between devices, to_mates(): lax.ppermute(x, 'grp', [(p, p ^ d * DEPTH) for p in range(peers)])  9.81 us
    pallas_call x1, Pallas kernels, per_device(): call(functools.partial(pack_kernel, number), (shaped(peers * BLOCK, LANES...  5.95 us
  transfers between devices with their start and end apart: 7, of which 4 were waited for; matrix products, arithmetic and copies ran while one was open for 3% of the time, Pallas kernels for 2%

profile of v6, /device:TPU:6, one launch (start us, length us, event | category | flops | bytes accessed | tf_op | source)
XLA Modules:
  0.0 285.3 jit_solution(6324070880582199960)
XLA Ops:
  0.6 0.0 copy-start.14
  0.6 0.0 copy-start.11
  0.7 0.0 copy-start.3
  0.7 0.0 copy-start.10
  0.7 0.0 copy-start.17
  0.7 2.1 shard_map.86
  2.8 4.9 %collective-permute-start.2 = (f32[432,256]{1,0:T(8,128)}, f32[432,256]{1,0:T(8,128)S(1)}, u32[]{:S(2)}, u32[]{:S(2)}) collective-permute-start(f32[432,256]{1,0:T(8,128)} %get-tuple-element.68.own_ref), channel_id=1, source_target_pairs={{0,384},{8,392},{16,400},{24,408},{32,416},{40,424},{48,432},{56,4... | collective-permute-start | bytes 1327112 | tf_op jit(solution)/shard_map/ppermute | solution.py:496
  7.7 2.5 collective-permute-start.1
  10.2 2.4 collective-permute-start
  12.6 18.7 %all-to-all-start.7 = ((f32[64,2,1,128]{3,1,2,0:T(2,128)}), f32[64,2,1,128]{3,1,2,0:T(2,128)S(1)}, u32[]{:S(2)}, u32[]{:S(2)}) async-start(f32[64,2,1,128]{3,1,2,0:T(2,128)} %bitcast.60), calls=%async_computation.7 | async-start | bytes 131072 | tf_op jit(solution)/shard_map/all_to_all | solution.py:20
  31.3 2.7 fusion.15
  34.1 12.0 %all-to-all-done.7 = f32[64,2,1,128]{3,1,2,0:T(2,128)S(1)} async-done(((f32[64,2,1,128]{3,1,2,0:T(2,128)}), f32[64,2,1,128]{3,1,2,0:T(2,128)S(1)}, u32[]{:S(2)}, u32[]{:S(2)}) %all-to-all-start.7) | async-done | bytes 65568 | tf_op jit(solution)/shard_map/all_to_all | solution.py:20
  46.0 0.0 collective-permute-done.2.third_ref
  46.0 0.0 copy-start.7
  46.1 0.0 collective-permute-done.1.second_ref
  46.1 0.0 copy-start.8
  46.1 0.0 collective-permute-done.first_ref
  46.1 0.0 copy-start.9
  46.1 0.7 copy-done.7
  46.8 0.1 copy-done.8
  47.0 0.2 copy-done.9
  47.1 5.9 %shard_map.87 = (f32[3840,128]{1,0:T(8,128)}, s32[64,128]{1,0:T(8,128)S(1)}, s32[1]{0:T(128)}) custom-call(s32[1]{0:T(128)} %bitcast.13.me_ref, f32[128,128]{1,0:T(8,128)S(1)} %bitcast.58, f32[432,256]{1,0:T(8,128)} %get-tuple-element.68.own_ref, f32[432,256]{1,0:T(8,128)} %copy-done.9, f32[432,256]{1,0:T(8,128)} %copy-done.8, f32[432,256]{1,0:T(8,128)} %copy-done.7), custom_call_target="tpu_custom_call" | custom-call | tf_op jit(solution)/shard_map/pallas_call | solution.py:558
  53.7 0.0 copy-done.14
  53.7 0.0 copy-done.11
  53.8 0.0 copy-done.3
  53.8 0.0 copy-done.10
  53.8 0.0 copy-done.17
  53.8 230.9 %conditional.1 = (f32[256]{0:T(256)S(1)}, f32[400,256]{1,0:T(8,128)}) conditional(s32[]{:T(128)} %bitcast.21, (f32[3840,128]{1,0:T(8,128)}, f32[128,128]{1,0:T(8,128)S(1)}, s32[1,512]{1,0:T(1,128)S(1)}, s32[1,512]{1,0:T(1,128)S(1)}, bf16[2,512,512]{2,1,0:T(8,128)(2,1)}, /*index=5*/bf16[2,512,512]{2,1,0:T(8,128)(2,1)S(1)}, s32[64,128]{1,0:T(8,128)S(1)}, ...), branch_computations={%region_0.1_spmd, %region_1.9_spmd} | conditional | flops 2912907008 | bytes 100213616 | solution.py:569
  53.8 4.9 %all-to-all-start = ((f32[64,60,1,128]{3,2,1,0:T(1,128)}), f32[64,60,1,128]{3,2,1,0:T(1,128)S(1)}, u32[]{:S(2)}, u32[]{:S(2)}) async-start(f32[64,60,1,128]{3,2,1,0:T(1,128)} %bitcast.56), calls=%async_computation | async-start | bytes 3932160 | tf_op jit(solution)/shard_map/cond/branch_0_fun/all_to_all | solution.py:20
  58.7 2.0 branch_0_fun.5
  60.6 1.7 copy.36.place_ref
  62.3 0.9 reduce.1
  63.3 1.3 pad_add_fusion.row_place_ref
  64.6 84.5 %all-to-all-done = f32[64,60,1,128]{3,2,1,0:T(1,128)S(1)} async-done(((f32[64,60,1,128]{3,2,1,0:T(1,128)}), f32[64,60,1,128]{3,2,1,0:T(1,128)S(1)}, u32[]{:S(2)}, u32[]{:S(2)}) %all-to-all-start) | async-done | bytes 1966112 | tf_op jit(solution)/shard_map/cond/branch_0_fun/all_to_all | solution.py:20
  149.1 1.3 copy-done.2
  150.4 15.0 %branch_0_fun.6 = f32[3840,128]{1,0:T(8,128)} custom-call(f32[3840,128]{1,0:T(8,128)} %bitcast.46, s32[1024,1]{1,0:T(8,128)} %copy.36.place_ref, s32[128,1]{1,0:T(8,128)} %get-tuple-element.43.neg_place_ref, s32[1,1152]{1,0:T(1,128)} %pad_add_fusion.row_place_ref, bf16[2,512,512]{2,1,0:T(8,128)(2,1)} %get-tuple-element.44.rel_hi_ref, ...), custom_call_target="tpu_custom_call" | custom-call | tf_op jit(solution)/shard_map/cond/branch_0_fun/pallas_call | solution.py:518
  165.3 7.6 %all-to-all-start.1 = ((f32[64,60,1,128]{3,2,1,0:T(1,128)}), f32[64,60,1,128]{3,2,1,0:T(1,128)S(1)}, u32[]{:S(2)}, u32[]{:S(2)}) async-start(f32[64,60,1,128]{3,2,1,0:T(1,128)} %bitcast.47), calls=%async_computation.1 | async-start | bytes 3932160 | tf_op jit(solution)/shard_map/cond/branch_0_fun/all_to_all | solution.py:20
  172.9 0.1 copy.51
  173.0 0.7 reshape.122.code_ref
  173.7 90.2 %all-to-all-done.1 = f32[64,60,1,128]{3,2,1,0:T(1,128)S(1)} async-done(((f32[64,60,1,128]{3,2,1,0:T(1,128)}), f32[64,60,1,128]{3,2,1,0:T(1,128)S(1)}, u32[]{:S(2)}, u32[]{:S(2)}) %all-to-all-start.1) | async-done | bytes 1966112 | tf_op jit(solution)/shard_map/cond/branch_0_fun/all_to_all | solution.py:20
  263.9 1.3 copy-done
  265.2 3.4 %branch_0_fun.8 = f32[4,64,512]{2,1,0:T(8,128)} custom-call(f32[3840,128]{1,0:T(8,128)} %bitcast.43, s32[1,1216]{1,0:T(1,128)} %reshape.122.code_ref), custom_call_target="tpu_custom_call" | custom-call | tf_op jit(solution)/shard_map/cond/branch_0_fun/pallas_call | solution.py:526
  268.6 4.6 %all-to-all-start.2 = ((f32[4,64,512]{2,1,0:T(8,128)}), f32[4,64,512]{2,1,0:T(8,128)S(1)}, u32[]{:S(2)}, u32[]{:S(2)}) async-start(f32[4,64,512]{2,1,0:T(8,128)} %branch_0_fun.8), calls=%async_computation.2 | async-start | bytes 1048576 | tf_op jit(solution)/shard_map/cond/branch_0_fun/all_to_all | solution.py:527
  273.2 3.4 %branch_0_fun.7.own_ref = f32[256,512]{1,0:T(8,128)} custom-call(f32[3840,128]{1,0:T(8,128)} %bitcast.44, s32[1,1216]{1,0:T(1,128)} %reshape.122.code_ref), custom_call_target="tpu_custom_call" | custom-call | tf_op jit(solution)/shard_map/cond/branch_0_fun/pallas_call | solution.py:531
  276.6 4.7 %all-to-all-done.2.lists_ref = f32[4,64,512]{2,1,0:T(8,128)S(1)} async-done(((f32[4,64,512]{2,1,0:T(8,128)}), f32[4,64,512]{2,1,0:T(8,128)S(1)}, u32[]{:S(2)}, u32[]{:S(2)}) %all-to-all-start.2) | async-done | bytes 524320 | tf_op jit(solution)/shard_map/cond/branch_0_fun/all_to_all | solution.py:527
  281.3 0.8 copy-done.5
  282.1 2.6 branch_0_fun.9
  284.7 0.6 copy-done.21
  (5 shorter events, 0.0 us)
Async XLA Ops:
  0.6 53.1 %copy-start.14 = (s32[512]{0:T(512)S(1)}, s32[512]{0:T(512)}, u32[]{:S(2)}) copy-start(s32[512]{0:T(512)} %param.14) | copy-start | bytes 6148
  0.6 53.1 %copy-start.11 = (s32[512]{0:T(512)S(1)}, s32[512]{0:T(512)}, u32[]{:S(2)}) copy-start(s32[512]{0:T(512)} %param.13) | copy-start | bytes 6148
  0.7 53.1 %copy-start.3 = (f32[256,400]{0,1:T(8,128)S(1)}, f32[256,400]{0,1:T(8,128)}, u32[]{:S(2)}) copy-start(f32[256,400]{0,1:T(8,128)} %param.9) | copy-start | bytes 1228804
  0.7 53.1 %copy-start.10 = (s32[64,32]{0,1:T(8,128)S(1)}, s32[64,32]{0,1:T(8,128)}, u32[]{:S(2)}) copy-start(s32[64,32]{0,1:T(8,128)} %param.12) | copy-start | bytes 24580
  0.7 53.1 %copy-start.17 = (f32[256]{0:T(256)S(1)}, f32[256]{0:T(256)}, u32[]{:S(2)}) copy-start(f32[256]{0:T(256)} %param.10) | copy-start | bytes 3076
  2.8 43.3 %collective-permute-start.2 = (f32[432,256]{1,0:T(8,128)}, f32[432,256]{1,0:T(8,128)S(1)}, u32[]{:S(2)}, u32[]{:S(2)}) collective-permute-start(f32[432,256]{1,0:T(8,128)} %get-tuple-element.68.own_ref), channel_id=1, source_target_pairs={{0,384},{8,392},{16,400},{24,408},{32,416},{40,424},{48,432},{56,4... | collective-permute-start | bytes 1327112 | tf_op jit(solution)/shard_map/ppermute | solution.py:496
  7.7 38.4 %collective-permute-start.1 = (f32[432,256]{1,0:T(8,128)}, f32[432,256]{1,0:T(8,128)S(1)}, u32[]{:S(2)}, u32[]{:S(2)}) collective-permute-start(f32[432,256]{1,0:T(8,128)} %get-tuple-element.68.own_ref), channel_id=1, source_target_pairs={{0,256},{8,264},{16,272},{24,280},{32,288},{40,296},{48,304},{56,3... | collective-permute-start | bytes 1327112 | tf_op jit(solution)/shard_map/ppermute | solution.py:496
  10.2 35.9 %collective-permute-start = (f32[432,256]{1,0:T(8,128)}, f32[432,256]{1,0:T(8,128)S(1)}, u32[]{:S(2)}, u32[]{:S(2)}) collective-permute-start(f32[432,256]{1,0:T(8,128)} %get-tuple-element.68.own_ref), channel_id=1, source_target_pairs={{0,128},{8,136},{16,144},{24,152},{32,160},{40,168},{48,176},{56,1... | collective-permute-start | bytes 1327112 | tf_op jit(solution)/shard_map/ppermute | solution.py:496
  12.6 33.5 %all-to-all-start.7 = ((f32[64,2,1,128]{3,1,2,0:T(2,128)}), f32[64,2,1,128]{3,1,2,0:T(2,128)S(1)}, u32[]{:S(2)}, u32[]{:S(2)}) async-start(f32[64,2,1,128]{3,1,2,0:T(2,128)} %bitcast.60), calls=%async_computation.7 | async-start | bytes 131072 | tf_op jit(solution)/shard_map/all_to_all | solution.py:20
  46.0 0.8 copy-start.7
  46.1 0.9 copy-start.8
  46.1 1.1 copy-start.9
  53.8 95.3 %all-to-all-start = ((f32[64,60,1,128]{3,2,1,0:T(1,128)}), f32[64,60,1,128]{3,2,1,0:T(1,128)S(1)}, u32[]{:S(2)}, u32[]{:S(2)}) async-start(f32[64,60,1,128]{3,2,1,0:T(1,128)} %bitcast.56), calls=%async_computation | async-start | bytes 3932160 | tf_op jit(solution)/shard_map/cond/branch_0_fun/all_to_all | solution.py:20
  149.1 1.3 copy-start.2
  165.3 98.6 %all-to-all-start.1 = ((f32[64,60,1,128]{3,2,1,0:T(1,128)}), f32[64,60,1,128]{3,2,1,0:T(1,128)S(1)}, u32[]{:S(2)}, u32[]{:S(2)}) async-start(f32[64,60,1,128]{3,2,1,0:T(1,128)} %bitcast.47), calls=%async_computation.1 | async-start | bytes 3932160 | tf_op jit(solution)/shard_map/cond/branch_0_fun/all_to_all | solution.py:20
  263.9 1.3 copy-start
  268.6 12.7 %all-to-all-start.2 = ((f32[4,64,512]{2,1,0:T(8,128)}), f32[4,64,512]{2,1,0:T(8,128)S(1)}, u32[]{:S(2)}, u32[]{:S(2)}) async-start(f32[4,64,512]{2,1,0:T(8,128)} %branch_0_fun.8), calls=%async_computation.2 | async-start | bytes 1048576 | tf_op jit(solution)/shard_map/cond/branch_0_fun/all_to_all | solution.py:527
  281.3 0.8 copy-start.5
  284.7 0.6 copy-start.21

commit v7 on v6

--- a/solution.py
+++ b/solution.py
@@ -81,7 +81,9 @@
 COLUMN = 4
 DEPTH = 16
 SENT = 32
-ROOM = 32
+NEG_ROOM = 24
+SLOT_ROOM = 8
+ROOM = NEG_ROOM + SLOT_ROOM
 AT_NEGS = 64
 CODE = 2048
 
@@ -248,10 +250,11 @@
     slots = jnp.where(lane < peers, info, 0.0)
     column = grid(same_depth)
     over_slots = jnp.sum(jnp.maximum(slots - CAP, 0.0), 0, keepdims=True)
-    sums = jnp.where(iota((PER_LINE, LANES), 0) == 0, earlier, over_slots).astype(BF16)
-    sums = jnp.max(dot(sums, column))
+    first = iota((PER_LINE, LANES), 0) == 0
+    sums = jnp.where(first, earlier, over_slots).astype(BF16)
+    sums = jnp.max(dot(sums, column) - jnp.where(first, NEG_ROOM, SLOT_ROOM))
     total = jnp.max(dot((slots + earlier).astype(BF16), column))
-    over = (total > COLUMN * CAP) | (sums > ROOM) | (jnp.max(over_slots) > ROOM)
+    over = (total > COLUMN * CAP) | (sums > 0.0)
     flag_ref[0] = over.astype(jnp.int32)
 
     neg_rows = jnp.broadcast_to(neg_rows, marks.shape)
@@ -283,19 +286,20 @@
     helped = jnp.where((place >= 0.0) & ~own, 1.0, 0.0)
     held = jnp.broadcast_to(jnp.sum(helped, 1, keepdims=True), marks.shape)
     entry = dot(before(peers), held.astype(BF16)) + dot(helped.astype(BF16), upto)
-    codes = touched + CODE * jnp.where(helped > 0.0, entry + ROOM, 0.0)
+    codes = touched + CODE * jnp.where(helped > 0.0, entry + NEG_ROOM, 0.0)
     neg_entry = dot(neg_marks.astype(BF16), upto)
     neg_codes = neg_rows + CODE * jnp.where((neg_place >= 0.0) & ~own, neg_entry, 0.0)
 
     mates = len(refs) - 1
-    column = iota((ROOM, LANES), 0)
-    of_slots = jnp.zeros((ROOM, LANES), F32)
-    for e in range(ROOM):
+    column = iota((SLOT_ROOM, LANES), 0)
+    of_slots = jnp.zeros((SLOT_ROOM, LANES), F32)
+    for e in range(SLOT_ROOM):
         row = jnp.sum(jnp.where((helped > 0.0) & (entry == e + 1.0), touched, 0.0), 0, keepdims=True)
         of_slots = jnp.where(column == e, row, of_slots)
+    column = iota((NEG_ROOM, LANES), 0)
     of_negs = jnp.where((neg_entry[:1] == column + 1.0) & (neg_marks[:1] > 0.0), neg_rows[:1], 0.0)
     row = jnp.sum(jnp.concatenate([of_negs, of_slots], 0), 1, keepdims=True).astype(jnp.int32)
-    from_mates = bits(iota((2 * ROOM, mates * owned), 1) == row - (owned + 1))
+    from_mates = bits(iota((ROOM, mates * owned), 1) == row - (owned + 1))
 
     spot = iota((peers, owned + LANES), 1)
     out = jnp.zeros(marks.shape, jnp.int32)
@@ -317,7 +321,7 @@
         return jnp.concatenate([of_hi[:, :MAIN] + of_lo, fold(of_hi[:, MAIN:])], 1)
 
     held = joined(dot(from_mates, hi[:, owned:], 1, 1), dot(from_mates, lo[:, owned:], 1, 1))
-    held = jnp.concatenate([held, jnp.zeros((LANES - 2 * ROOM, WIDE), F32)], 0)
+    held = jnp.concatenate([held, jnp.zeros((LANES - ROOM, WIDE), F32)], 0)
     held_hi, held_lo = pieces(held, 2)
     held_hi = jnp.concatenate([held_hi[:, :MAIN], halves(held_hi[:, MAIN:], held_lo[:, MAIN:])], 1)
     held_lo = held_lo[:, :MAIN]
@@ -454,31 +458,29 @@
     pack(jnp.concatenate([of_main, fold(of_hi[:, MAIN:])], 1), out_ref)
 
 
-def help_kernel(block_ref, code_ref, out_ref, hi_ref, lo_ref):
+def sum_kernel(block_ref, code_ref, list_ref, own_ref, hi_ref, lo_ref):
     unpack(block_ref, hi_ref, lo_ref)
     code = code_ref[...]
+    row = lax.bitwise_and(code, CODE - 1) - 1
     entry = shift_down(code, 11) - 1
-    here = iota((out_ref.shape[1], code.shape[1]), 0) == entry
-    row = jnp.where(here, (lax.bitwise_and(code, CODE - 1) - 1).astype(F32), -1.0)
-    row = jnp.max(row, 1, keepdims=True)
-    main, tails = gathered(bits(here), hi_ref, lo_ref)
-    tails = jnp.where(iota(tails.shape, 1) < TAIL, tails, row)
-    for y in range(out_ref.shape[0]):
-        out_ref[y] = jnp.concatenate([main, tails], 1)
-
-
-def sum_kernel(block_ref, code_ref, out_ref, hi_ref, lo_ref):
-    unpack(block_ref, hi_ref, lo_ref)
-    row = lax.bitwise_and(code_ref[...], CODE - 1) - 1
-    chosen = bits(iota((out_ref.shape[0], row.shape[1]), 0) == row)
-    out_ref[...] = jnp.concatenate(gathered(chosen, hi_ref, lo_ref), 1)
+    listed = iota((ROOM, code.shape[1]), 0) == entry
+    number = jnp.max(jnp.where(listed, row.astype(F32), -1.0), 1, keepdims=True)
+    mine = iota((own_ref.shape[0], code.shape[1]), 0) == row
+    chosen = jnp.concatenate([jnp.where(mine, 1.0, 0.0), jnp.where(listed, 1.0, 0.0)], 0)
+    main, tails = gathered(chosen.astype(BF16), hi_ref, lo_ref)
+    owned = own_ref.shape[0]
+    own_ref[...] = jnp.concatenate([main[:owned], tails[:owned]], 1)
+    tails = tails[owned:]
+    tails = jnp.where(iota(tails.shape, 1) < TAIL, tails, number)
+    for y in range(COLUMN):
+        list_ref[y] = jnp.concatenate([main[owned:], tails], 1)
 
 
 def update_kernel(me_ref, own_ref, lists_ref, table_ref, state_ref, new_table_ref, new_state_ref):
     width, owned = table_ref.shape
     rows = lists_ref[...].reshape(-1, WIDE)
     up = lax.shift_right_logical(me_ref[0], jnp.int32(4))
-    mate = iota((rows.shape[0], 1), 0) // (2 * ROOM)
+    mate = iota((rows.shape[0], 1), 0) // ROOM
     first = lax.bitwise_xor(mate, jnp.broadcast_to(up, mate.shape)) * owned
     at = rows[:, WIDE - 1 :].astype(jnp.int32) - first
     chosen = bits(iota((rows.shape[0], owned), 1) == at)
@@ -523,12 +525,15 @@
     )(blocks, edge_place.reshape(-1, 1), neg_place, row_place, rel_hi, rel_lo)
     returned = exchange_blocks(grads)
     codes = codes[:, :CAP].T.reshape(1, -1)
-    lists = call(help_kernel, shaped(COLUMN, 2 * ROOM, WIDE), scratch_shapes=split)(returned, codes)
+    lists, own = call(
+        sum_kernel,
+        (shaped(COLUMN, ROOM, WIDE), shaped(owned, WIDE)),
+        scratch_shapes=split,
+    )(returned, codes)
     lists = lax.all_to_all(
         lists, "grp", 0, 0, tiled=True,
         axis_index_groups=[list(range(z, peers, DEPTH)) for z in range(DEPTH)],
     )
-    own = call(sum_kernel, shaped(owned, WIDE), scratch_shapes=split)(returned, codes)
     return call(
         update_kernel,
         (shaped(width, owned), shaped(1, owned)),

time: 286 us -> 284 us (level)
  blocking collectives: 0 us -> 11.1 us
  starting transfers between devices: 45.7 us -> 40.9 us
  Pallas kernels: 34.3 us -> 30.1 us
  waiting for transfers between devices: 191 us -> 187 us
    all_to_all x0 -> x1, blocking collectives: none -> 11.1 us  [compact_path(): lax.all_to_all(lists, 'grp', 0, 0, tiled=True, axis_index_groups=[list(ra...]
    all_to_all x1 -> x0, waiting for transfers between devices: 4.67 us -> none  [compact_path(): lax.all_to_all(lists, 'grp', 0, 0, tiled=True, axis_index_groups=[list(ra...]
    all_to_all x1 -> x0, starting transfers between devices: 4.64 us -> none  [compact_path(): lax.all_to_all(lists, 'grp', 0, 0, tiled=True, axis_index_groups=[list(ra...]
    pallas_call x2 -> x1, Pallas kernels: 6.76 us -> 3.56 us  [compact_path(): call(sum_kernel, (shaped(COLUMN, ROOM, WIDE), shaped(owned, WIDE)), scrat...]
  transfers between devices with their start and end apart: 7 -> 6, of which waited for: 4 -> 3; matrix products, arithmetic and copies ran while one was open for 3% -> 3% of each run, Pallas kernels for 2% -> 1%
where the time goes in v7:
time: 284 us; the launch traced here: 283 us
  waiting for transfers between devices  187 us (66%)
  starting transfers between devices  40.9 us (14%)
  Pallas kernels  30.1 us (11%)
  blocking collectives  11.1 us (4%)
  local copies, waits for them, and re-layouts  6.61 us (2%)
  other arithmetic  4.93 us (2%)
    all_to_all x3, waiting for transfers between devices, exchange(): lax.all_to_all(blocks, 'grp', split_axis=0, concat_axis=0, tiled=True)  187 us
    all_to_all x3, starting transfers between devices, exchange(): lax.all_to_all(blocks, 'grp', split_axis=0, concat_axis=0, tiled=True)  31.1 us
    pallas_call x1, Pallas kernels, compact_path(): call(edges_kernel, shaped(*blocks.shape), scratch_shapes=split + [pltpu.V...  15 us
    all_to_all x1, blocking collectives, compact_path(): lax.all_to_all(lists, 'grp', 0, 0, tiled=True, axis_index_groups=[list(ra...  11.1 us
    ppermute x3, starting transfers between devices, to_mates(): lax.ppermute(x, 'grp', [(p, p ^ d * DEPTH) for p in range(peers)])  9.81 us
    pallas_call x1, Pallas kernels, per_device(): call(functools.partial(pack_kernel, number), (shaped(peers * BLOCK, LANES...  5.7 us
  transfers between devices with their start and end apart: 6, of which 3 were waited for; matrix products, arithmetic and copies ran while one was open for 3% of the time, Pallas kernels for 1%

profile of v7, /device:TPU:6, one launch (start us, length us, event | category | flops | bytes accessed | tf_op | source)
XLA Modules:
  0.0 282.9 jit_solution(2117918738067300949)
XLA Ops:
  0.6 0.0 copy-start.12
  0.6 0.0 copy-start.8
  0.7 0.0 copy-start.7
  0.7 0.0 copy-start.6
  0.7 0.0 copy-start
  0.7 0.0 copy-start.9
  0.7 2.1 shard_map.86
  2.8 4.9 %collective-permute-start.2 = (f32[432,256]{1,0:T(8,128)}, f32[432,256]{1,0:T(8,128)S(1)}, u32[]{:S(2)}, u32[]{:S(2)}) collective-permute-start(f32[432,256]{1,0:T(8,128)} %get-tuple-element.70.own_ref), channel_id=1, source_target_pairs={{0,384},{8,392},{16,400},{24,408},{32,416},{40,424},{48,432},{56,4... | collective-permute-start | bytes 1327112 | tf_op jit(solution)/shard_map/ppermute | solution.py:498
  7.8 2.5 collective-permute-start.1
  10.3 2.3 collective-permute-start
  12.7 18.7 %all-to-all-start.7 = ((f32[64,2,1,128]{3,1,2,0:T(2,128)}), f32[64,2,1,128]{3,1,2,0:T(2,128)S(1)}, u32[]{:S(2)}, u32[]{:S(2)}) async-start(f32[64,2,1,128]{3,1,2,0:T(2,128)} %bitcast.59), calls=%async_computation.7 | async-start | bytes 131072 | tf_op jit(solution)/shard_map/all_to_all | solution.py:20
  31.4 2.7 fusion.15
  34.1 12.0 %all-to-all-done.7 = f32[64,2,1,128]{3,1,2,0:T(2,128)S(1)} async-done(((f32[64,2,1,128]{3,1,2,0:T(2,128)}), f32[64,2,1,128]{3,1,2,0:T(2,128)S(1)}, u32[]{:S(2)}, u32[]{:S(2)}) %all-to-all-start.7) | async-done | bytes 65568 | tf_op jit(solution)/shard_map/all_to_all | solution.py:20
  46.1 0.0 collective-permute-done.2.third_ref
  46.1 0.0 copy-start.5
  46.1 0.0 collective-permute-done.1.second_ref
  46.1 0.0 collective-permute-done.first_ref
  46.2 0.8 copy-done.5
  46.9 5.7 %shard_map.87 = (f32[3840,128]{1,0:T(8,128)}, s32[64,128]{1,0:T(8,128)S(1)}, s32[1]{0:T(128)}) custom-call(s32[1]{0:T(128)} %bitcast.13.me_ref, f32[128,128]{1,0:T(8,128)S(1)} %bitcast.57, f32[432,256]{1,0:T(8,128)} %get-tuple-element.70.own_ref, f32[432,256]{1,0:T(8,128)} %collective-permute-done.first_ref, f32[432,256]{1,0:T(8,128)} %collective-permute-done.1.second_ref, ...), custom_call_target="tpu_custom_call" | custom-call | tf_op jit(solution)/shard_map/pallas_call | solution.py:563
  53.3 0.0 copy-done.12
  53.3 0.0 copy-done.8
  53.3 0.0 copy-done.7
  53.3 0.0 copy-done.6
  53.3 0.0 copy-done
  53.3 0.0 copy-done.9
  53.3 228.8 %conditional.1 = (f32[256]{0:T(256)S(1)}, f32[400,256]{1,0:T(8,128)S(1)}) conditional(s32[]{:T(128)} %bitcast.21, (f32[3840,128]{1,0:T(8,128)}, f32[128,128]{1,0:T(8,128)S(1)}, s32[1,512]{1,0:T(1,128)S(1)}, s32[1,512]{1,0:T(1,128)S(1)}, bf16[2,512,512]{2,1,0:T(8,128)(2,1)}, /*index=5*/bf16[2,512,512]{2,1,0:T(8,128)(2,1)S(1)}, ...), branch_computations={%region_0.1_spmd, %region_1.9_spmd} | conditional | flops 2912907008 | bytes 93422224 | solution.py:574
  53.3 4.9 %all-to-all-start = ((f32[64,60,1,128]{3,2,1,0:T(1,128)}), f32[64,60,1,128]{3,2,1,0:T(1,128)S(1)}, u32[]{:S(2)}, u32[]{:S(2)}) async-start(f32[64,60,1,128]{3,2,1,0:T(1,128)} %bitcast.55), calls=%async_computation | async-start | bytes 3932160 | tf_op jit(solution)/shard_map/cond/branch_0_fun/all_to_all | solution.py:20
  58.2 2.0 branch_0_fun.4
  60.2 1.7 copy.36.place_ref
  61.9 0.9 reduce.1
  62.8 1.3 pad_add_fusion.row_place_ref
  64.1 84.5 %all-to-all-done = f32[64,60,1,128]{3,2,1,0:T(1,128)S(1)} async-done(((f32[64,60,1,128]{3,2,1,0:T(1,128)}), f32[64,60,1,128]{3,2,1,0:T(1,128)S(1)}, u32[]{:S(2)}, u32[]{:S(2)}) %all-to-all-start) | async-done | bytes 1966112 | tf_op jit(solution)/shard_map/cond/branch_0_fun/all_to_all | solution.py:20
  148.6 0.0 copy-start.1
  148.6 1.3 copy-done.1
  149.9 15.0 %branch_0_fun.5 = f32[3840,128]{1,0:T(8,128)} custom-call(f32[3840,128]{1,0:T(8,128)} %bitcast.44, s32[1024,1]{1,0:T(8,128)} %copy.36.place_ref, s32[128,1]{1,0:T(8,128)} %get-tuple-element.43.neg_place_ref, s32[1,1152]{1,0:T(1,128)} %pad_add_fusion.row_place_ref, bf16[2,512,512]{2,1,0:T(8,128)(2,1)} %get-tuple-element.44.rel_hi_ref, ...), custom_call_target="tpu_custom_call" | custom-call | tf_op jit(solution)/shard_map/cond/branch_0_fun/pallas_call | solution.py:520
  164.9 7.5 %all-to-all-start.1 = ((f32[64,60,1,128]{3,2,1,0:T(1,128)}), f32[64,60,1,128]{3,2,1,0:T(1,128)S(1)}, u32[]{:S(2)}, u32[]{:S(2)}) async-start(f32[64,60,1,128]{3,2,1,0:T(1,128)} %bitcast.46), calls=%async_computation.1 | async-start | bytes 3932160 | tf_op jit(solution)/shard_map/cond/branch_0_fun/all_to_all | solution.py:20
  172.4 0.1 copy.51
  172.5 0.7 reshape.122.code_ref
  173.2 90.8 %all-to-all-done.1 = f32[64,60,1,128]{3,2,1,0:T(1,128)S(1)} async-done(((f32[64,60,1,128]{3,2,1,0:T(1,128)}), f32[64,60,1,128]{3,2,1,0:T(1,128)S(1)}, u32[]{:S(2)}, u32[]{:S(2)}) %all-to-all-start.1) | async-done | bytes 1966112 | tf_op jit(solution)/shard_map/cond/branch_0_fun/all_to_all | solution.py:20
  263.9 1.3 copy-done.2
  265.2 3.6 %branch_0_fun.6 = (f32[4,32,512]{2,1,0:T(8,128)}, f32[256,512]{1,0:T(8,128)}) custom-call(f32[3840,128]{1,0:T(8,128)} %bitcast.45, s32[1,1216]{1,0:T(1,128)} %reshape.122.code_ref), custom_call_target="tpu_custom_call" | custom-call | tf_op jit(solution)/shard_map/cond/branch_0_fun/pallas_call | solution.py:528
  268.8 11.1 %all_to_all.33.lists_ref = f32[4,32,512]{2,1,0:T(8,128)} all-to-all(f32[4,32,512]{2,1,0:T(8,128)} %get-tuple-element.48), channel_id=1, replica_groups={{0,128,256,384},{8,136,264,392},{16,144,272,400},{24,152,280,408},{32,1..., dimensions={0} | all-to-all | bytes 524288 | tf_op jit(solution)/shard_map/cond/branch_0_fun/all_to_all | solution.py:533
  279.9 0.0 copy-done.3
  279.9 1.7 branch_0_fun.7
  282.2 0.0 copy-start.13
  282.2 0.0 copy-start.14
  282.2 0.7 copy-done.13
  282.9 0.0 copy-done.14
  (3 shorter events, 0.0 us)
Async XLA Ops:
  0.6 52.6 %copy-start.12 = (s32[2]{0:T(128)S(1)}, s32[2]{0:T(128)}, u32[]{:S(2)}) copy-start(s32[2]{0:T(128)} %negs_ref.1) | copy-start | bytes 28
  0.6 52.6 %copy-start.8 = (s32[512]{0:T(512)S(1)}, s32[512]{0:T(512)}, u32[]{:S(2)}) copy-start(s32[512]{0:T(512)} %param.14) | copy-start | bytes 6148
  0.7 52.6 %copy-start.7 = (s32[512]{0:T(512)S(1)}, s32[512]{0:T(512)}, u32[]{:S(2)}) copy-start(s32[512]{0:T(512)} %param.13) | copy-start | bytes 6148
  0.7 52.6 %copy-start.6 = (s32[64,32]{0,1:T(8,128)S(1)}, s32[64,32]{0,1:T(8,128)}, u32[]{:S(2)}) copy-start(s32[64,32]{0,1:T(8,128)} %param.12) | copy-start | bytes 24580
  0.7 52.6 %copy-start = (f32[2,400,400]{2,1,0:T(8,128)S(1)}, f32[2,400,400]{2,1,0:T(8,128)}, u32[]{:S(2)}) copy-start(f32[2,400,400]{2,1,0:T(8,128)} %param.11) | copy-start | bytes 3840004
  0.7 52.6 %copy-start.9 = (f32[256]{0:T(256)S(1)}, f32[256]{0:T(256)}, u32[]{:S(2)}) copy-start(f32[256]{0:T(256)} %param.10) | copy-start | bytes 3076
  2.8 43.3 %collective-permute-start.2 = (f32[432,256]{1,0:T(8,128)}, f32[432,256]{1,0:T(8,128)S(1)}, u32[]{:S(2)}, u32[]{:S(2)}) collective-permute-start(f32[432,256]{1,0:T(8,128)} %get-tuple-element.70.own_ref), channel_id=1, source_target_pairs={{0,384},{8,392},{16,400},{24,408},{32,416},{40,424},{48,432},{56,4... | collective-permute-start | bytes 1327112 | tf_op jit(solution)/shard_map/ppermute | solution.py:498
  7.8 38.4 %collective-permute-start.1 = (f32[432,256]{1,0:T(8,128)}, f32[432,256]{1,0:T(8,128)}, u32[]{:S(2)}, u32[]{:S(2)}) collective-permute-start(f32[432,256]{1,0:T(8,128)} %get-tuple-element.70.own_ref), channel_id=1, source_target_pairs={{0,256},{8,264},{16,272},{24,280},{32,288},{40,296},{48,304},{56,3... | collective-permute-start | bytes 1327112 | tf_op jit(solution)/shard_map/ppermute | solution.py:498
  10.3 35.8 %collective-permute-start = (f32[432,256]{1,0:T(8,128)}, f32[432,256]{1,0:T(8,128)}, u32[]{:S(2)}, u32[]{:S(2)}) collective-permute-start(f32[432,256]{1,0:T(8,128)} %get-tuple-element.70.own_ref), channel_id=1, source_target_pairs={{0,128},{8,136},{16,144},{24,152},{32,160},{40,168},{48,176},{56,1... | collective-permute-start | bytes 1327112 | tf_op jit(solution)/shard_map/ppermute | solution.py:498
  12.7 33.5 %all-to-all-start.7 = ((f32[64,2,1,128]{3,1,2,0:T(2,128)}), f32[64,2,1,128]{3,1,2,0:T(2,128)S(1)}, u32[]{:S(2)}, u32[]{:S(2)}) async-start(f32[64,2,1,128]{3,1,2,0:T(2,128)} %bitcast.59), calls=%async_computation.7 | async-start | bytes 131072 | tf_op jit(solution)/shard_map/all_to_all | solution.py:20
  46.1 0.8 copy-start.5
  53.3 95.3 %all-to-all-start = ((f32[64,60,1,128]{3,2,1,0:T(1,128)}), f32[64,60,1,128]{3,2,1,0:T(1,128)S(1)}, u32[]{:S(2)}, u32[]{:S(2)}) async-start(f32[64,60,1,128]{3,2,1,0:T(1,128)} %bitcast.55), calls=%async_computation | async-start | bytes 3932160 | tf_op jit(solution)/shard_map/cond/branch_0_fun/all_to_all | solution.py:20
  148.6 1.3 copy-start.1
  164.9 115.0 %copy-start.3 = (f32[400,256]{1,0:T(8,128)S(1)}, f32[400,256]{1,0:T(8,128)}, u32[]{:S(2)}) copy-start(f32[400,256]{1,0:T(8,128)} %get-tuple-element.49.table_ref) | copy-start | bytes 1228804 | tf_op jit(solution)/shard_map/cond
  164.9 99.0 %all-to-all-start.1 = ((f32[64,60,1,128]{3,2,1,0:T(1,128)}), f32[64,60,1,128]{3,2,1,0:T(1,128)S(1)}, u32[]{:S(2)}, u32[]{:S(2)}) async-start(f32[64,60,1,128]{3,2,1,0:T(1,128)} %bitcast.46), calls=%async_computation.1 | async-start | bytes 3932160 | tf_op jit(solution)/shard_map/cond/branch_0_fun/all_to_all | solution.py:20
  263.9 1.3 copy-start.2
  282.2 0.8 copy-start.13
  282.2 0.7 copy-start.14

commit v8 on v7

--- a/solution.py
+++ b/solution.py
@@ -124,8 +124,9 @@
 def dot3(a, b, a_dim=1, b_dim=0):
     a_hi, a_lo = a if isinstance(a, tuple) else pieces(a, 2)
     b_hi, b_lo = b if isinstance(b, tuple) else pieces(b, 2)
-    small = dot(a_lo, b_hi, a_dim, b_dim) + dot(a_hi, b_lo, a_dim, b_dim)
-    return small + dot(a_hi, b_hi, a_dim, b_dim)
+    rows = a_hi.shape[0]
+    both = dot(jnp.concatenate([a_lo, a_hi], 0), b_hi, a_dim, b_dim)
+    return both[:rows] + dot(a_hi, b_lo, a_dim, b_dim) + both[rows:]
 
 
 def halves(hi, lo):
@@ -313,23 +314,18 @@
         onehot[k * peers : (k + 1) * peers, :] = bits(spot == at)
     codes_ref[...] = out
 
-    hi, lo = pieces(jnp.concatenate([ref[:width] for ref in refs], 1), 2)
-    tails = [hi[MAIN:]] * (PER_LINE // 2) + [lo[MAIN:]] * (PER_LINE // 2)
-    hi, lo = jnp.concatenate([hi[:MAIN]] + tails, 0), lo[:MAIN]
-
-    def joined(of_hi, of_lo):
-        return jnp.concatenate([of_hi[:, :MAIN] + of_lo, fold(of_hi[:, MAIN:])], 1)
-
-    held = joined(dot(from_mates, hi[:, owned:], 1, 1), dot(from_mates, lo[:, owned:], 1, 1))
-    held = jnp.concatenate([held, jnp.zeros((LANES - ROOM, WIDE), F32)], 0)
-    held_hi, held_lo = pieces(held, 2)
-    held_hi = jnp.concatenate([held_hi[:, :MAIN], halves(held_hi[:, MAIN:], held_lo[:, MAIN:])], 1)
-    held_lo = held_lo[:, :MAIN]
-    own, other = onehot[:, :owned], onehot[:, owned:]
-    got = joined(
-        dot(own, hi[:, :owned], 1, 1) + dot(other, held_hi),
-        dot(own, lo[:, :owned], 1, 1) + dot(other, held_lo),
-    )
+    def split(rows):
+        hi, lo = pieces(rows, 2)
+        return jnp.concatenate([hi[:, :MAIN], halves(hi[:, MAIN:], lo[:, MAIN:])], 1), lo[:, :MAIN]
+
+    def fetched(chosen, hi, lo):
+        of_hi = dot(chosen, hi)
+        return jnp.concatenate([of_hi[:, :MAIN] + dot(chosen, lo), fold(of_hi[:, MAIN:])], 1)
+
+    tables = [jnp.concatenate([ref[:MAIN]] + [ref[MAIN:width]] * PER_LINE, 0).T for ref in refs]
+    held = fetched(from_mates, *split(jnp.concatenate(tables[1:], 0)))
+    held = jnp.concatenate([tables[0], held, jnp.zeros((LANES - ROOM, WIDE), F32)], 0)
+    got = fetched(onehot[...], *split(held))
     pack(got, out_ref)
 
 
@@ -433,23 +429,20 @@
         grad_hi[span, :MAIN], grad_lo[span, :] = pieces(grad[:, :MAIN], 2)
         grad_hi[span, MAIN:] = halves(*pieces(spread(grad[:, MAIN:]), 2))
 
-    negs = tuple(pieces(got[2 * edges :], 2))
-    shares = jnp.zeros((total, WIDE), F32)
-    for kind in range(kinds):
-        start = kind * per_rel
-        relation = rel_hi_ref[kind], rel_lo_ref[kind]
-        query = dot3(got[start : start + per_rel], relation)
-        tail = got[edges + start : edges + start + per_rel]
-        positive = jnp.sum(query * tail, 1, keepdims=True)
-        grad_pos = jax.nn.sigmoid(positive) - 1.0
-        keep(edges + start, grad_pos * query)
-        query = tuple(pieces(query, 2))
-        grad_neg = jax.nn.sigmoid(dot3(query, negs, 1, 1)) / total
-        grad_query = grad_pos * tail + dot3(grad_neg, negs)
-        keep(start, dot3(grad_query, relation, 1, 1))
-        grad_neg = jax.nn.sigmoid(dot3(negs, query, 1, 1)) / total
-        shares = shares + dot3(grad_neg, query)
-    keep(2 * edges, shares)
+    spans = [slice(kind * per_rel, (kind + 1) * per_rel) for kind in range(kinds)]
+    relations = [(rel_hi_ref[kind], rel_lo_ref[kind]) for kind in range(kinds)]
+    query = jnp.concatenate([dot3(got[span], to) for span, to in zip(spans, relations)], 0)
+    tail, negs = got[edges : 2 * edges], tuple(pieces(got[2 * edges :], 2))
+    positive = jnp.sum(query * tail, 1, keepdims=True)
+    grad_pos = jax.nn.sigmoid(positive) - 1.0
+    keep(edges, grad_pos * query)
+    query = tuple(pieces(query, 2))
+    grad_neg = jax.nn.sigmoid(dot3(query, negs, 1, 1)) / total
+    grad_query = grad_pos * tail + dot3(grad_neg, negs)
+    for span, to in zip(spans, relations):
+        keep(span.start, dot3(grad_query[span], to, 1, 1))
+    grad_neg = jax.nn.sigmoid(dot3(negs, query, 1, 1)) / total
+    keep(2 * edges, dot3(grad_neg, query))
 
     spot = row_place_ref[...]
     chosen = bits(iota((count, spot.shape[1]), 0) == spot)

time: 284 us -> 282 us (level)
  no operation moved by 1% of the time
where the time goes in v8:
time: 282 us
  waiting for transfers between devices  187 us (66%)
  starting transfers between devices  40.9 us (15%)
  Pallas kernels  28.7 us (10%)
  blocking collectives  11.1 us (4%)
  local copies, waits for them, and re-layouts  6.61 us (2%)
  other arithmetic  4.93 us (2%)
    all_to_all x3, waiting for transfers between devices, exchange(): lax.all_to_all(blocks, 'grp', split_axis=0, concat_axis=0, tiled=True)  187 us
    all_to_all x3, starting transfers between devices, exchange(): lax.all_to_all(blocks, 'grp', split_axis=0, concat_axis=0, tiled=True)  31.1 us
    pallas_call x1, Pallas kernels, compact_path(): call(edges_kernel, shaped(*blocks.shape), scratch_shapes=split + [pltpu.V...  13.8 us
    all_to_all x1, blocking collectives, compact_path(): lax.all_to_all(lists, 'grp', 0, 0, tiled=True, axis_index_groups=[list(ra...  11.1 us
    ppermute x3, starting transfers between devices, to_mates(): lax.ppermute(x, 'grp', [(p, p ^ d * DEPTH) for p in range(peers)])  9.81 us
  transfers between devices with their start and end apart: 6, of which 3 were waited for; matrix products, arithmetic and copies ran while one was open for 3% of the time, Pallas kernels for 1%

profile of v8, /device:TPU:6, one launch (start us, length us, event | category | flops | bytes accessed | tf_op | source)
XLA Modules:
  0.0 281.6 jit_solution(10360294279922402916)
XLA Ops:
  0.6 0.0 copy-start.12
  0.6 0.0 copy-start.8
  0.7 0.0 copy-start.7
  0.7 0.0 copy-start.6
  0.7 0.0 copy-start
  0.7 0.0 copy-start.9
  0.7 2.1 shard_map.86
  2.8 4.9 %collective-permute-start.2 = (f32[432,256]{1,0:T(8,128)}, f32[432,256]{1,0:T(8,128)S(1)}, u32[]{:S(2)}, u32[]{:S(2)}) collective-permute-start(f32[432,256]{1,0:T(8,128)} %get-tuple-element.70.own_ref), channel_id=1, source_target_pairs={{0,384},{8,392},{16,400},{24,408},{32,416},{40,424},{48,432},{56,4... | collective-permute-start | bytes 1327112 | tf_op jit(solution)/shard_map/ppermute | solution.py:491
  7.8 2.5 collective-permute-start.1
  10.3 2.3 collective-permute-start
  12.7 18.7 %all-to-all-start.7 = ((f32[64,2,1,128]{3,1,2,0:T(2,128)}), f32[64,2,1,128]{3,1,2,0:T(2,128)S(1)}, u32[]{:S(2)}, u32[]{:S(2)}) async-start(f32[64,2,1,128]{3,1,2,0:T(2,128)} %bitcast.59), calls=%async_computation.7 | async-start | bytes 131072 | tf_op jit(solution)/shard_map/all_to_all | solution.py:20
  31.4 2.7 fusion.15
  34.1 12.0 %all-to-all-done.7 = f32[64,2,1,128]{3,1,2,0:T(2,128)S(1)} async-done(((f32[64,2,1,128]{3,1,2,0:T(2,128)}), f32[64,2,1,128]{3,1,2,0:T(2,128)S(1)}, u32[]{:S(2)}, u32[]{:S(2)}) %all-to-all-start.7) | async-done | bytes 65568 | tf_op jit(solution)/shard_map/all_to_all | solution.py:20
  46.1 0.0 collective-permute-done.2.third_ref
  46.1 0.0 copy-start.5
  46.1 0.0 collective-permute-done.1.second_ref
  46.1 0.0 collective-permute-done.first_ref
  46.2 0.8 copy-done.5
  46.9 5.5 %shard_map.87 = (f32[3840,128]{1,0:T(8,128)}, s32[64,128]{1,0:T(8,128)S(1)}, s32[1]{0:T(128)}) custom-call(s32[1]{0:T(128)} %bitcast.13.me_ref, f32[128,128]{1,0:T(8,128)S(1)} %bitcast.57, f32[432,256]{1,0:T(8,128)} %get-tuple-element.70.own_ref, f32[432,256]{1,0:T(8,128)} %collective-permute-done.first_ref, f32[432,256]{1,0:T(8,128)} %collective-permute-done.1.second_ref, ...), custom_call_target="tpu_custom_call" | custom-call | tf_op jit(solution)/shard_map/pallas_call | solution.py:556
  53.1 0.0 copy-done.12
  53.1 0.0 copy-done.8
  53.1 0.0 copy-done.7
  53.1 0.0 copy-done.6
  53.1 0.0 copy-done
  53.1 0.0 copy-done.9
  53.1 227.7 %conditional.1 = (f32[256]{0:T(256)S(1)}, f32[400,256]{1,0:T(8,128)S(1)}) conditional(s32[]{:T(128)} %bitcast.21, (f32[3840,128]{1,0:T(8,128)}, f32[128,128]{1,0:T(8,128)S(1)}, s32[1,512]{1,0:T(1,128)S(1)}, s32[1,512]{1,0:T(1,128)S(1)}, bf16[2,512,512]{2,1,0:T(8,128)(2,1)}, /*index=5*/bf16[2,512,512]{2,1,0:T(8,128)(2,1)S(1)}, ...), branch_computations={%region_0.1_spmd, %region_1.9_spmd} | conditional | flops 2912907008 | bytes 93422224 | solution.py:567
  53.1 4.9 %all-to-all-start = ((f32[64,60,1,128]{3,2,1,0:T(1,128)}), f32[64,60,1,128]{3,2,1,0:T(1,128)S(1)}, u32[]{:S(2)}, u32[]{:S(2)}) async-start(f32[64,60,1,128]{3,2,1,0:T(1,128)} %bitcast.55), calls=%async_computation | async-start | bytes 3932160 | tf_op jit(solution)/shard_map/cond/branch_0_fun/all_to_all | solution.py:20
  58.0 2.0 branch_0_fun.4
  60.0 1.7 copy.36.place_ref
  61.7 0.9 reduce.1
  62.6 1.3 pad_add_fusion.row_place_ref
  63.9 84.5 %all-to-all-done = f32[64,60,1,128]{3,2,1,0:T(1,128)S(1)} async-done(((f32[64,60,1,128]{3,2,1,0:T(1,128)}), f32[64,60,1,128]{3,2,1,0:T(1,128)S(1)}, u32[]{:S(2)}, u32[]{:S(2)}) %all-to-all-start) | async-done | bytes 1966112 | tf_op jit(solution)/shard_map/cond/branch_0_fun/all_to_all | solution.py:20
  148.4 0.0 copy-start.1
  148.4 1.3 copy-done.1
  149.7 13.8 %branch_0_fun.5 = f32[3840,128]{1,0:T(8,128)} custom-call(f32[3840,128]{1,0:T(8,128)} %bitcast.44, s32[1024,1]{1,0:T(8,128)} %copy.36.place_ref, s32[128,1]{1,0:T(8,128)} %get-tuple-element.43.neg_place_ref, s32[1,1152]{1,0:T(1,128)} %pad_add_fusion.row_place_ref, bf16[2,512,512]{2,1,0:T(8,128)(2,1)} %get-tuple-element.44.rel_hi_ref, ...), custom_call_target="tpu_custom_call" | custom-call | tf_op jit(solution)/shard_map/cond/branch_0_fun/pallas_call | solution.py:513
  163.5 7.5 %all-to-all-start.1 = ((f32[64,60,1,128]{3,2,1,0:T(1,128)}), f32[64,60,1,128]{3,2,1,0:T(1,128)S(1)}, u32[]{:S(2)}, u32[]{:S(2)}) async-start(f32[64,60,1,128]{3,2,1,0:T(1,128)} %bitcast.46), calls=%async_computation.1 | async-start | bytes 3932160 | tf_op jit(solution)/shard_map/cond/branch_0_fun/all_to_all | solution.py:20
  171.0 0.1 copy.51
  171.1 0.7 reshape.122.code_ref
  171.8 90.7 %all-to-all-done.1 = f32[64,60,1,128]{3,2,1,0:T(1,128)S(1)} async-done(((f32[64,60,1,128]{3,2,1,0:T(1,128)}), f32[64,60,1,128]{3,2,1,0:T(1,128)S(1)}, u32[]{:S(2)}, u32[]{:S(2)}) %all-to-all-start.1) | async-done | bytes 1966112 | tf_op jit(solution)/shard_map/cond/branch_0_fun/all_to_all | solution.py:20
  262.5 1.3 copy-done.2
  263.9 3.6 %branch_0_fun.6 = (f32[4,32,512]{2,1,0:T(8,128)}, f32[256,512]{1,0:T(8,128)}) custom-call(f32[3840,128]{1,0:T(8,128)} %bitcast.45, s32[1,1216]{1,0:T(1,128)} %reshape.122.code_ref), custom_call_target="tpu_custom_call" | custom-call | tf_op jit(solution)/shard_map/cond/branch_0_fun/pallas_call | solution.py:521
  267.4 11.1 %all_to_all.33.lists_ref = f32[4,32,512]{2,1,0:T(8,128)} all-to-all(f32[4,32,512]{2,1,0:T(8,128)} %get-tuple-element.48), channel_id=1, replica_groups={{0,128,256,384},{8,136,264,392},{16,144,272,400},{24,152,280,408},{32,1..., dimensions={0} | all-to-all | bytes 524288 | tf_op jit(solution)/shard_map/cond/branch_0_fun/all_to_all | solution.py:526
  278.5 0.0 copy-done.3
  278.5 1.7 branch_0_fun.7
  280.8 0.0 copy-start.13
  280.8 0.0 copy-start.14
  280.8 0.7 copy-done.13
  281.6 0.0 copy-done.14
  (3 shorter events, 0.0 us)
Async XLA Ops:
  0.6 52.4 %copy-start.12 = (s32[2]{0:T(128)S(1)}, s32[2]{0:T(128)}, u32[]{:S(2)}) copy-start(s32[2]{0:T(128)} %negs_ref.1) | copy-start | bytes 28
  0.6 52.4 %copy-start.8 = (s32[512]{0:T(512)S(1)}, s32[512]{0:T(512)}, u32[]{:S(2)}) copy-start(s32[512]{0:T(512)} %param.14) | copy-start | bytes 6148
  0.7 52.4 %copy-start.7 = (s32[512]{0:T(512)S(1)}, s32[512]{0:T(512)}, u32[]{:S(2)}) copy-start(s32[512]{0:T(512)} %param.13) | copy-start | bytes 6148
  0.7 52.4 %copy-start.6 = (s32[64,32]{0,1:T(8,128)S(1)}, s32[64,32]{0,1:T(8,128)}, u32[]{:S(2)}) copy-start(s32[64,32]{0,1:T(8,128)} %param.12) | copy-start | bytes 24580
  0.7 52.4 %copy-start = (f32[2,400,400]{2,1,0:T(8,128)S(1)}, f32[2,400,400]{2,1,0:T(8,128)}, u32[]{:S(2)}) copy-start(f32[2,400,400]{2,1,0:T(8,128)} %param.11) | copy-start | bytes 3840004
  0.7 52.4 %copy-start.9 = (f32[256]{0:T(256)S(1)}, f32[256]{0:T(256)}, u32[]{:S(2)}) copy-start(f32[256]{0:T(256)} %param.10) | copy-start | bytes 3076
  2.8 43.3 %collective-permute-start.2 = (f32[432,256]{1,0:T(8,128)}, f32[432,256]{1,0:T(8,128)S(1)}, u32[]{:S(2)}, u32[]{:S(2)}) collective-permute-start(f32[432,256]{1,0:T(8,128)} %get-tuple-element.70.own_ref), channel_id=1, source_target_pairs={{0,384},{8,392},{16,400},{24,408},{32,416},{40,424},{48,432},{56,4... | collective-permute-start | bytes 1327112 | tf_op jit(solution)/shard_map/ppermute | solution.py:491
  7.8 38.4 %collective-permute-start.1 = (f32[432,256]{1,0:T(8,128)}, f32[432,256]{1,0:T(8,128)}, u32[]{:S(2)}, u32[]{:S(2)}) collective-permute-start(f32[432,256]{1,0:T(8,128)} %get-tuple-element.70.own_ref), channel_id=1, source_target_pairs={{0,256},{8,264},{16,272},{24,280},{32,288},{40,296},{48,304},{56,3... | collective-permute-start | bytes 1327112 | tf_op jit(solution)/shard_map/ppermute | solution.py:491
  10.3 35.8 %collective-permute-start = (f32[432,256]{1,0:T(8,128)}, f32[432,256]{1,0:T(8,128)}, u32[]{:S(2)}, u32[]{:S(2)}) collective-permute-start(f32[432,256]{1,0:T(8,128)} %get-tuple-element.70.own_ref), channel_id=1, source_target_pairs={{0,128},{8,136},{16,144},{24,152},{32,160},{40,168},{48,176},{56,1... | collective-permute-start | bytes 1327112 | tf_op jit(solution)/shard_map/ppermute | solution.py:491
  12.7 33.5 %all-to-all-start.7 = ((f32[64,2,1,128]{3,1,2,0:T(2,128)}), f32[64,2,1,128]{3,1,2,0:T(2,128)S(1)}, u32[]{:S(2)}, u32[]{:S(2)}) async-start(f32[64,2,1,128]{3,1,2,0:T(2,128)} %bitcast.59), calls=%async_computation.7 | async-start | bytes 131072 | tf_op jit(solution)/shard_map/all_to_all | solution.py:20
  46.1 0.8 copy-start.5
  53.1 95.3 %all-to-all-start = ((f32[64,60,1,128]{3,2,1,0:T(1,128)}), f32[64,60,1,128]{3,2,1,0:T(1,128)S(1)}, u32[]{:S(2)}, u32[]{:S(2)}) async-start(f32[64,60,1,128]{3,2,1,0:T(1,128)} %bitcast.55), calls=%async_computation | async-start | bytes 3932160 | tf_op jit(solution)/shard_map/cond/branch_0_fun/all_to_all | solution.py:20
  148.4 1.3 copy-start.1
  163.5 115.0 %copy-start.3 = (f32[400,256]{1,0:T(8,128)S(1)}, f32[400,256]{1,0:T(8,128)}, u32[]{:S(2)}) copy-start(f32[400,256]{1,0:T(8,128)} %get-tuple-element.49.table_ref) | copy-start | bytes 1228804 | tf_op jit(solution)/shard_map/cond
  163.5 99.0 %all-to-all-start.1 = ((f32[64,60,1,128]{3,2,1,0:T(1,128)}), f32[64,60,1,128]{3,2,1,0:T(1,128)S(1)}, u32[]{:S(2)}, u32[]{:S(2)}) async-start(f32[64,60,1,128]{3,2,1,0:T(1,128)} %bitcast.46), calls=%async_computation.1 | async-start | bytes 3932160 | tf_op jit(solution)/shard_map/cond/branch_0_fun/all_to_all | solution.py:20
  262.5 1.3 copy-start.2
  280.8 0.8 copy-start.13
  280.8 0.7 copy-start.14

commit v9 on v8

--- a/solution.py
+++ b/solution.py
@@ -441,8 +441,7 @@
     grad_query = grad_pos * tail + dot3(grad_neg, negs)
     for span, to in zip(spans, relations):
         keep(span.start, dot3(grad_query[span], to, 1, 1))
-    grad_neg = jax.nn.sigmoid(dot3(negs, query, 1, 1)) / total
-    keep(2 * edges, dot3(grad_neg, query))
+    keep(2 * edges, dot3(grad_neg.T, query))
 
     spot = row_place_ref[...]
     chosen = bits(iota((count, spot.shape[1]), 0) == spot)

time: 282 us -> 282 us (level)
  no operation moved by 1% of the time
where the time goes in v9:
time: 282 us; the launch traced here: 281 us
  waiting for transfers between devices  187 us (66%)
  starting transfers between devices  40.9 us (15%)
  Pallas kernels  28.3 us (10%)
  blocking collectives  11.1 us (4%)
  local copies, waits for them, and re-layouts  6.61 us (2%)
  other arithmetic  4.93 us (2%)
    all_to_all x3, waiting for transfers between devices, exchange(): lax.all_to_all(blocks, 'grp', split_axis=0, concat_axis=0, tiled=True)  187 us
    all_to_all x3, starting transfers between devices, exchange(): lax.all_to_all(blocks, 'grp', split_axis=0, concat_axis=0, tiled=True)  31.1 us
    pallas_call x1, Pallas kernels, compact_path(): call(edges_kernel, shaped(*blocks.shape), scratch_shapes=split + [pltpu.V...  13.4 us
    all_to_all x1, blocking collectives, compact_path(): lax.all_to_all(lists, 'grp', 0, 0, tiled=True, axis_index_groups=[list(ra...  11.1 us
    ppermute x3, starting transfers between devices, to_mates(): lax.ppermute(x, 'grp', [(p, p ^ d * DEPTH) for p in range(peers)])  9.81 us
  transfers between devices with their start and end apart: 6, of which 3 were waited for; matrix products, arithmetic and copies ran while one was open for 3% of the time, Pallas kernels for 1%

profile of v9, /device:TPU:6, one launch (start us, length us, event | category | flops | bytes accessed | tf_op | source)
XLA Modules:
  0.0 281.2 jit_solution(10884337209478536593)
XLA Ops:
  0.6 0.0 copy-start.12
  0.6 0.0 copy-start.8
  0.7 0.0 copy-start.7
  0.7 0.0 copy-start.6
  0.7 0.0 copy-start
  0.7 0.0 copy-start.9
  0.7 2.1 shard_map.86
  2.8 4.9 %collective-permute-start.2 = (f32[432,256]{1,0:T(8,128)}, f32[432,256]{1,0:T(8,128)S(1)}, u32[]{:S(2)}, u32[]{:S(2)}) collective-permute-start(f32[432,256]{1,0:T(8,128)} %get-tuple-element.70.own_ref), channel_id=1, source_target_pairs={{0,384},{8,392},{16,400},{24,408},{32,416},{40,424},{48,432},{56,4... | collective-permute-start | bytes 1327112 | tf_op jit(solution)/shard_map/ppermute | solution.py:490
  7.8 2.5 collective-permute-start.1
  10.3 2.3 collective-permute-start
  12.7 18.7 %all-to-all-start.7 = ((f32[64,2,1,128]{3,1,2,0:T(2,128)}), f32[64,2,1,128]{3,1,2,0:T(2,128)S(1)}, u32[]{:S(2)}, u32[]{:S(2)}) async-start(f32[64,2,1,128]{3,1,2,0:T(2,128)} %bitcast.59), calls=%async_computation.7 | async-start | bytes 131072 | tf_op jit(solution)/shard_map/all_to_all | solution.py:20
  31.4 2.7 fusion.15
  34.1 12.0 %all-to-all-done.7 = f32[64,2,1,128]{3,1,2,0:T(2,128)S(1)} async-done(((f32[64,2,1,128]{3,1,2,0:T(2,128)}), f32[64,2,1,128]{3,1,2,0:T(2,128)S(1)}, u32[]{:S(2)}, u32[]{:S(2)}) %all-to-all-start.7) | async-done | bytes 65568 | tf_op jit(solution)/shard_map/all_to_all | solution.py:20
  46.1 0.0 collective-permute-done.2.third_ref
  46.1 0.0 copy-start.5
  46.1 0.0 collective-permute-done.1.second_ref
  46.1 0.0 collective-permute-done.first_ref
  46.2 0.8 copy-done.5
  46.9 5.5 %shard_map.87 = (f32[3840,128]{1,0:T(8,128)}, s32[64,128]{1,0:T(8,128)S(1)}, s32[1]{0:T(128)}) custom-call(s32[1]{0:T(128)} %bitcast.13.me_ref, f32[128,128]{1,0:T(8,128)S(1)} %bitcast.57, f32[432,256]{1,0:T(8,128)} %get-tuple-element.70.own_ref, f32[432,256]{1,0:T(8,128)} %collective-permute-done.first_ref, f32[432,256]{1,0:T(8,128)} %collective-permute-done.1.second_ref, ...), custom_call_target="tpu_custom_call" | custom-call | tf_op jit(solution)/shard_map/pallas_call | solution.py:555
  53.1 0.0 copy-done.12
  53.1 0.0 copy-done.8
  53.1 0.0 copy-done.7
  53.1 0.0 copy-done.6
  53.1 0.0 copy-done
  53.1 0.0 copy-done.9
  53.1 227.3 %conditional.1 = (f32[256]{0:T(256)S(1)}, f32[400,256]{1,0:T(8,128)S(1)}) conditional(s32[]{:T(128)} %bitcast.21, (f32[3840,128]{1,0:T(8,128)}, f32[128,128]{1,0:T(8,128)S(1)}, s32[1,512]{1,0:T(1,128)S(1)}, s32[1,512]{1,0:T(1,128)S(1)}, bf16[2,512,512]{2,1,0:T(8,128)(2,1)}, /*index=5*/bf16[2,512,512]{2,1,0:T(8,128)(2,1)S(1)}, ...), branch_computations={%region_0.1_spmd, %region_1.9_spmd} | conditional | flops 2912907008 | bytes 93422224 | solution.py:566
  53.1 4.9 %all-to-all-start = ((f32[64,60,1,128]{3,2,1,0:T(1,128)}), f32[64,60,1,128]{3,2,1,0:T(1,128)S(1)}, u32[]{:S(2)}, u32[]{:S(2)}) async-start(f32[64,60,1,128]{3,2,1,0:T(1,128)} %bitcast.55), calls=%async_computation | async-start | bytes 3932160 | tf_op jit(solution)/shard_map/cond/branch_0_fun/all_to_all | solution.py:20
  58.0 2.0 branch_0_fun.4
  60.0 1.7 copy.36.place_ref
  61.7 0.9 reduce.1
  62.6 1.3 pad_add_fusion.row_place_ref
  63.9 84.5 %all-to-all-done = f32[64,60,1,128]{3,2,1,0:T(1,128)S(1)} async-done(((f32[64,60,1,128]{3,2,1,0:T(1,128)}), f32[64,60,1,128]{3,2,1,0:T(1,128)S(1)}, u32[]{:S(2)}, u32[]{:S(2)}) %all-to-all-start) | async-done | bytes 1966112 | tf_op jit(solution)/shard_map/cond/branch_0_fun/all_to_all | solution.py:20
  148.4 0.0 copy-start.1
  148.4 1.3 copy-done.1
  149.7 13.4 %branch_0_fun.5 = f32[3840,128]{1,0:T(8,128)} custom-call(f32[3840,128]{1,0:T(8,128)} %bitcast.44, s32[1024,1]{1,0:T(8,128)} %copy.36.place_ref, s32[128,1]{1,0:T(8,128)} %get-tuple-element.43.neg_place_ref, s32[1,1152]{1,0:T(1,128)} %pad_add_fusion.row_place_ref, bf16[2,512,512]{2,1,0:T(8,128)(2,1)} %get-tuple-element.44.rel_hi_ref, ...), custom_call_target="tpu_custom_call" | custom-call | tf_op jit(solution)/shard_map/cond/branch_0_fun/pallas_call | solution.py:512
  163.1 7.5 %all-to-all-start.1 = ((f32[64,60,1,128]{3,2,1,0:T(1,128)}), f32[64,60,1,128]{3,2,1,0:T(1,128)S(1)}, u32[]{:S(2)}, u32[]{:S(2)}) async-start(f32[64,60,1,128]{3,2,1,0:T(1,128)} %bitcast.46), calls=%async_computation.1 | async-start | bytes 3932160 | tf_op jit(solution)/shard_map/cond/branch_0_fun/all_to_all | solution.py:20
  170.6 0.1 copy.51
  170.7 0.7 reshape.122.code_ref
  171.4 90.7 %all-to-all-done.1 = f32[64,60,1,128]{3,2,1,0:T(1,128)S(1)} async-done(((f32[64,60,1,128]{3,2,1,0:T(1,128)}), f32[64,60,1,128]{3,2,1,0:T(1,128)S(1)}, u32[]{:S(2)}, u32[]{:S(2)}) %all-to-all-start.1) | async-done | bytes 1966112 | tf_op jit(solution)/shard_map/cond/branch_0_fun/all_to_all | solution.py:20
  262.1 1.3 copy-done.2
  263.5 3.6 %branch_0_fun.6 = (f32[4,32,512]{2,1,0:T(8,128)}, f32[256,512]{1,0:T(8,128)}) custom-call(f32[3840,128]{1,0:T(8,128)} %bitcast.45, s32[1,1216]{1,0:T(1,128)} %reshape.122.code_ref), custom_call_target="tpu_custom_call" | custom-call | tf_op jit(solution)/shard_map/cond/branch_0_fun/pallas_call | solution.py:520
  267.0 11.1 %all_to_all.33.lists_ref = f32[4,32,512]{2,1,0:T(8,128)} all-to-all(f32[4,32,512]{2,1,0:T(8,128)} %get-tuple-element.48), channel_id=1, replica_groups={{0,128,256,384},{8,136,264,392},{16,144,272,400},{24,152,280,408},{32,1..., dimensions={0} | all-to-all | bytes 524288 | tf_op jit(solution)/shard_map/cond/branch_0_fun/all_to_all | solution.py:525
  278.1 0.0 copy-done.3
  278.1 1.7 branch_0_fun.7
  280.4 0.0 copy-start.13
  280.4 0.0 copy-start.14
  280.4 0.7 copy-done.13
  281.2 0.0 copy-done.14
  (3 shorter events, 0.0 us)
Async XLA Ops:
  0.6 52.4 %copy-start.12 = (s32[2]{0:T(128)S(1)}, s32[2]{0:T(128)}, u32[]{:S(2)}) copy-start(s32[2]{0:T(128)} %negs_ref.1) | copy-start | bytes 28
  0.6 52.4 %copy-start.8 = (s32[512]{0:T(512)S(1)}, s32[512]{0:T(512)}, u32[]{:S(2)}) copy-start(s32[512]{0:T(512)} %param.14) | copy-start | bytes 6148
  0.7 52.4 %copy-start.7 = (s32[512]{0:T(512)S(1)}, s32[512]{0:T(512)}, u32[]{:S(2)}) copy-start(s32[512]{0:T(512)} %param.13) | copy-start | bytes 6148
  0.7 52.4 %copy-start.6 = (s32[64,32]{0,1:T(8,128)S(1)}, s32[64,32]{0,1:T(8,128)}, u32[]{:S(2)}) copy-start(s32[64,32]{0,1:T(8,128)} %param.12) | copy-start | bytes 24580
  0.7 52.4 %copy-start = (f32[2,400,400]{2,1,0:T(8,128)S(1)}, f32[2,400,400]{2,1,0:T(8,128)}, u32[]{:S(2)}) copy-start(f32[2,400,400]{2,1,0:T(8,128)} %param.11) | copy-start | bytes 3840004
  0.7 52.4 %copy-start.9 = (f32[256]{0:T(256)S(1)}, f32[256]{0:T(256)}, u32[]{:S(2)}) copy-start(f32[256]{0:T(256)} %param.10) | copy-start | bytes 3076
  2.8 43.3 %collective-permute-start.2 = (f32[432,256]{1,0:T(8,128)}, f32[432,256]{1,0:T(8,128)S(1)}, u32[]{:S(2)}, u32[]{:S(2)}) collective-permute-start(f32[432,256]{1,0:T(8,128)} %get-tuple-element.70.own_ref), channel_id=1, source_target_pairs={{0,384},{8,392},{16,400},{24,408},{32,416},{40,424},{48,432},{56,4... | collective-permute-start | bytes 1327112 | tf_op jit(solution)/shard_map/ppermute | solution.py:490
  7.8 38.4 %collective-permute-start.1 = (f32[432,256]{1,0:T(8,128)}, f32[432,256]{1,0:T(8,128)}, u32[]{:S(2)}, u32[]{:S(2)}) collective-permute-start(f32[432,256]{1,0:T(8,128)} %get-tuple-element.70.own_ref), channel_id=1, source_target_pairs={{0,256},{8,264},{16,272},{24,280},{32,288},{40,296},{48,304},{56,3... | collective-permute-start | bytes 1327112 | tf_op jit(solution)/shard_map/ppermute | solution.py:490
  10.3 35.8 %collective-permute-start = (f32[432,256]{1,0:T(8,128)}, f32[432,256]{1,0:T(8,128)}, u32[]{:S(2)}, u32[]{:S(2)}) collective-permute-start(f32[432,256]{1,0:T(8,128)} %get-tuple-element.70.own_ref), channel_id=1, source_target_pairs={{0,128},{8,136},{16,144},{24,152},{32,160},{40,168},{48,176},{56,1... | collective-permute-start | bytes 1327112 | tf_op jit(solution)/shard_map/ppermute | solution.py:490
  12.7 33.5 %all-to-all-start.7 = ((f32[64,2,1,128]{3,1,2,0:T(2,128)}), f32[64,2,1,128]{3,1,2,0:T(2,128)S(1)}, u32[]{:S(2)}, u32[]{:S(2)}) async-start(f32[64,2,1,128]{3,1,2,0:T(2,128)} %bitcast.59), calls=%async_computation.7 | async-start | bytes 131072 | tf_op jit(solution)/shard_map/all_to_all | solution.py:20
  46.1 0.8 copy-start.5
  53.1 95.3 %all-to-all-start = ((f32[64,60,1,128]{3,2,1,0:T(1,128)}), f32[64,60,1,128]{3,2,1,0:T(1,128)S(1)}, u32[]{:S(2)}, u32[]{:S(2)}) async-start(f32[64,60,1,128]{3,2,1,0:T(1,128)} %bitcast.55), calls=%async_computation | async-start | bytes 3932160 | tf_op jit(solution)/shard_map/cond/branch_0_fun/all_to_all | solution.py:20
  148.4 1.3 copy-start.1
  163.1 115.0 %copy-start.3 = (f32[400,256]{1,0:T(8,128)S(1)}, f32[400,256]{1,0:T(8,128)}, u32[]{:S(2)}) copy-start(f32[400,256]{1,0:T(8,128)} %get-tuple-element.49.table_ref) | copy-start | bytes 1228804 | tf_op jit(solution)/shard_map/cond
  163.1 99.0 %all-to-all-start.1 = ((f32[64,60,1,128]{3,2,1,0:T(1,128)}), f32[64,60,1,128]{3,2,1,0:T(1,128)S(1)}, u32[]{:S(2)}, u32[]{:S(2)}) async-start(f32[64,60,1,128]{3,2,1,0:T(1,128)} %bitcast.46), calls=%async_computation.1 | async-start | bytes 3932160 | tf_op jit(solution)/shard_map/cond/branch_0_fun/all_to_all | solution.py:20
  262.1 1.3 copy-start.2
  280.4 0.8 copy-start.13
  280.4 0.7 copy-start.14
